TPU v7x, 128 devices: a whole 4x4x4 slice. The times are simulated.
128 devices in a mesh: scan: 4 (over z_lo, core), pts: 32 (over y, x, z_hi).
Axes of the slice: x: 4, y: 4, z: 4 (z_hi: 2, z_lo: 2; z = z_hi * 2 + z_lo), core: 2. Of those that a mesh axis runs over, the one named last changes fastest.
Arguments:
- cotangent: bfloat16 [2048, 131072], P('scan', 'pts'), may hold values from -6 to 6
- scan_paths: bfloat16 [2048, 256], P('scan'), may hold values from -6 to 6
- query_points: bfloat16 [4, 131072], P(None, 'pts'), may hold values from -1 to 1
- branch_in: bfloat16 [256, 2048], replicated, may hold values from -0.375 to 0.375
- branch_in_bias: float32 [2048], replicated, may hold values from -3 to 3
- branch_out: bfloat16 [2048, 512], replicated, may hold values from -0.125 to 0.125
- branch_out_bias: float32 [512], replicated, may hold values from -3 to 3
- trunk_in: bfloat16 [4, 1024], replicated, may hold values from -6 to 6
- trunk_in_bias: float32 [1024], replicated, may hold values from -4.5 to 4.5
- trunk_mid: bfloat16 [1, 1024, 1024], replicated, may hold values from -0.1875 to 0.1875
- trunk_mid_bias: float32 [1, 1024], replicated, may hold values from -3 to 3
- trunk_out: bfloat16 [1024, 512], replicated, may hold values from -0.1875 to 0.1875
- trunk_out_bias: float32 [512], replicated, may hold values from -3 to 3
Outputs:
- grad_branch_in: float32 [256, 2048], replicated
- grad_branch_in_bias: float32 [2048], replicated
- grad_branch_out: float32 [2048, 512], replicated
- grad_branch_out_bias: float32 [512], replicated
- grad_trunk_in: float32 [4, 1024], replicated
- grad_trunk_in_bias: float32 [1024], replicated
- grad_trunk_mid: float32 [1, 1024, 1024], replicated
- grad_trunk_mid_bias: float32 [1, 1024], replicated
- grad_trunk_out: float32 [1024, 512], replicated
- grad_trunk_out_bias: float32 [512], replicated
All inputs are finite; a program needn't handle non-finite values.
Results may differ from a plain program's by a relative error of at most 0.012.
Values may be sent and summed in bfloat16 or wider, within the bound.
No kernel may reach another device: no remote copies, remote signals or barrier semaphores. Data moves between devices by JAX's collectives and lax.ppermute only.
A program may use at most 128 MiB of HBM per device.

v0:
```python
import functools
import math

import jax
import jax.numpy as jnp
from jax import lax
from jax.experimental import pallas as pl
from jax.experimental.pallas import tpu as pltpu
from jax.sharding import Mesh, PartitionSpec as P

ALL = ("zl", "core", "y", "x", "zh")
CHIPS = ("zl", "y", "x", "zh")
PTS = ("y", "x", "zh")
BF = jnp.bfloat16
F32 = jnp.float32


def dot(left, right, dims):
    return lax.dot_general(left, right, (dims, ((), ())), preferred_element_type=F32)


def rows_rows(left, right):
    return dot(left, right, ((0,), (0,)))


def swap(values, axis):
    return lax.ppermute(values, axis, [(0, 1), (1, 0)])


def exchange(values, axes):
    return lax.all_to_all(values, axes, split_axis=0, concat_axis=0, tiled=True)


def sum_parts(values):
    return jnp.sum(values.astype(F32), axis=0)


def tanh_layer(inputs, weights, offsets):
    return jnp.tanh(dot(inputs, weights, ((1,), (0,))) + offsets).astype(BF)


def slope(values):
    wide = values.astype(F32)
    return 1.0 - wide * wide


TILE = 512
CHUNK = 256


def trunk_back_kernel(
    factor,
    core_ref,
    kept_ref,
    theirs_ref,
    coeffs_ref,
    basis_ref,
    low_ref,
    high_ref,
    lead_ref,
    out_ref,
    mid_ref,
    other_ref,
    mine_ref,
    sum_mid,
    sum_out,
    sum_lead,
    sum_one,
    sum_two,
    delta_2,
    delta_1,
    delta_0,
):
    step = pl.program_id(0)
    width, tile = low_ref.shape
    basis = basis_ref.shape[0]
    scans = kept_ref.shape[0]

    @pl.when(step == 0)
    def _():
        for total in (sum_mid, sum_out, sum_lead, sum_one, sum_two):
            total[...] = jnp.zeros_like(total)

    def lanes(values):
        return functools.reduce(
            jnp.add, [values[:, at : at + 128] for at in range(0, tile, 128)]
        )

    plain, across = ((1,), (0,)), ((1,), (1,))
    for at in range(0, basis, CHUNK):
        rows = slice(at, at + CHUNK)
        pulled = dot(coeffs_ref[rows, :scans], kept_ref[...], plain)
        pulled += dot(coeffs_ref[rows, scans:], theirs_ref[...], plain)
        delta = factor * pulled * slope(basis_ref[rows, :])
        sum_two[rows, :] += lanes(delta)
        delta_2[rows, :] = delta.astype(BF)
    for at in range(0, width, CHUNK):
        rows = slice(at, at + CHUNK)
        delta = dot(out_ref[rows, :], delta_2[...], plain) * slope(high_ref[rows, :])
        sum_one[rows, :] += lanes(delta)
        delta_1[rows, :] = delta.astype(BF)
    for at in range(0, width, CHUNK):
        rows = slice(at, at + CHUNK)
        delta = dot(mid_ref[rows, :], delta_1[...], plain) * slope(low_ref[rows, :])
        delta_0[rows, :] = delta.astype(BF)
    for at in range(0, width, CHUNK):
        rows = slice(at, at + CHUNK)
        sum_out[rows, :] += dot(high_ref[rows, :], delta_2[...], across)
        sum_mid[rows, :] += dot(low_ref[rows, :], delta_1[...], across)
        sum_lead[rows, :] += dot(delta_0[rows, :], lead_ref[...], across)

    @pl.when(step == pl.num_programs(0) - 1)
    def _():
        lane = lax.broadcasted_iota(jnp.int32, (width, 128), 1)
        one = jnp.sum(sum_one[...], axis=1, keepdims=True)
        sum_lead[...] = jnp.where(lane == 5, one, sum_lead[...])
        two = jnp.sum(sum_two[...], axis=1, keepdims=True)
        sum_lead[:basis, :] = jnp.where(lane[:basis] == 6, two, sum_lead[:basis, :])
        core = core_ref[0]
        half = width // 2
        for target, start in ((other_ref, (1 - core) * half), (mine_ref, core * half)):
            rows = pl.ds(pl.multiple_of(start, half), half)
            at = 0
            for total in (sum_mid, sum_out, sum_lead):
                target[:, at : at + total.shape[1]] = total[rows, :].astype(target.dtype)
                at += total.shape[1]


def trunk_back(core, cotangent, theirs, coeffs, basis_vals, low, high, lead, out, mid, factor):
    width, half = low.shape
    basis = basis_vals.shape[0]
    scans = cotangent.shape[0]
    steps = half // TILE
    columns = width + basis + 128

    def whole(values):
        return pl.BlockSpec(values.shape, lambda i, c: (0, 0))

    def part(rows):
        return pl.BlockSpec((rows, TILE), lambda i, c: (0, i))

    product = 2 * half * (2 * scans * basis + 2 * width * basis + 2 * width * width + width * 128)
    return pl.pallas_call(
        functools.partial(trunk_back_kernel, factor),
        grid_spec=pltpu.PrefetchScalarGridSpec(
            num_scalar_prefetch=1,
            grid=(steps,),
            in_specs=[
                pl.BlockSpec((scans, TILE), lambda i, c: (0, c[0] * steps + i)),
                part(scans),
                whole(coeffs),
                part(basis),
                part(width),
                part(width),
                part(128),
                whole(out),
                whole(mid),
            ],
            out_specs=[pl.BlockSpec((width // 2, columns), lambda i, c: (0, 0))] * 2,
            scratch_shapes=[
                pltpu.VMEM((width, width), F32),
                pltpu.VMEM((width, basis), F32),
                pltpu.VMEM((width, 128), F32),
                pltpu.VMEM((width, 128), F32),
                pltpu.VMEM((basis, 128), F32),
                pltpu.VMEM((basis, TILE), BF),
                pltpu.VMEM((width, TILE), BF),
                pltpu.VMEM((width, TILE), BF),
            ],
        ),
        out_shape=[
            jax.ShapeDtypeStruct((width // 2, columns), BF),
            jax.ShapeDtypeStruct((width // 2, columns), F32),
        ],
        compiler_params=pltpu.CompilerParams(
            dimension_semantics=("arbitrary",), vmem_limit_bytes=48 * 1024 * 1024
        ),
        cost_estimate=pl.CostEstimate(
            flops=product, bytes_accessed=24 * 1024 * 1024, transcendentals=0
        ),
        name="trunk_back",
    )(core.reshape(1), cotangent, theirs, coeffs, basis_vals, low, high, lead, out, mid)


def on_device(
    cotangent,
    scan_paths,
    query_points,
    branch_in,
    branch_in_bias,
    branch_out,
    branch_out_bias,
    trunk_in,
    trunk_in_bias,
    trunk_mid,
    trunk_mid_bias,
    trunk_out,
    trunk_out_bias,
):
    core = lax.axis_index("core")
    scan_rows, point_cols = cotangent.shape
    half = point_cols // 2
    chips = lax.axis_size(CHIPS)
    pts = lax.axis_size(PTS)
    factor = 1.0 / math.sqrt(scan_rows * 4 * point_cols * pts)
    width = trunk_in.shape[1]
    basis = trunk_out.shape[1]

    zl = lax.axis_index("zl")
    sent = lax.dynamic_slice_in_dim(cotangent, (1 - core) * half, half, 1)
    pair_got = swap(jnp.concatenate([sent, scan_paths], axis=1), "core")
    points = lax.dynamic_slice_in_dim(query_points, core * half, half, 1)

    trunk_0 = dot(trunk_in, points, ((0,), (0,))) + trunk_in_bias[:, None]
    trunk_0 = jnp.tanh(trunk_0).astype(BF)
    trunk_1 = dot(trunk_mid[0], trunk_0, ((0,), (0,))) + trunk_mid_bias[0][:, None]
    trunk_1 = jnp.tanh(trunk_1).astype(BF)
    basis_vals = dot(trunk_out, trunk_1, ((0,), (0,))) + trunk_out_bias[:, None]
    basis_vals = jnp.tanh(basis_vals).astype(BF)

    local_paths = jnp.concatenate([scan_paths, pair_got[:, half:]], axis=0)
    side_paths = swap(local_paths, "zl")

    coef_theirs = dot(pair_got[:, :half], basis_vals, ((1,), (1,))).astype(BF)
    coef_swapped = swap(coef_theirs, "core")
    kept = lax.dynamic_slice_in_dim(cotangent, core * half, half, 1)
    coef_mine = dot(kept, basis_vals, ((1,), (1,)))

    hidden_local = tanh_layer(local_paths, branch_in, branch_in_bias)
    coeffs = dot(branch_out, hidden_local, ((0,), (1,))) + branch_out_bias[:, None]
    coeffs = coeffs.astype(BF)

    coef_part = (coef_mine + coef_swapped.astype(F32)).astype(BF)
    coef_part, coeffs, side_paths = lax.optimization_barrier((coef_part, coeffs, side_paths))
    coef_parts = exchange(coef_part.reshape(pts, scan_rows // pts, basis), PTS)

    lead = jnp.concatenate([points, jnp.ones((1, half), BF), jnp.zeros((123, half), BF)], axis=0)
    other, mine = trunk_back(
        core,
        cotangent,
        pair_got,
        coeffs,
        basis_vals,
        trunk_0,
        trunk_1,
        lead,
        trunk_out,
        trunk_mid[0],
        factor,
    )
    coef_parts, other = lax.optimization_barrier((coef_parts, other))
    coef_low = (factor * sum_parts(coef_parts)).astype(BF)

    pair = (mine + swap(other, "core").astype(F32)).astype(BF)
    columns = pair.shape[1]
    rows = width // 2 // chips
    coef_flat = jnp.concatenate([coef_low[:rows], coef_low[rows:]], axis=1)
    load = jnp.concatenate(
        [
            pair.reshape(chips, rows, columns),
            jnp.broadcast_to(coef_flat[None], (chips,) + coef_flat.shape),
        ],
        axis=2,
    )
    got = exchange(load, CHIPS)
    local = local_paths.reshape(2, scan_rows, -1)
    side = side_paths.reshape(2, scan_rows, -1)
    paths = jnp.where(
        zl == 0, jnp.stack([local, side], axis=1), jnp.stack([side, local], axis=1)
    ).reshape(4 * scan_rows, -1)
    hidden = tanh_layer(paths, branch_in, branch_in_bias)
    got, hidden = lax.optimization_barrier((got, hidden))
    total = sum_parts(got[:, :, :columns]).astype(BF)
    wide = jnp.broadcast_to(total[None], (chips, rows, columns))
    wide, got = lax.optimization_barrier((wide, got))
    spread = exchange(wide, CHIPS)

    coef_own = jnp.stack([got[:, :, columns : columns + basis], got[:, :, columns + basis :]], 1)
    coef_own = coef_own.reshape(2, scan_rows, basis)
    coef_other = swap(coef_own, "core")
    coef_all = jnp.stack([coef_own, coef_other]).reshape(4 * scan_rows, basis)
    grad_branch_out = rows_rows(hidden, coef_all)
    grad_branch_out_bias = jnp.sum(coef_all.astype(F32), axis=0)
    branch_delta = (dot(coef_all, branch_out, ((1,), (1,))) * slope(hidden)).astype(BF)
    grad_branch_in = rows_rows(paths, branch_delta)
    grad_branch_in_bias = jnp.sum(branch_delta.astype(F32), axis=0)

    spread, grad_branch_out, grad_branch_in = lax.optimization_barrier(
        (spread, grad_branch_out, grad_branch_in)
    )
    spread = spread.reshape(width // 2, columns)
    spread_theirs = swap(spread, "core")

    full = jnp.where(
        core == 0,
        jnp.concatenate([spread, spread_theirs], axis=0),
        jnp.concatenate([spread_theirs, spread], axis=0),
    ).astype(F32)
    tail = full[:, width + basis :]
    return (
        grad_branch_in,
        grad_branch_in_bias,
        grad_branch_out,
        grad_branch_out_bias,
        tail[:, :4].T,
        tail[:, 4],
        full[:, :width][None],
        tail[:, 5][None],
        full[:, width : width + basis],
        tail[:basis, 6],
    )


def solution(mesh):
    fine = Mesh(mesh.devices.reshape(2, 2, 4, 4, 2), ALL)
    scan, pts = ("zl", "core"), PTS
    placed = (P(scan, pts), P(scan, None), P(None, pts)) + (P(),) * 10
    return jax.shard_map(
        on_device, mesh=fine, in_specs=placed, out_specs=(P(),) * 10, check_vma=False
    )
```

profile of v0, /device:TPU:1, one launch (start us, length us, event | category | flops | bytes accessed | tf_op | source)
XLA Modules:
  0.0 178.7 jit_solution(9347320757514440452)
XLA Ops:
  0.7 2.0 %constant_dynamic-slice_fusion.1 = bf16[512,2048]{1,0:T(8,128)(2,1)S(1)} fusion(bf16[512,4096]{1,0:T(8,128)(2,1)} %kept_ref.1, s32[]{:T(128)S(6)} %select_n.27), kind=kLoop, calls=%fused_computation.40 | loop fusion | bytes 4194308 | tf_op jit(solution)/shard_map/dynamic_slice | solution.py:210
  7.5 5.1 %tanh_convert_fusion.2 = bf16[2048,1024]{0,1:T(8,128)(2,1)S(1)} fusion(f32[1024]{0:T(1024)S(1)} %bitcast.67, bf16[2048,1024]{0,1:T(8,128)(2,1)S(1)} %tanh_convert_fusion.3, bf16[1,1024,1024]{2,1,0:T(8,128)(2,1)S(1)} %copy-done.12), kind=kOutput, calls=%fused_computation.4 | convolution fusion | flops 4299161600 | bytes 10489856 | tf_op jit(solution)/shard_map/dot_general | solution.py:19
  12.7 2.5 %tanh_convert_fusion.4 = bf16[2048,512]{0,1:T(8,128)(2,1)S(1)} fusion(bf16[2048,1024]{0,1:T(8,128)(2,1)S(1)} %tanh_convert_fusion.2, bf16[1024,512]{1,0:T(8,128)(2,1)S(1)} %copy-done.2, f32[512]{0:T(512)S(1)} %copy-done.17), kind=kOutput, calls=%fused_computation.8 | convolution fusion | flops 2149580800 | bytes 7342080 | tf_op jit(solution)/shard_map/dot_general | solution.py:19
  16.4 2.3 %fusion.3 = f32[512,512]{1,0:T(8,128)} fusion(bf16[2048,512]{0,1:T(8,128)(2,1)S(1)} %tanh_convert_fusion.4, bf16[512,4096]{1,0:T(8,128)(2,1)S(1)} %copy-done.8, s32[]{:T(128)S(6)} %select_n.28), kind=kOutput, calls=%fused_computation.18 | convolution fusion | flops 1073741824 | bytes 5242884 | tf_op jit(solution)/shard_map/dot_general | solution.py:19
  20.5 1.8 %collective-permute-start.2 = (bf16[1024,256]{1,0:T(8,128)(2,1)S(1)}, bf16[1024,256]{1,0:T(8,128)(2,1)}, u32[]{:S(2)}, u32[]{:S(2)}) collective-permute-start(bf16[1024,256]{1,0:T(8,128)(2,1)S(1)} %pad_maximum_fusion.4), channel_id=1, source_target_pairs={{0,64},{64,0},{1,65},{65,1},{2,66},{66,2},{3,67},{67,3},{4,68},{68... | collective-permute-start | bytes 1572872 | tf_op jit(solution)/shard_map/ppermute | solution.py:27
  22.3 3.7 %fusion.7 = bf16[512,512]{1,0:T(8,128)(2,1)} fusion(bf16[2048,512]{0,1:T(8,128)(2,1)S(1)} %tanh_convert_fusion.4, bf16[512,2304]{1,0:T(8,128)(2,1)} %collective-permute-done.theirs_ref), kind=kOutput, calls=%fused_computation.23 | convolution fusion | flops 1074003968 | bytes 4718592 | tf_op jit(solution)/shard_map/dot_general | solution.py:19
  26.3 5.7 %fusion.6.coeffs_ref = bf16[512,1024]{1,0:T(8,128)(2,1)} fusion(bf16[2048,512]{1,0:T(8,128)(2,1)S(1)} %copy-done, bf16[256,2048]{1,0:T(8,128)(2,1)} %param.16, f32[2048]{0:T(1024)S(1)} %copy-done.14, f32[512]{0:T(512)S(1)} %copy-done.18, bf16[512,256]{1,0:T(8,128)(2,1)} %copy-done.10, bf16[512,256]{1,0:T(8,128)(2,1)S(1)} %copy-done.9), kind=kOutput, calls=%fused_computation.22 | convolution fusion | flops 3227516928 | bytes 4728832 | tf_op jit(solution)/shard_map/dot_general | solution.py:19
  32.0 2.3 %add_convert_fusion.2 = bf16[512,512]{1,0:T(8,128)(2,1)} fusion(f32[512,512]{1,0:T(8,128)} %fusion.3, bf16[512,512]{1,0:T(8,128)(2,1)} %collective-permute-done.1), kind=kLoop, calls=%fused_computation.27 | loop fusion | flops 786432 | bytes 2097152 | tf_op jit(solution)/shard_map/convert_element_type | solution.py:233
  34.7 10.1 %all-to-all-start = ((bf16[32,16,512]{2,1,0:T(8,128)(2,1)}), bf16[32,16,512]{2,1,0:T(8,128)(2,1)}, u32[]{:S(2)}, u32[]{:S(2)}) async-start(bf16[32,16,512]{2,1,0:T(8,128)(2,1)} %bitcast.64), calls=%async_computation | async-start | bytes 1048576 | tf_op jit(solution)/shard_map/all_to_all | solution.py:31
  47.3 23.3 %trunk_back.1 = (bf16[512,1664]{1,0:T(8,128)(2,1)S(1)}, f32[512,1664]{1,0:T(8,128)}) custom-call(s32[1]{0:T(128)} %bitcast.core_ref, bf16[512,4096]{1,0:T(8,128)(2,1)} %kept_ref.1, bf16[512,2304]{1,0:T(8,128)(2,1)} %collective-permute-done.theirs_ref, bf16[512,1024]{1,0:T(8,128)(2,1)S(1)} %copy-done.4, bf16[512,2048]{1,0:T(8,128)(2,1)} %bitcast.70, ...), custom_call_target="tpu_custom_call" | custom-call | flops 15569256448 | bytes 25165824 | tf_op jit(solution)/shard_map/trunk_back/pallas_call | solution.py:143
  74.0 2.3 %collective-permute-done.3 = bf16[512,1664]{1,0:T(8,128)(2,1)S(1)} collective-permute-done((bf16[512,1664]{1,0:T(8,128)(2,1)}, bf16[512,1664]{1,0:T(8,128)(2,1)S(1)}, u32[]{:S(2)}, u32[]{:S(2)}) %collective-permute-start.3) | collective-permute-done | bytes 1703968 | tf_op jit(solution)/shard_map/ppermute | solution.py:27
  76.3 2.2 %fusion.5 = bf16[64,8,1664]{2,1,0:T(8,128)(2,1)S(1)} fusion(f32[512,1664]{1,0:T(8,128)} %get-tuple-element.25, bf16[512,1664]{1,0:T(8,128)(2,1)S(1)} %collective-permute-done.3), kind=kLoop, calls=%fused_computation.20 | loop fusion | flops 2555904 | bytes 6815744 | tf_op jit(solution)/shard_map/reshape | solution.py:260
  80.4 10.7 %all-to-all-start.1 = ((bf16[64,8,2688]{2,1,0:T(8,128)(2,1)}), bf16[64,8,2688]{2,1,0:T(8,128)(2,1)}, u32[]{:S(2)}, u32[]{:S(2)}) async-start(bf16[64,8,2688]{2,1,0:T(8,128)(2,1)} %pad_maximum_fusion), calls=%async_computation.1 | async-start | bytes 5505024 | tf_op jit(solution)/shard_map/all_to_all | solution.py:31
  93.5 5.7 %tanh_convert_fusion = bf16[2048,2048]{1,0:T(8,128)(2,1)} fusion(bf16[2048,256]{1,0:T(8,128)(2,1)S(1)} %bitcast.59, bf16[256,2048]{1,0:T(8,128)(2,1)} %param.16, f32[2048]{0:T(1024)S(1)} %copy-done.14), kind=kOutput, calls=%fused_computation.2 | convolution fusion | flops 2155872256 | bytes 10493952 | tf_op jit(solution)/shard_map/dot_general | solution.py:19
  99.2 25.8 %all-to-all-done.1 = bf16[64,8,2688]{2,1,0:T(8,128)(2,1)} async-done(((bf16[64,8,2688]{2,1,0:T(8,128)(2,1)}), bf16[64,8,2688]{2,1,0:T(8,128)(2,1)}, u32[]{:S(2)}, u32[]{:S(2)}) %all-to-all-start.1) | async-done | bytes 2752544 | tf_op jit(solution)/shard_map/all_to_all | solution.py:31
  129.4 2.3 %collective-permute-start.4 = (bf16[2,512,512]{2,1,0:T(8,128)(2,1)S(1)}, bf16[2,512,512]{2,1,0:T(8,128)(2,1)}, u32[]{:S(2)}, u32[]{:S(2)}) collective-permute-start(bf16[2,512,512]{2,1,0:T(8,128)(2,1)S(1)} %bitcast.56), channel_id=1, source_target_pairs={{0,32},{32,0},{1,33},{33,1},{2,34},{34,2},{3,35},{35,3},{4,36},{36... | collective-permute-start | bytes 3145736 | tf_op jit(solution)/shard_map/ppermute | solution.py:27
  131.7 7.3 %all-to-all-start.2 = ((bf16[64,8,1664]{2,1,0:T(8,128)(2,1)}), bf16[64,8,1664]{2,1,0:T(8,128)(2,1)}, u32[]{:S(2)}, u32[]{:S(2)}) async-start(bf16[64,8,1664]{2,1,0:T(8,128)(2,1)} %broadcast_in_dim.13), calls=%async_computation.2 | async-start | bytes 3407872 | tf_op jit(solution)/shard_map/all_to_all | solution.py:31
  139.0 2.7 %pad_maximum_fusion.2 = bf16[2,2,512,512]{3,2,1,0:T(8,128)(2,1)} fusion(bf16[1,2,512,512]{3,2,1,0:T(8,128)(2,1)} %bitcast.21, bf16[1,2,512,512]{3,2,1,0:T(8,128)(2,1)S(1)} %bitcast.57), kind=kLoop, calls=%fused_computation.16 | loop fusion | flops 1048576 | bytes 4194304 | tf_op jit(solution)/shard_map/stack | solution.py:281
  141.7 9.1 %convert_reduce_fusion = (f32[2048]{0:T(1024)}, bf16[2048,2048]{1,0:T(8,128)(2,1)S(1)}) fusion(bf16[2048,2048]{1,0:T(8,128)(2,1)} %tanh_convert_fusion, bf16[2048,512]{1,0:T(8,128)(2,1)} %bitcast.62, bf16[2048,512]{1,0:T(8,128)(2,1)S(1)} %copy-done), kind=kOutput, calls=%fused_computation | convolution fusion | flops 4324325376 | bytes 20979712 | tf_op jit(solution)/shard_map/dot_general | solution.py:19
  150.8 3.7 %fusion.14 = f32[256,2048]{1,0:T(8,128)} fusion(bf16[2048,256]{1,0:T(8,128)(2,1)S(1)} %bitcast.60, bf16[2048,2048]{1,0:T(8,128)(2,1)S(1)} %get-tuple-element.65), kind=kOutput, calls=%fused_computation.44 | convolution fusion | flops 2147483648 | bytes 11534336 | tf_op jit(solution)/shard_map/dot_general | solution.py:19
  154.5 9.7 %fusion.13 = f32[2048,512]{1,0:T(8,128)} fusion(bf16[2048,2048]{1,0:T(8,128)(2,1)} %tanh_convert_fusion, bf16[2048,512]{1,0:T(8,128)(2,1)S(1)} %bitcast.63), kind=kOutput, calls=%fused_computation.43 | convolution fusion | flops 4294967296 | bytes 14680064 | tf_op jit(solution)/shard_map/dot_general | solution.py:19
  164.5 2.1 %convert_reduce_fusion.1 = f32[512]{0:T(512)} fusion(bf16[1,2,512,512]{3,2,1,0:T(8,128)(2,1)} %bitcast.21, bf16[1,2,512,512]{3,2,1,0:T(8,128)(2,1)S(1)} %bitcast.58), kind=kLoop, calls=%fused_computation.7 | loop fusion | flops 3145216 | bytes 2099200 | tf_op jit(solution)/shard_map/reduce_sum | solution.py:283
  168.1 3.5 %fusion = f32[1024,1664]{1,0:T(8,128)S(1)} fusion(bf16[512,1664]{1,0:T(8,128)(2,1)} %collective-permute-done.5, bf16[512,1664]{1,0:T(8,128)(2,1)} %bitcast.23, pred[]{:T(512)S(6)} %eq.7), kind=kLoop, calls=%fused_computation.10 | loop fusion | flops 17039360 | bytes 10223617 | tf_op jit(solution)/shard_map/convert_element_type | solution.py:298
  175.3 2.6 %slice_bitcast_fusion = f32[1,1024,1024]{2,1,0:T(8,128)} fusion(f32[1024,1664]{1,0:T(8,128)S(1)} %fusion), kind=kLoop, calls=%fused_computation.6 | loop fusion | bytes 8388608 | tf_op jit(solution)/shard_map/broadcast_in_dim | solution.py:307
  (80 shorter events, 29.1 us)
Async XLA Ops:
  0.6 25.7 %copy-start = (bf16[2048,512]{1,0:T(8,128)(2,1)S(1)}, bf16[2048,512]{1,0:T(8,128)(2,1)}, u32[]{:S(2)}) copy-start(bf16[2048,512]{1,0:T(8,128)(2,1)} %param.18) | copy-start | bytes 6291460
  2.7 3.2 %copy-start.11 = (bf16[4,4096]{1,0:T(4,128)(2,1)S(1)}, bf16[4,4096]{1,0:T(4,128)(2,1)}, u32[]{:S(2)}) copy-start(bf16[4,4096]{1,0:T(4,128)(2,1)} %param.15) | copy-start | bytes 98308
  2.7 3.2 %copy-start.13 = (bf16[4,1024]{1,0:T(4,128)(2,1)S(1)}, bf16[4,1024]{1,0:T(4,128)(2,1)}, u32[]{:S(2)}) copy-start(bf16[4,1024]{1,0:T(4,128)(2,1)} %param.20) | copy-start | bytes 24580
  2.7 3.2 %copy-start.15 = (f32[1024]{0:T(1024)S(1)}, f32[1024]{0:T(1024)}, u32[]{:S(2)}) copy-start(f32[1024]{0:T(1024)} %param.21) | copy-start | bytes 12292
  4.3 3.0 %copy-start.16 = (f32[1,1024]{1,0:T(1,128)S(1)}, f32[1,1024]{1,0:T(1,128)}, u32[]{:S(2)}) copy-start(f32[1,1024]{1,0:T(1,128)} %param.23) | copy-start | bytes 12292
  4.3 14.4 %collective-permute-start = (bf16[512,2304]{1,0:T(8,128)(2,1)}, bf16[512,2304]{1,0:T(8,128)(2,1)}, u32[]{:S(2)}, u32[]{:S(2)}) collective-permute-start(bf16[512,2304]{1,0:T(8,128)(2,1)} %pad_maximum_fusion.1), channel_id=1, source_target_pairs={{0,32},{32,0},{1,33},{33,1},{2,34},{34,2},{3,35},{35,3},{4,36},{36... | collective-permute-start | bytes 7077896 | tf_op jit(solution)/shard_map/ppermute | solution.py:27
  7.3 5.3 %copy-start.19 = (bf16[2048,1024]{0,1:T(8,128)(2,1)}, bf16[2048,1024]{0,1:T(8,128)(2,1)S(1)}, u32[]{:S(2)}) copy-start(bf16[2048,1024]{0,1:T(8,128)(2,1)S(1)} %tanh_convert_fusion.3) | copy-start | bytes 12582916
  7.5 5.2 %copy-start.2 = (bf16[1024,512]{1,0:T(8,128)(2,1)S(1)}, bf16[1024,512]{1,0:T(8,128)(2,1)}, u32[]{:S(2)}) copy-start(bf16[1024,512]{1,0:T(8,128)(2,1)} %out_ref.1) | copy-start | bytes 3145732
  7.5 5.2 %copy-start.17 = (f32[512]{0:T(512)S(1)}, f32[512]{0:T(512)}, u32[]{:S(2)}) copy-start(f32[512]{0:T(512)} %param.25) | copy-start | bytes 6148
  12.7 2.6 %copy-start.20 = (bf16[2048,1024]{0,1:T(8,128)(2,1)}, bf16[2048,1024]{0,1:T(8,128)(2,1)S(1)}, u32[]{:S(2)}) copy-start(bf16[2048,1024]{0,1:T(8,128)(2,1)S(1)} %tanh_convert_fusion.2) | copy-start | bytes 12582916
  12.7 3.7 %copy-start.8 = (bf16[512,4096]{1,0:T(8,128)(2,1)S(1)}, bf16[512,4096]{1,0:T(8,128)(2,1)}, u32[]{:S(2)}) copy-start(bf16[512,4096]{1,0:T(8,128)(2,1)} %kept_ref.1) | copy-start | bytes 12582916
  16.4 5.9 %copy-start.21 = (bf16[2048,512]{0,1:T(8,128)(2,1)}, bf16[2048,512]{0,1:T(8,128)(2,1)S(1)}, u32[]{:S(2)}) copy-start(bf16[2048,512]{0,1:T(8,128)(2,1)S(1)} %tanh_convert_fusion.4) | copy-start | bytes 6291460
  20.5 5.8 %copy-start.14 = (f32[2048]{0:T(1024)S(1)}, f32[2048]{0:T(1024)}, u32[]{:S(2)}) copy-start(f32[2048]{0:T(1024)} %param.17) | copy-start | bytes 24580
  20.5 5.8 %copy-start.18 = (f32[512]{0:T(512)S(1)}, f32[512]{0:T(512)}, u32[]{:S(2)}) copy-start(f32[512]{0:T(512)} %param.19) | copy-start | bytes 6148
  20.5 14.2 %collective-permute-start.2 = (bf16[1024,256]{1,0:T(8,128)(2,1)S(1)}, bf16[1024,256]{1,0:T(8,128)(2,1)}, u32[]{:S(2)}, u32[]{:S(2)}) collective-permute-start(bf16[1024,256]{1,0:T(8,128)(2,1)S(1)} %pad_maximum_fusion.4), channel_id=1, source_target_pairs={{0,64},{64,0},{1,65},{65,1},{2,66},{66,2},{3,67},{67,3},{4,68},{68... | collective-permute-start | bytes 1572872 | tf_op jit(solution)/shard_map/ppermute | solution.py:27
  26.0 6.0 %collective-permute-start.1 = (bf16[512,512]{1,0:T(8,128)(2,1)}, bf16[512,512]{1,0:T(8,128)(2,1)}, u32[]{:S(2)}, u32[]{:S(2)}) collective-permute-start(bf16[512,512]{1,0:T(8,128)(2,1)} %fusion.7), channel_id=1, source_target_pairs={{0,32},{32,0},{1,33},{33,1},{2,34},{34,2},{3,35},{35,3},{4,36},{36... | collective-permute-start | bytes 1572872 | tf_op jit(solution)/shard_map/ppermute | solution.py:27
  34.7 37.1 %all-to-all-start = ((bf16[32,16,512]{2,1,0:T(8,128)(2,1)}), bf16[32,16,512]{2,1,0:T(8,128)(2,1)}, u32[]{:S(2)}, u32[]{:S(2)}) async-start(bf16[32,16,512]{2,1,0:T(8,128)(2,1)} %bitcast.64), calls=%async_computation | async-start | bytes 1048576 | tf_op jit(solution)/shard_map/all_to_all | solution.py:31
  71.8 4.5 %collective-permute-start.3 = (bf16[512,1664]{1,0:T(8,128)(2,1)}, bf16[512,1664]{1,0:T(8,128)(2,1)S(1)}, u32[]{:S(2)}, u32[]{:S(2)}) collective-permute-start(bf16[512,1664]{1,0:T(8,128)(2,1)} %copy-done.1), channel_id=1, source_target_pairs={{0,32},{32,0},{1,33},{33,1},{2,34},{34,2},{3,35},{35,3},{4,36},{36... | collective-permute-start | bytes 5111816 | tf_op jit(solution)/shard_map/ppermute | solution.py:27
  80.4 44.6 %all-to-all-start.1 = ((bf16[64,8,2688]{2,1,0:T(8,128)(2,1)}), bf16[64,8,2688]{2,1,0:T(8,128)(2,1)}, u32[]{:S(2)}, u32[]{:S(2)}) async-start(bf16[64,8,2688]{2,1,0:T(8,128)(2,1)} %pad_maximum_fusion), calls=%async_computation.1 | async-start | bytes 5505024 | tf_op jit(solution)/shard_map/all_to_all | solution.py:31
  129.4 9.6 %collective-permute-start.4 = (bf16[2,512,512]{2,1,0:T(8,128)(2,1)S(1)}, bf16[2,512,512]{2,1,0:T(8,128)(2,1)}, u32[]{:S(2)}, u32[]{:S(2)}) collective-permute-start(bf16[2,512,512]{2,1,0:T(8,128)(2,1)S(1)} %bitcast.56), channel_id=1, source_target_pairs={{0,32},{32,0},{1,33},{33,1},{2,34},{34,2},{3,35},{35,3},{4,36},{36... | collective-permute-start | bytes 3145736 | tf_op jit(solution)/shard_map/ppermute | solution.py:27
  131.7 32.5 %all-to-all-start.2 = ((bf16[64,8,1664]{2,1,0:T(8,128)(2,1)}), bf16[64,8,1664]{2,1,0:T(8,128)(2,1)}, u32[]{:S(2)}, u32[]{:S(2)}) async-start(bf16[64,8,1664]{2,1,0:T(8,128)(2,1)} %broadcast_in_dim.13), calls=%async_computation.2 | async-start | bytes 3407872 | tf_op jit(solution)/shard_map/all_to_all | solution.py:31
  141.7 9.1 %copy-start.6 = (bf16[2,2,512,256]{3,2,1,0:T(8,128)(2,1)S(1)}, bf16[2,2,512,256]{3,2,1,0:T(8,128)(2,1)}, u32[]{:S(2)}) copy-start(bf16[2,2,512,256]{3,2,1,0:T(8,128)(2,1)} %copy-done.5) | copy-start | bytes 3145732
  150.8 3.7 %copy-start.7 = (bf16[2,2,512,512]{3,2,1,0:T(8,128)(2,1)S(1)}, bf16[2,2,512,512]{3,2,1,0:T(8,128)(2,1)}, u32[]{:S(2)}) copy-start(bf16[2,2,512,512]{3,2,1,0:T(8,128)(2,1)} %pad_maximum_fusion.2) | copy-start | bytes 6291460
  164.2 3.9 %collective-permute-start.5 = (bf16[512,1664]{1,0:T(8,128)(2,1)}, bf16[512,1664]{1,0:T(8,128)(2,1)}, u32[]{:S(2)}, u32[]{:S(2)}) collective-permute-start(bf16[512,1664]{1,0:T(8,128)(2,1)} %bitcast.23), channel_id=1, source_target_pairs={{0,32},{32,0},{1,33},{33,1},{2,34},{34,2},{3,35},{35,3},{4,36},{36... | collective-permute-start | bytes 5111816 | tf_op jit(solution)/shard_map/ppermute | solution.py:27
  (7 other events, 8.9 us)
where the time goes:
time: 180 us; the launch traced here: 179 us
  matrix products  48.9 us (27%)
  starting transfers between devices  35.2 us (20%)
  waiting for transfers between devices  29.9 us (17%)
  Pallas kernels  23.3 us (13%)
  other arithmetic  20.8 us (12%)
  local copies, waits for them, and re-layouts  19.6 us (11%)
    dot_general x10, matrix products, dot(): lax.dot_general(left, right, (dims, ((), ())), preferred_element_type=F32)  48.9 us
    all_to_all x3, starting transfers between devices, exchange(): return lax.all_to_all(values, axes, split_axis=0, concat_axis=0, tiled=True)  28.1 us
    all_to_all x3, waiting for transfers between devices, exchange(): return lax.all_to_all(values, axes, split_axis=0, concat_axis=0, tiled=True)  25.8 us
    pallas_call x1, Pallas kernels, trunk_back(): pl.pallas_call(functools.partial(trunk_back_kernel, factor), grid_spec=pl...  23.3 us
    unnamed x45, local copies, waits for them, and re-layouts  7.49 us
    ppermute x6, starting transfers between devices, swap(): return lax.ppermute(values, axis, [(0, 1), (1, 0)])  7.13 us
    ppermute x6, waiting for transfers between devices, swap(): return lax.ppermute(values, axis, [(0, 1), (1, 0)])  4.12 us
  transfers between devices with their start and end apart: 9, of which 4 were waited for; matrix products, arithmetic and copies ran while one was open for 33% of the time, Pallas kernels for 13%

commit v1 on v0

--- a/solution.py
+++ b/solution.py
@@ -29,10 +29,6 @@
 
 def exchange(values, axes):
     return lax.all_to_all(values, axes, split_axis=0, concat_axis=0, tiled=True)
-
-
-def sum_parts(values):
-    return jnp.sum(values.astype(F32), axis=0)
 
 
 def tanh_layer(inputs, weights, offsets):
@@ -173,13 +169,229 @@
             jax.ShapeDtypeStruct((width // 2, columns), F32),
         ],
         compiler_params=pltpu.CompilerParams(
-            dimension_semantics=("arbitrary",), vmem_limit_bytes=48 * 1024 * 1024
+            dimension_semantics=("arbitrary",), vmem_limit_bytes=60 * 1024 * 1024
         ),
         cost_estimate=pl.CostEstimate(
             flops=product, bytes_accessed=24 * 1024 * 1024, transcendentals=0
         ),
         name="trunk_back",
     )(core.reshape(1), cotangent, theirs, coeffs, basis_vals, low, high, lead, out, mid)
+
+
+def call(kernel, grid, ins, outs, shapes, scratch, flops, moved, limit=60):
+    return pl.pallas_call(
+        kernel,
+        grid_spec=pltpu.PrefetchScalarGridSpec(
+            num_scalar_prefetch=1, grid=(grid,), in_specs=ins, out_specs=outs, scratch_shapes=scratch
+        ),
+        out_shape=shapes,
+        compiler_params=pltpu.CompilerParams(
+            dimension_semantics=("arbitrary",), vmem_limit_bytes=limit * 1024 * 1024
+        ),
+        cost_estimate=pl.CostEstimate(flops=flops, bytes_accessed=moved, transcendentals=0),
+    )
+
+
+def head_kernel(
+    core_ref,
+    kept_ref,
+    theirs_ref,
+    high_ref,
+    out_ref,
+    bias_ref,
+    basis_ref,
+    coef_ref,
+    flipped,
+    column,
+    mine,
+    other,
+):
+    step = pl.program_id(0)
+    scans = kept_ref.shape[0]
+    basis = basis_ref.shape[0]
+
+    @pl.when(step == 0)
+    def _():
+        flipped[...] = out_ref[...].T
+        column[...] = jnp.broadcast_to(bias_ref[...], (128, basis)).T
+        mine[...] = jnp.zeros_like(mine)
+        other[...] = jnp.zeros_like(other)
+
+    for at in range(0, basis, CHUNK):
+        rows = slice(at, at + CHUNK)
+        summed = dot(flipped[rows, :], high_ref[...], ((1,), (0,))) + column[rows, :1]
+        basis_ref[rows, :] = jnp.tanh(summed).astype(BF)
+    for at in range(0, basis, CHUNK):
+        rows = slice(at, at + CHUNK)
+        mine[:, rows] += dot(kept_ref[...], basis_ref[rows, :], ((1,), (1,)))
+        other[:, rows] += dot(theirs_ref[...], basis_ref[rows, :], ((1,), (1,)))
+
+    @pl.when(step == pl.num_programs(0) - 1)
+    def _():
+        core = core_ref[0]
+        coef_ref[pl.ds(pl.multiple_of(core * scans, scans), scans), :] = mine[...].astype(BF)
+        coef_ref[pl.ds(pl.multiple_of((1 - core) * scans, scans), scans), :] = other[...].astype(BF)
+
+
+def trunk_head(core, cotangent, theirs, high, out, bias):
+    width, half = high.shape
+    basis = out.shape[1]
+    scans = cotangent.shape[0]
+    steps = half // TILE
+    return call(
+        head_kernel,
+        steps,
+        [
+            pl.BlockSpec((scans, TILE), lambda i, c: (0, c[0] * steps + i)),
+            pl.BlockSpec((scans, TILE), lambda i, c: (0, i)),
+            pl.BlockSpec((width, TILE), lambda i, c: (0, i)),
+            pl.BlockSpec((width, basis), lambda i, c: (0, 0)),
+            pl.BlockSpec((1, basis), lambda i, c: (0, 0)),
+        ],
+        [
+            pl.BlockSpec((basis, TILE), lambda i, c: (0, i)),
+            pl.BlockSpec((2 * scans, basis), lambda i, c: (0, 0)),
+        ],
+        [
+            jax.ShapeDtypeStruct((basis, half), BF),
+            jax.ShapeDtypeStruct((2 * scans, basis), BF),
+        ],
+        [
+            pltpu.VMEM((basis, width), BF),
+            pltpu.VMEM((basis, 128), F32),
+            pltpu.VMEM((scans, basis), F32),
+            pltpu.VMEM((scans, basis), F32),
+        ],
+        2 * half * basis * (width + 2 * scans),
+        14 * 1024 * 1024,
+    )(core.reshape(1), cotangent, theirs, high, out, bias.reshape(1, basis))
+
+
+def load_kernel(factor, core_ref, parts_ref, mine_ref, swapped_ref, load_ref, coef):
+    columns = mine_ref.shape[1]
+    basis = parts_ref.shape[1]
+
+    @pl.when(pl.program_id(0) == 0)
+    def _():
+        total = jnp.zeros((16, basis), F32)
+        for at in range(0, parts_ref.shape[0], 16):
+            total += parts_ref[at : at + 16, :].astype(F32)
+        total = total * factor
+        flat = jnp.concatenate([total[:8], total[8:]], axis=1)
+        coef[...] = jnp.concatenate([flat, flat], axis=0).astype(BF)
+
+    load_ref[:, :columns] = (mine_ref[...] + swapped_ref[...].astype(F32)).astype(BF)
+    for at in range(0, load_ref.shape[0], 16):
+        load_ref[at : at + 16, columns:] = coef[...]
+
+
+def pack_load(core, parts, mine, swapped, factor):
+    rows, columns = mine.shape
+    basis = parts.shape[1]
+    tile = 128
+    return call(
+        functools.partial(load_kernel, factor),
+        rows // tile,
+        [
+            pl.BlockSpec(parts.shape, lambda i, c: (0, 0)),
+            pl.BlockSpec((tile, columns), lambda i, c: (i, 0)),
+            pl.BlockSpec((tile, columns), lambda i, c: (i, 0)),
+        ],
+        pl.BlockSpec((tile, columns + 2 * basis), lambda i, c: (i, 0)),
+        jax.ShapeDtypeStruct((rows, columns + 2 * basis), BF),
+        [pltpu.VMEM((16, 2 * basis), BF)],
+        0,
+        9 * 1024 * 1024,
+    )(core.reshape(1), parts, mine, swapped)
+
+
+def total_kernel(core_ref, got_ref, wide_ref, coef_ref):
+    rows, columns = wide_ref.shape
+    total = jnp.zeros((16, columns), F32)
+    for at in range(0, rows, 16):
+        total += got_ref[at : at + 16, :columns].astype(F32)
+        coef_ref[at : at + 16, :] = got_ref[at : at + 16, columns:]
+    total = total[:8] + total[8:]
+    both = jnp.concatenate([total, total], axis=0).astype(BF)
+    for at in range(0, rows, 16):
+        wide_ref[at : at + 16, :] = both
+
+
+def sum_spread(core, got, columns):
+    rows, wide = got.shape
+    return call(
+        total_kernel,
+        1,
+        [pl.BlockSpec((rows, wide), lambda i, c: (0, 0))],
+        [
+            pl.BlockSpec((rows, columns), lambda i, c: (0, 0)),
+            pl.BlockSpec((rows, wide - columns), lambda i, c: (0, 0)),
+        ],
+        [
+            jax.ShapeDtypeStruct((rows, columns), BF),
+            jax.ShapeDtypeStruct((rows, wide - columns), BF),
+        ],
+        [],
+        0,
+        2 * rows * wide * 2,
+    )(core.reshape(1), got)
+
+
+def unpack_kernel(core_ref, own_ref, *refs):
+    mid_ref, out_ref, in_ref, zero_ref, one_ref, two_ref = refs[-6:]
+    width, basis = mid_ref.shape[1], out_ref.shape[1]
+    mid_ref[...] = own_ref[:, :width].astype(F32)
+    out_ref[...] = own_ref[:, width : width + basis].astype(F32)
+    small = own_ref[:, width + basis :].astype(F32).T
+    in_ref[...] = small[:4]
+    zero_ref[...] = small[4:5]
+    one_ref[...] = small[5:6]
+    two_ref[...] = small[6:7]
+
+
+def unpack(side, own, width, basis, earlier=()):
+    rows, columns = own.shape
+    tile = 256
+    steps = rows // tile
+
+    def row(i, c):
+        return (c[0] * steps + i, 0)
+
+    def lane(i, c):
+        return (0, c[0] * steps + i)
+
+    return pl.pallas_call(
+        unpack_kernel,
+        grid_spec=pltpu.PrefetchScalarGridSpec(
+            num_scalar_prefetch=1,
+            grid=(steps,),
+            in_specs=[pl.BlockSpec((tile, columns), lambda i, c: (i, 0))]
+            + [pl.BlockSpec(memory_space=pl.ANY)] * len(earlier),
+            out_specs=[
+                pl.BlockSpec((tile, width), row),
+                pl.BlockSpec((tile, basis), row),
+                pl.BlockSpec((4, tile), lane),
+                pl.BlockSpec((1, tile), lane),
+                pl.BlockSpec((1, tile), lane),
+                pl.BlockSpec((1, tile), lane),
+            ],
+        ),
+        out_shape=[
+            jax.ShapeDtypeStruct((width, width), F32),
+            jax.ShapeDtypeStruct((width, basis), F32),
+            jax.ShapeDtypeStruct((4, width), F32),
+            jax.ShapeDtypeStruct((1, width), F32),
+            jax.ShapeDtypeStruct((1, width), F32),
+            jax.ShapeDtypeStruct((1, width), F32),
+        ],
+        input_output_aliases={2 + at: at for at in range(len(earlier))},
+        compiler_params=pltpu.CompilerParams(
+            dimension_semantics=("arbitrary",), vmem_limit_bytes=60 * 1024 * 1024
+        ),
+        cost_estimate=pl.CostEstimate(
+            flops=0, bytes_accessed=5 * 1024 * 1024, transcendentals=0
+        ),
+    )(side.reshape(1), own, *earlier)
 
 
 def on_device(
@@ -207,38 +419,33 @@
     basis = trunk_out.shape[1]
 
     zl = lax.axis_index("zl")
-    sent = lax.dynamic_slice_in_dim(cotangent, (1 - core) * half, half, 1)
-    pair_got = swap(jnp.concatenate([sent, scan_paths], axis=1), "core")
+    theirs = swap(lax.dynamic_slice_in_dim(cotangent, (1 - core) * half, half, 1), "core")
+    pair_paths = swap(scan_paths, "core")
     points = lax.dynamic_slice_in_dim(query_points, core * half, half, 1)
 
     trunk_0 = dot(trunk_in, points, ((0,), (0,))) + trunk_in_bias[:, None]
     trunk_0 = jnp.tanh(trunk_0).astype(BF)
     trunk_1 = dot(trunk_mid[0], trunk_0, ((0,), (0,))) + trunk_mid_bias[0][:, None]
     trunk_1 = jnp.tanh(trunk_1).astype(BF)
-    basis_vals = dot(trunk_out, trunk_1, ((0,), (0,))) + trunk_out_bias[:, None]
-    basis_vals = jnp.tanh(basis_vals).astype(BF)
-
-    local_paths = jnp.concatenate([scan_paths, pair_got[:, half:]], axis=0)
+    basis_vals, coef_part = trunk_head(
+        core, cotangent, theirs, trunk_1, trunk_out, trunk_out_bias
+    )
+
+    local_paths = jnp.concatenate([scan_paths, pair_paths], axis=0)
     side_paths = swap(local_paths, "zl")
-
-    coef_theirs = dot(pair_got[:, :half], basis_vals, ((1,), (1,))).astype(BF)
-    coef_swapped = swap(coef_theirs, "core")
-    kept = lax.dynamic_slice_in_dim(cotangent, core * half, half, 1)
-    coef_mine = dot(kept, basis_vals, ((1,), (1,)))
 
     hidden_local = tanh_layer(local_paths, branch_in, branch_in_bias)
     coeffs = dot(branch_out, hidden_local, ((0,), (1,))) + branch_out_bias[:, None]
     coeffs = coeffs.astype(BF)
 
-    coef_part = (coef_mine + coef_swapped.astype(F32)).astype(BF)
-    coef_part, coeffs, side_paths = lax.optimization_barrier((coef_part, coeffs, side_paths))
-    coef_parts = exchange(coef_part.reshape(pts, scan_rows // pts, basis), PTS)
+    coef_part, coeffs = lax.optimization_barrier((coef_part, coeffs))
+    coef_parts = exchange(coef_part, ("core",) + PTS)
 
     lead = jnp.concatenate([points, jnp.ones((1, half), BF), jnp.zeros((123, half), BF)], axis=0)
     other, mine = trunk_back(
         core,
         cotangent,
-        pair_got,
+        theirs,
         coeffs,
         basis_vals,
         trunk_0,
@@ -248,20 +455,10 @@
         trunk_mid[0],
         factor,
     )
-    coef_parts, other = lax.optimization_barrier((coef_parts, other))
-    coef_low = (factor * sum_parts(coef_parts)).astype(BF)
-
-    pair = (mine + swap(other, "core").astype(F32)).astype(BF)
-    columns = pair.shape[1]
-    rows = width // 2 // chips
-    coef_flat = jnp.concatenate([coef_low[:rows], coef_low[rows:]], axis=1)
-    load = jnp.concatenate(
-        [
-            pair.reshape(chips, rows, columns),
-            jnp.broadcast_to(coef_flat[None], (chips,) + coef_flat.shape),
-        ],
-        axis=2,
-    )
+    coef_parts, side_paths, other = lax.optimization_barrier((coef_parts, side_paths, other))
+
+    columns = mine.shape[1]
+    load = pack_load(core, coef_parts, mine, swap(other, "core"), factor)
     got = exchange(load, CHIPS)
     local = local_paths.reshape(2, scan_rows, -1)
     side = side_paths.reshape(2, scan_rows, -1)
@@ -270,44 +467,38 @@
     ).reshape(4 * scan_rows, -1)
     hidden = tanh_layer(paths, branch_in, branch_in_bias)
     got, hidden = lax.optimization_barrier((got, hidden))
-    total = sum_parts(got[:, :, :columns]).astype(BF)
-    wide = jnp.broadcast_to(total[None], (chips, rows, columns))
-    wide, got = lax.optimization_barrier((wide, got))
+    wide, coef_own = sum_spread(core, got, columns)
     spread = exchange(wide, CHIPS)
 
-    coef_own = jnp.stack([got[:, :, columns : columns + basis], got[:, :, columns + basis :]], 1)
-    coef_own = coef_own.reshape(2, scan_rows, basis)
-    coef_other = swap(coef_own, "core")
-    coef_all = jnp.stack([coef_own, coef_other]).reshape(4 * scan_rows, basis)
+    coef_all = jnp.stack([coef_own, swap(coef_own, "core")])
+    rows = coef_own.shape[0] // chips
+    coef_all = coef_all.reshape(2, chips, rows, 2, basis).transpose(0, 1, 3, 2, 4)
+    coef_all = coef_all.reshape(4 * scan_rows, basis)
     grad_branch_out = rows_rows(hidden, coef_all)
     grad_branch_out_bias = jnp.sum(coef_all.astype(F32), axis=0)
     branch_delta = (dot(coef_all, branch_out, ((1,), (1,))) * slope(hidden)).astype(BF)
     grad_branch_in = rows_rows(paths, branch_delta)
     grad_branch_in_bias = jnp.sum(branch_delta.astype(F32), axis=0)
 
-    spread, grad_branch_out, grad_branch_in = lax.optimization_barrier(
-        (spread, grad_branch_out, grad_branch_in)
-    )
-    spread = spread.reshape(width // 2, columns)
+    spread, grad_branch_out, grad_branch_in, grad_branch_out_bias = lax.optimization_barrier(
+        (spread, grad_branch_out, grad_branch_in, grad_branch_out_bias)
+    )
     spread_theirs = swap(spread, "core")
-
-    full = jnp.where(
-        core == 0,
-        jnp.concatenate([spread, spread_theirs], axis=0),
-        jnp.concatenate([spread_theirs, spread], axis=0),
-    ).astype(F32)
-    tail = full[:, width + basis :]
+    first = unpack(core, spread, width, basis)
+    grad_mid, grad_out, grad_in, bias_0, bias_1, bias_2 = unpack(
+        1 - core, spread_theirs, width, basis, first
+    )
     return (
         grad_branch_in,
         grad_branch_in_bias,
         grad_branch_out,
         grad_branch_out_bias,
-        tail[:, :4].T,
-        tail[:, 4],
-        full[:, :width][None],
-        tail[:, 5][None],
-        full[:, width : width + basis],
-        tail[:basis, 6],
+        grad_in,
+        bias_0[0],
+        grad_mid[None],
+        bias_1,
+        grad_out,
+        bias_2[0, :basis],
     )
 
 

time: 180 us -> 172 us (0.956)
  Pallas kernels: 23.3 us -> 49 us
  other arithmetic: 20.8 us -> 6.64 us
  local copies, waits for them, and re-layouts: 19.6 us -> 7.64 us
  matrix products: 48.9 us -> 41.9 us
    pallas_call x0 -> x5, Pallas kernels: none -> 23.9 us  [the longest x1 9.49 us: trunk_head(): call(head_kernel, steps, [pl.BlockSpec((scans, TILE), lambda i, c: (0, c[...]
    dot_general x10 -> x7, matrix products: 48.9 us -> 41.9 us  [dot(): lax.dot_general(left, right, (dims, ((), ())), preferred_element_type=F32)]
    convert_element_type x3 -> x0, other arithmetic: 5.81 us -> none  [the longest x1 3.49 us: on_device(): full = jnp.where(core == 0, jnp.concatenate([spread, spread_theirs], axis...]
    unnamed x45 -> x31, local copies, waits for them, and re-layouts: 7.49 us -> 2.19 us
    broadcast_in_dim x3 -> x0, local copies, waits for them, and re-layouts: 4.01 us -> none  [the longest x1 2.59 us: on_device(): full[:, :width][None]]
    concatenate x4 -> x0, other arithmetic: 3.4 us -> none  [the longest x1 1.75 us: on_device(): jnp.concatenate([pair.reshape(chips, rows, columns), jnp.broadcast_to(coe...]
    slice x5 -> x1, local copies, waits for them, and re-layouts: 4.62 us -> 1.26 us  [on_device(): bias_2[0, :basis]]
    reduce_sum x2 -> x0, other arithmetic: 2.84 us -> none  [sum_parts(): return jnp.sum(values.astype(F32), axis=0)]
  transfers between devices with their start and end apart: 9 -> 9, of which waited for: 4 -> 3; matrix products, arithmetic and copies ran while one was open for 33% -> 29% of each run, Pallas kernels for 13% -> 22%
where the time goes in v1:
time: 172 us; the launch traced here: 171 us
  Pallas kernels  49 us (28%)
  matrix products  41.9 us (24%)
  starting transfers between devices  34.3 us (20%)
  waiting for transfers between devices  31 us (18%)
  local copies, waits for them, and re-layouts  7.64 us (4%)
  other arithmetic  6.64 us (4%)
    dot_general x7, matrix products, dot(): lax.dot_general(left, right, (dims, ((), ())), preferred_element_type=F32)  41.9 us
    all_to_all x3, starting transfers between devices, exchange(): return lax.all_to_all(values, axes, split_axis=0, concat_axis=0, tiled=True)  28.3 us
    all_to_all x3, waiting for transfers between devices, exchange(): return lax.all_to_all(values, axes, split_axis=0, concat_axis=0, tiled=True)  26.8 us
    pallas_call x1, Pallas kernels, trunk_back(): pl.pallas_call(functools.partial(trunk_back_kernel, factor), grid_spec=pl...  25.1 us
    pallas_call x1, Pallas kernels, trunk_head(): call(head_kernel, steps, [pl.BlockSpec((scans, TILE), lambda i, c: (0, c[...  9.49 us
    ppermute x6, starting transfers between devices, swap(): return lax.ppermute(values, axis, [(0, 1), (1, 0)])  5.93 us
    pallas_call x2, Pallas kernels, unpack(): pl.pallas_call(unpack_kernel, grid_spec=pltpu.PrefetchScalarGridSpec(num_...  5.77 us
    pallas_call x1, Pallas kernels, pack_load(): call(functools.partial(load_kernel, factor), rows // tile, [pl.BlockSpec(...  5.29 us
  transfers between devices with their start and end apart: 9, of which 3 were waited for; matrix products, arithmetic and copies ran while one was open for 29% of the time, Pallas kernels for 22%

profile of v1, /device:TPU:1, one launch (start us, length us, event | category | flops | bytes accessed | tf_op | source)
XLA Modules:
  0.0 171.3 jit_solution(8023134755568890131)
XLA Ops:
  0.7 3.3 %constant_dynamic-slice_fusion.1 = bf16[512,2048]{1,0:T(8,128)(2,1)} fusion(bf16[512,4096]{1,0:T(8,128)(2,1)} %kept_ref.3, s32[]{:T(128)S(6)} %select_n.18), kind=kLoop, calls=%fused_computation.16 | loop fusion | bytes 4194308 | tf_op jit(solution)/shard_map/dynamic_slice | solution.py:422
  4.0 1.4 collective-permute-start
  7.2 6.4 %fusion.high_ref = bf16[1024,2048]{1,0:T(8,128)(2,1)} fusion(f32[1024]{0:T(1024)S(1)} %bitcast.59, bf16[2048,1024]{0,1:T(8,128)(2,1)S(1)} %tanh_convert_fusion.3, bf16[1,1024,1024]{2,1,0:T(8,128)(2,1)S(1)} %copy-done.8), kind=kOutput, calls=%fused_computation.6 | convolution fusion | flops 4299161600 | bytes 10489856 | tf_op jit(solution)/shard_map/dot_general | solution.py:19
  16.0 1.7 %collective-permute-start.2 = (bf16[1024,256]{1,0:T(8,128)(2,1)}, bf16[1024,256]{1,0:T(8,128)(2,1)}, u32[]{:S(2)}, u32[]{:S(2)}) collective-permute-start(bf16[1024,256]{1,0:T(8,128)(2,1)} %constant_dynamic-update-slice_fusion), channel_id=1, source_target_pairs={{0,64},{64,0},{1,65},{65,1},{2,66},{66,2},{3,67},{67,3},{4,68},{68... | collective-permute-start | bytes 1572872 | tf_op jit(solution)/shard_map/ppermute | solution.py:27
  17.8 5.9 %fusion.1.coeffs_ref = bf16[512,1024]{1,0:T(8,128)(2,1)} fusion(bf16[2048,512]{1,0:T(8,128)(2,1)S(1)} %copy-done, bf16[1024,256]{1,0:T(8,128)(2,1)} %constant_dynamic-update-slice_fusion, bf16[256,2048]{1,0:T(8,128)(2,1)} %param.16, f32[2048]{0:T(1024)S(1)} %copy-done.10, f32[512]{0:T(512)S(1)} %copy-done.13), kind=kOutput, calls=%fused_computation.10 | convolution fusion | flops 3226468352 | bytes 4728832 | tf_op jit(solution)/shard_map/dot_general | solution.py:19
  23.6 9.5 %shard_map.204 = (bf16[512,2048]{1,0:T(8,128)(2,1)}, bf16[1024,512]{1,0:T(8,128)(2,1)}) custom-call(s32[1]{0:T(128)} %bitcast.core_ref, bf16[512,4096]{1,0:T(8,128)(2,1)} %kept_ref.3, bf16[512,2048]{1,0:T(8,128)(2,1)} %collective-permute-done.theirs_ref, bf16[1024,2048]{1,0:T(8,128)(2,1)} %fusion.high_ref, bf16[1024,512]{1,0:T(8,128)(2,1)} %out_ref.3, ...), custom_call_target="tpu_custom_call" | custom-call | flops 4294967296 | bytes 14680064 | tf_op jit(solution)/shard_map/pallas_call | solution.py:241
  33.1 11.4 %all-to-all-start = ((bf16[64,16,512]{2,1,0:T(8,128)(2,1)}), bf16[64,16,512]{2,1,0:T(8,128)(2,1)S(1)}, u32[]{:S(2)}, u32[]{:S(2)}) async-start(bf16[64,16,512]{2,1,0:T(8,128)(2,1)} %bitcast.55), calls=%async_computation | async-start | bytes 2097152 | tf_op jit(solution)/shard_map/all_to_all | solution.py:31
  44.5 25.1 %trunk_back.1 = (bf16[512,1664]{1,0:T(8,128)(2,1)}, f32[512,1664]{1,0:T(8,128)}) custom-call(s32[1]{0:T(128)} %bitcast.core_ref, bf16[512,4096]{1,0:T(8,128)(2,1)} %kept_ref.3, bf16[512,2048]{1,0:T(8,128)(2,1)} %collective-permute-done.theirs_ref, bf16[512,1024]{1,0:T(8,128)(2,1)} %fusion.1.coeffs_ref, bf16[512,2048]{1,0:T(8,128)(2,1)} %get-tuple-element.42.basis_ref, ...), custom_call_target="tpu_custom_call" | custom-call | flops 15569256448 | bytes 25165824 | tf_op jit(solution)/shard_map/trunk_back/pallas_call | solution.py:139
  70.2 3.6 %collective-permute-done.3.swapped_ref = bf16[512,1664]{1,0:T(8,128)(2,1)} collective-permute-done((bf16[512,1664]{1,0:T(8,128)(2,1)}, bf16[512,1664]{1,0:T(8,128)(2,1)}, u32[]{:S(2)}, u32[]{:S(2)}) %collective-permute-start.3) | collective-permute-done | bytes 1703968 | tf_op jit(solution)/shard_map/ppermute | solution.py:27
  73.8 5.3 %shard_map.205 = bf16[512,2688]{1,0:T(8,128)(2,1)} custom-call(s32[1]{0:T(128)} %bitcast.core_ref, bf16[1024,512]{1,0:T(8,128)(2,1)} %bitcast.48, f32[512,1664]{1,0:T(8,128)} %get-tuple-element.45.mine_ref, bf16[512,1664]{1,0:T(8,128)(2,1)} %collective-permute-done.3.swapped_ref), custom_call_target="tpu_custom_call" | custom-call | bytes 9437184 | tf_op jit(solution)/shard_map/pallas_call | solution.py:292
  79.1 10.2 %all-to-all-start.1 = ((bf16[64,8,2688]{2,1,0:T(8,128)(2,1)}), bf16[64,8,2688]{2,1,0:T(8,128)(2,1)}, u32[]{:S(2)}, u32[]{:S(2)}) async-start(bf16[64,8,2688]{2,1,0:T(8,128)(2,1)} %bitcast.45), calls=%async_computation.1 | async-start | bytes 5505024 | tf_op jit(solution)/shard_map/all_to_all | solution.py:31
  89.3 1.8 %maximum_select_fusion = bf16[2,2,512,256]{3,2,1,0:T(8,128)(2,1)S(1)} fusion(bf16[2,1,512,256]{3,2,1,0:T(8,128)(2,1)} %bitcast.12, bf16[2,1,512,256]{3,2,1,0:T(8,128)(2,1)} %bitcast.11, pred[]{:T(512)S(6)} %eq.3), kind=kLoop, calls=%fused_computation.11 | loop fusion | flops 1572864 | bytes 2097153 | tf_op jit(solution)/shard_map/jit(_where)/select_n | solution.py:465
  91.0 5.8 %tanh_convert_fusion = bf16[2048,2048]{1,0:T(8,128)(2,1)} fusion(bf16[2048,256]{1,0:T(8,128)(2,1)S(1)} %bitcast.46, bf16[256,2048]{1,0:T(8,128)(2,1)} %param.16, f32[2048]{0:T(1024)S(1)} %copy-done.10), kind=kOutput, calls=%fused_computation.2 | convolution fusion | flops 2155872256 | bytes 10493952 | tf_op jit(solution)/shard_map/dot_general | solution.py:19
  96.8 26.8 %all-to-all-done.1 = bf16[64,8,2688]{2,1,0:T(8,128)(2,1)} async-done(((bf16[64,8,2688]{2,1,0:T(8,128)(2,1)}), bf16[64,8,2688]{2,1,0:T(8,128)(2,1)}, u32[]{:S(2)}, u32[]{:S(2)}) %all-to-all-start.1) | async-done | bytes 2752544 | tf_op jit(solution)/shard_map/all_to_all | solution.py:31
  123.6 3.4 %shard_map.206 = (bf16[512,1664]{1,0:T(8,128)(2,1)}, bf16[512,1024]{1,0:T(8,128)(2,1)}) custom-call(s32[1]{0:T(128)} %bitcast.core_ref, bf16[512,2688]{1,0:T(8,128)(2,1)} %bitcast.10.got_ref), custom_call_target="tpu_custom_call" | custom-call | bytes 5505024 | tf_op jit(solution)/shard_map/pallas_call | solution.py:322
  127.0 1.9 %collective-permute-start.4 = (bf16[512,1024]{1,0:T(8,128)(2,1)}, bf16[512,1024]{1,0:T(8,128)(2,1)}, u32[]{:S(2)}, u32[]{:S(2)}) collective-permute-start(bf16[512,1024]{1,0:T(8,128)(2,1)} %get-tuple-element.51), channel_id=1, source_target_pairs={{0,32},{32,0},{1,33},{33,1},{2,34},{34,2},{3,35},{35,3},{4,36},{36... | collective-permute-start | bytes 3145736 | tf_op jit(solution)/shard_map/ppermute | solution.py:27
  128.9 6.7 %all-to-all-start.2 = ((bf16[64,8,1664]{2,1,0:T(8,128)(2,1)}), bf16[64,8,1664]{2,1,0:T(8,128)(2,1)}, u32[]{:S(2)}, u32[]{:S(2)}) async-start(bf16[64,8,1664]{2,1,0:T(8,128)(2,1)} %bitcast.54), calls=%async_computation.2 | async-start | bytes 3407872 | tf_op jit(solution)/shard_map/all_to_all | solution.py:31
  135.7 1.7 %pad_maximum_fusion = bf16[2,64,8,2,512]{4,2,3,1,0:T(8,128)(2,1)S(1)} fusion(bf16[1,64,8,2,512]{4,2,3,1,0:T(8,128)(2,1)} %bitcast.17, bf16[1,64,8,2,512]{4,2,3,1,0:T(8,128)(2,1)} %bitcast.50), kind=kLoop, calls=%fused_computation.8 | loop fusion | flops 1048576 | bytes 4194304 | tf_op jit(solution)/shard_map/stack | solution.py:473
  137.4 9.1 %convert_reduce_fusion = (f32[2048]{0:T(1024)}, bf16[2048,2048]{1,0:T(8,128)(2,1)S(1)}) fusion(bf16[2048,2048]{1,0:T(8,128)(2,1)} %tanh_convert_fusion, bf16[2048,512]{1,0:T(8,128)(2,1)S(1)} %bitcast.52, bf16[2048,512]{1,0:T(8,128)(2,1)S(1)} %copy-done), kind=kOutput, calls=%fused_computation | convolution fusion | flops 4324325376 | bytes 20979712 | tf_op jit(solution)/shard_map/dot_general | solution.py:19
  146.5 3.7 %fusion.4 = f32[256,2048]{1,0:T(8,128)} fusion(bf16[2048,256]{1,0:T(8,128)(2,1)S(1)} %bitcast.47, bf16[2048,2048]{1,0:T(8,128)(2,1)S(1)} %get-tuple-element.69), kind=kOutput, calls=%fused_computation.19 | convolution fusion | flops 2147483648 | bytes 11534336 | tf_op jit(solution)/shard_map/dot_general | solution.py:19
  150.2 2.2 %convert_reduce_fusion.1 = f32[512]{0:T(512)} fusion(bf16[1,64,8,2,512]{4,2,3,1,0:T(8,128)(2,1)} %bitcast.17, bf16[1,64,8,2,512]{4,2,3,1,0:T(8,128)(2,1)S(1)} %bitcast.51), kind=kLoop, calls=%fused_computation.7 | loop fusion | flops 3145216 | bytes 2099200 | tf_op jit(solution)/shard_map/reduce_sum | solution.py:478
  152.4 9.7 %fusion.3 = f32[2048,512]{1,0:T(8,128)} fusion(bf16[2048,2048]{1,0:T(8,128)(2,1)} %tanh_convert_fusion, bf16[2048,512]{1,0:T(8,128)(2,1)S(1)} %bitcast.53), kind=kOutput, calls=%fused_computation.18 | convolution fusion | flops 4294967296 | bytes 14680064 | tf_op jit(solution)/shard_map/dot_general | solution.py:19
  162.4 2.9 %shard_map.207 = (f32[1024,1024]{1,0:T(8,128)}, f32[1024,512]{1,0:T(8,128)}, f32[4,1024]{1,0:T(4,128)}, f32[1,1024]{1,0:T(1,128)}, f32[1,1024]{1,0:T(1,128)}, /*index=5*/f32[1,1024]{1,0:T(1,128)}) custom-call(s32[1]{0:T(128)} %bitcast.core_ref, bf16[512,1664]{1,0:T(8,128)(2,1)} %bitcast.15.own_ref), custom_call_target="tpu_custom_call" | custom-call | bytes 5242880 | tf_op jit(solution)/shard_map/pallas_call | solution.py:363
  167.2 2.9 %shard_map.208 = (f32[1024,1024]{1,0:T(8,128)}, f32[1024,512]{1,0:T(8,128)}, f32[4,1024]{1,0:T(4,128)}, f32[1,1024]{1,0:T(1,128)}, f32[1,1024]{1,0:T(1,128)}, /*index=5*/f32[1,1024]{1,0:T(1,128)}) custom-call(s32[1]{0:T(128)} %bitcast.21.core_ref, ...), custom_call_target="tpu_custom_call", output_to_operand_aliasing={{0}: (2, {}), {1}: (3, {}), {2}: (4, {}), {3}: (5, {}), {4}... | custom-call | bytes 5242880 | tf_op jit(solution)/shard_map/pallas_call | solution.py:363
  (49 shorter events, 8.1 us)
Async XLA Ops:
  0.6 17.1 %copy-start = (bf16[2048,512]{1,0:T(8,128)(2,1)S(1)}, bf16[2048,512]{1,0:T(8,128)(2,1)}, u32[]{:S(2)}) copy-start(bf16[2048,512]{1,0:T(8,128)(2,1)} %param.18) | copy-start | bytes 6291460
  0.7 4.8 %copy-start.6 = (bf16[512,256]{1,0:T(8,128)(2,1)S(1)}, bf16[512,256]{1,0:T(8,128)(2,1)}, u32[]{:S(2)}) copy-start(bf16[512,256]{1,0:T(8,128)(2,1)} %param.14) | copy-start | bytes 786436
  0.7 5.0 %copy-start.7 = (bf16[4,4096]{1,0:T(4,128)(2,1)S(1)}, bf16[4,4096]{1,0:T(4,128)(2,1)}, u32[]{:S(2)}) copy-start(bf16[4,4096]{1,0:T(4,128)(2,1)} %param.15) | copy-start | bytes 98308
  0.7 5.0 %copy-start.9 = (bf16[4,1024]{1,0:T(4,128)(2,1)S(1)}, bf16[4,1024]{1,0:T(4,128)(2,1)}, u32[]{:S(2)}) copy-start(bf16[4,1024]{1,0:T(4,128)(2,1)} %param.20) | copy-start | bytes 24580
  0.7 5.0 %copy-start.11 = (f32[1024]{0:T(1024)S(1)}, f32[1024]{0:T(1024)}, u32[]{:S(2)}) copy-start(f32[1024]{0:T(1024)} %param.21) | copy-start | bytes 12292
  0.7 6.3 %copy-start.12 = (f32[1,1024]{1,0:T(1,128)S(1)}, f32[1,1024]{1,0:T(1,128)}, u32[]{:S(2)}) copy-start(f32[1,1024]{1,0:T(1,128)} %param.23) | copy-start | bytes 12292
  4.0 19.6 %collective-permute-start = (bf16[512,2048]{1,0:T(8,128)(2,1)}, bf16[512,2048]{1,0:T(8,128)(2,1)}, u32[]{:S(2)}, u32[]{:S(2)}) collective-permute-start(bf16[512,2048]{1,0:T(8,128)(2,1)} %constant_dynamic-slice_fusion.1), channel_id=1, source_target_pairs={{0,32},{32,0},{1,33},{33,1},{2,34},{34,2},{3,35},{35,3},{4,36},{36... | collective-permute-start | bytes 6291464 | tf_op jit(solution)/shard_map/ppermute | solution.py:27
  5.5 9.9 %collective-permute-start.1 = (bf16[512,256]{1,0:T(8,128)(2,1)S(1)}, bf16[512,256]{1,0:T(8,128)(2,1)S(1)}, u32[]{:S(2)}, u32[]{:S(2)}) collective-permute-start(bf16[512,256]{1,0:T(8,128)(2,1)S(1)} %copy-done.6), channel_id=1, source_target_pairs={{0,32},{32,0},{1,33},{33,1},{2,34},{34,2},{3,35},{35,3},{4,36},{36... | collective-permute-start | bytes 786440 | tf_op jit(solution)/shard_map/ppermute | solution.py:27
  5.6 1.6 copy-start.8
  7.0 6.6 %copy-start.14 = (bf16[2048,1024]{0,1:T(8,128)(2,1)}, bf16[2048,1024]{0,1:T(8,128)(2,1)S(1)}, u32[]{:S(2)}) copy-start(bf16[2048,1024]{0,1:T(8,128)(2,1)S(1)} %tanh_convert_fusion.3) | copy-start | bytes 12582916
  7.2 10.5 %copy-start.10 = (f32[2048]{0:T(1024)S(1)}, f32[2048]{0:T(1024)}, u32[]{:S(2)}) copy-start(f32[2048]{0:T(1024)} %param.17) | copy-start | bytes 24580
  7.2 10.5 %copy-start.13 = (f32[512]{0:T(512)S(1)}, f32[512]{0:T(512)}, u32[]{:S(2)}) copy-start(f32[512]{0:T(512)} %param.19) | copy-start | bytes 6148
  16.0 53.6 %collective-permute-start.2 = (bf16[1024,256]{1,0:T(8,128)(2,1)}, bf16[1024,256]{1,0:T(8,128)(2,1)}, u32[]{:S(2)}, u32[]{:S(2)}) collective-permute-start(bf16[1024,256]{1,0:T(8,128)(2,1)} %constant_dynamic-update-slice_fusion), channel_id=1, source_target_pairs={{0,64},{64,0},{1,65},{65,1},{2,66},{66,2},{3,67},{67,3},{4,68},{68... | collective-permute-start | bytes 1572872 | tf_op jit(solution)/shard_map/ppermute | solution.py:27
  33.1 36.5 %all-to-all-start = ((bf16[64,16,512]{2,1,0:T(8,128)(2,1)}), bf16[64,16,512]{2,1,0:T(8,128)(2,1)S(1)}, u32[]{:S(2)}, u32[]{:S(2)}) async-start(bf16[64,16,512]{2,1,0:T(8,128)(2,1)} %bitcast.55), calls=%async_computation | async-start | bytes 2097152 | tf_op jit(solution)/shard_map/all_to_all | solution.py:31
  69.6 4.2 %copy-start.1 = (bf16[64,16,512]{2,1,0:T(8,128)(2,1)}, bf16[64,16,512]{2,1,0:T(8,128)(2,1)S(1)}, u32[]{:S(2)}) copy-start(bf16[64,16,512]{2,1,0:T(8,128)(2,1)S(1)} %all-to-all-done) | copy-start | bytes 3145732
  69.6 4.2 %collective-permute-start.3 = (bf16[512,1664]{1,0:T(8,128)(2,1)}, bf16[512,1664]{1,0:T(8,128)(2,1)}, u32[]{:S(2)}, u32[]{:S(2)}) collective-permute-start(bf16[512,1664]{1,0:T(8,128)(2,1)} %get-tuple-element.46), channel_id=1, source_target_pairs={{0,32},{32,0},{1,33},{33,1},{2,34},{34,2},{3,35},{35,3},{4,36},{36... | collective-permute-start | bytes 5111816 | tf_op jit(solution)/shard_map/ppermute | solution.py:27
  79.1 44.6 %all-to-all-start.1 = ((bf16[64,8,2688]{2,1,0:T(8,128)(2,1)}), bf16[64,8,2688]{2,1,0:T(8,128)(2,1)}, u32[]{:S(2)}, u32[]{:S(2)}) async-start(bf16[64,8,2688]{2,1,0:T(8,128)(2,1)} %bitcast.45), calls=%async_computation.1 | async-start | bytes 5505024 | tf_op jit(solution)/shard_map/all_to_all | solution.py:31
  127.0 8.7 %collective-permute-start.4 = (bf16[512,1024]{1,0:T(8,128)(2,1)}, bf16[512,1024]{1,0:T(8,128)(2,1)}, u32[]{:S(2)}, u32[]{:S(2)}) collective-permute-start(bf16[512,1024]{1,0:T(8,128)(2,1)} %get-tuple-element.51), channel_id=1, source_target_pairs={{0,32},{32,0},{1,33},{33,1},{2,34},{34,2},{3,35},{35,3},{4,36},{36... | collective-permute-start | bytes 3145736 | tf_op jit(solution)/shard_map/ppermute | solution.py:27
  128.9 33.2 %all-to-all-start.2 = ((bf16[64,8,1664]{2,1,0:T(8,128)(2,1)}), bf16[64,8,1664]{2,1,0:T(8,128)(2,1)}, u32[]{:S(2)}, u32[]{:S(2)}) async-start(bf16[64,8,1664]{2,1,0:T(8,128)(2,1)} %bitcast.54), calls=%async_computation.2 | async-start | bytes 3407872 | tf_op jit(solution)/shard_map/all_to_all | solution.py:31
  137.4 9.1 %copy-start.3 = (bf16[2,64,8,2,512]{4,2,3,1,0:T(8,128)(2,1)}, bf16[2,64,8,2,512]{4,2,3,1,0:T(8,128)(2,1)S(1)}, u32[]{:S(2)}) copy-start(bf16[2,64,8,2,512]{4,2,3,1,0:T(8,128)(2,1)S(1)} %pad_maximum_fusion) | copy-start | bytes 6291460
  146.5 3.7 %copy-start.2 = (bf16[512,1024]{1,0:T(8,128)(2,1)S(1)}, bf16[512,1024]{1,0:T(8,128)(2,1)}, u32[]{:S(2)}) copy-start(bf16[512,1024]{1,0:T(8,128)(2,1)} %get-tuple-element.51) | copy-start | bytes 3145732
  146.5 5.9 %copy-start.4 = (bf16[2,64,8,2,512]{4,2,3,1,0:T(8,128)(2,1)S(1)}, bf16[2,64,8,2,512]{4,2,3,1,0:T(8,128)(2,1)}, u32[]{:S(2)}) copy-start(bf16[2,64,8,2,512]{4,2,3,1,0:T(8,128)(2,1)} %copy-done.3) | copy-start | bytes 6291460
  162.1 3.8 %collective-permute-start.5 = (bf16[512,1664]{1,0:T(8,128)(2,1)}, bf16[512,1664]{1,0:T(8,128)(2,1)S(1)}, u32[]{:S(2)}, u32[]{:S(2)}) collective-permute-start(bf16[512,1664]{1,0:T(8,128)(2,1)} %bitcast.15.own_ref), channel_id=1, source_target_pairs={{0,32},{32,0},{1,33},{33,1},{2,34},{34,2},{3,35},{35,3},{4,36},{36... | collective-permute-start | bytes 5111816 | tf_op jit(solution)/shard_map/ppermute | solution.py:27
  165.9 1.2 copy-start.5

commit v2 on v1

--- a/solution.py
+++ b/solution.py
@@ -41,6 +41,7 @@
 
 
 TILE = 512
+ROOM = 60
 CHUNK = 256
 
 
@@ -53,7 +54,7 @@
     basis_ref,
     low_ref,
     high_ref,
-    lead_ref,
+    points_ref,
     out_ref,
     mid_ref,
     other_ref,
@@ -66,6 +67,7 @@
     delta_2,
     delta_1,
     delta_0,
+    lead,
 ):
     step = pl.program_id(0)
     width, tile = low_ref.shape
@@ -76,6 +78,10 @@
     def _():
         for total in (sum_mid, sum_out, sum_lead, sum_one, sum_two):
             total[...] = jnp.zeros_like(total)
+        lead[...] = jnp.zeros_like(lead)
+
+    ones, blank = jnp.ones((1, tile), F32), jnp.zeros((11, tile), F32)
+    lead[:16, :] = jnp.concatenate([points_ref[...].astype(F32), ones, blank], axis=0).astype(BF)
 
     def lanes(values):
         return functools.reduce(
@@ -103,7 +109,7 @@
         rows = slice(at, at + CHUNK)
         sum_out[rows, :] += dot(high_ref[rows, :], delta_2[...], across)
         sum_mid[rows, :] += dot(low_ref[rows, :], delta_1[...], across)
-        sum_lead[rows, :] += dot(delta_0[rows, :], lead_ref[...], across)
+        sum_lead[rows, :] += dot(delta_0[rows, :], lead[...], across)
 
     @pl.when(step == pl.num_programs(0) - 1)
     def _():
@@ -122,7 +128,7 @@
                 at += total.shape[1]
 
 
-def trunk_back(core, cotangent, theirs, coeffs, basis_vals, low, high, lead, out, mid, factor):
+def trunk_back(core, cotangent, theirs, coeffs, basis_vals, low, high, points, out, mid, factor):
     width, half = low.shape
     basis = basis_vals.shape[0]
     scans = cotangent.shape[0]
@@ -130,7 +136,7 @@
     columns = width + basis + 128
 
     def whole(values):
-        return pl.BlockSpec(values.shape, lambda i, c: (0, 0))
+        return pl.BlockSpec(values.shape, lambda i, c: (0, 0), pipeline_mode=pl.Buffered(1))
 
     def part(rows):
         return pl.BlockSpec((rows, TILE), lambda i, c: (0, i))
@@ -148,7 +154,7 @@
                 part(basis),
                 part(width),
                 part(width),
-                part(128),
+                pl.BlockSpec((points.shape[0], TILE), lambda i, c: (0, c[0] * steps + i)),
                 whole(out),
                 whole(mid),
             ],
@@ -162,23 +168,24 @@
                 pltpu.VMEM((basis, TILE), BF),
                 pltpu.VMEM((width, TILE), BF),
                 pltpu.VMEM((width, TILE), BF),
+                pltpu.VMEM((128, TILE), BF),
             ],
         ),
         out_shape=[
             jax.ShapeDtypeStruct((width // 2, columns), BF),
-            jax.ShapeDtypeStruct((width // 2, columns), F32),
+            jax.ShapeDtypeStruct((width // 2, columns), BF),
         ],
         compiler_params=pltpu.CompilerParams(
-            dimension_semantics=("arbitrary",), vmem_limit_bytes=60 * 1024 * 1024
+            dimension_semantics=("arbitrary",), vmem_limit_bytes=ROOM * 1024 * 1024
         ),
         cost_estimate=pl.CostEstimate(
             flops=product, bytes_accessed=24 * 1024 * 1024, transcendentals=0
         ),
         name="trunk_back",
-    )(core.reshape(1), cotangent, theirs, coeffs, basis_vals, low, high, lead, out, mid)
-
-
-def call(kernel, grid, ins, outs, shapes, scratch, flops, moved, limit=60):
+    )(core.reshape(1), cotangent, theirs, coeffs, basis_vals, low, high, points, out, mid)
+
+
+def call(kernel, grid, ins, outs, shapes, scratch, flops, moved, limit=ROOM):
     return pl.pallas_call(
         kernel,
         grid_spec=pltpu.PrefetchScalarGridSpec(
@@ -280,7 +287,7 @@
         flat = jnp.concatenate([total[:8], total[8:]], axis=1)
         coef[...] = jnp.concatenate([flat, flat], axis=0).astype(BF)
 
-    load_ref[:, :columns] = (mine_ref[...] + swapped_ref[...].astype(F32)).astype(BF)
+    load_ref[:, :columns] = (mine_ref[...].astype(F32) + swapped_ref[...].astype(F32)).astype(BF)
     for at in range(0, load_ref.shape[0], 16):
         load_ref[at : at + 16, columns:] = coef[...]
 
@@ -288,7 +295,7 @@
 def pack_load(core, parts, mine, swapped, factor):
     rows, columns = mine.shape
     basis = parts.shape[1]
-    tile = 128
+    tile = 256
     return call(
         functools.partial(load_kernel, factor),
         rows // tile,
@@ -346,7 +353,8 @@
     in_ref[...] = small[:4]
     zero_ref[...] = small[4:5]
     one_ref[...] = small[5:6]
-    two_ref[...] = small[6:7]
+    kept = refs[5][...] if len(refs) > 6 else small[6:7]
+    two_ref[...] = jnp.where(core_ref[0] == 0, small[6:7], kept)
 
 
 def unpack(side, own, width, basis, earlier=()):
@@ -366,14 +374,15 @@
             num_scalar_prefetch=1,
             grid=(steps,),
             in_specs=[pl.BlockSpec((tile, columns), lambda i, c: (i, 0))]
-            + [pl.BlockSpec(memory_space=pl.ANY)] * len(earlier),
+            + [pl.BlockSpec(memory_space=pl.ANY)] * (len(earlier) - 1)
+            + [pl.BlockSpec((1, tile), lambda i, c: (0, i))] * (len(earlier) > 0),
             out_specs=[
                 pl.BlockSpec((tile, width), row),
                 pl.BlockSpec((tile, basis), row),
                 pl.BlockSpec((4, tile), lane),
                 pl.BlockSpec((1, tile), lane),
                 pl.BlockSpec((1, tile), lane),
-                pl.BlockSpec((1, tile), lane),
+                pl.BlockSpec((1, tile), lambda i, c: (0, i)),
             ],
         ),
         out_shape=[
@@ -382,11 +391,11 @@
             jax.ShapeDtypeStruct((4, width), F32),
             jax.ShapeDtypeStruct((1, width), F32),
             jax.ShapeDtypeStruct((1, width), F32),
-            jax.ShapeDtypeStruct((1, width), F32),
+            jax.ShapeDtypeStruct((1, basis), F32),
         ],
         input_output_aliases={2 + at: at for at in range(len(earlier))},
         compiler_params=pltpu.CompilerParams(
-            dimension_semantics=("arbitrary",), vmem_limit_bytes=60 * 1024 * 1024
+            dimension_semantics=("arbitrary",), vmem_limit_bytes=16 * 1024 * 1024
         ),
         cost_estimate=pl.CostEstimate(
             flops=0, bytes_accessed=5 * 1024 * 1024, transcendentals=0
@@ -418,9 +427,9 @@
     width = trunk_in.shape[1]
     basis = trunk_out.shape[1]
 
-    zl = lax.axis_index("zl")
     theirs = swap(lax.dynamic_slice_in_dim(cotangent, (1 - core) * half, half, 1), "core")
     pair_paths = swap(scan_paths, "core")
+    zl = lax.axis_index("zl")
     points = lax.dynamic_slice_in_dim(query_points, core * half, half, 1)
 
     trunk_0 = dot(trunk_in, points, ((0,), (0,))) + trunk_in_bias[:, None]
@@ -441,7 +450,6 @@
     coef_part, coeffs = lax.optimization_barrier((coef_part, coeffs))
     coef_parts = exchange(coef_part, ("core",) + PTS)
 
-    lead = jnp.concatenate([points, jnp.ones((1, half), BF), jnp.zeros((123, half), BF)], axis=0)
     other, mine = trunk_back(
         core,
         cotangent,
@@ -450,7 +458,7 @@
         basis_vals,
         trunk_0,
         trunk_1,
-        lead,
+        query_points,
         trunk_out,
         trunk_mid[0],
         factor,
@@ -498,7 +506,7 @@
         grad_mid[None],
         bias_1,
         grad_out,
-        bias_2[0, :basis],
+        bias_2[0],
     )
 
 

time: 172 us -> 166 us (0.965)
  Pallas kernels: 49 us -> 46.2 us
  local copies, waits for them, and re-layouts: 7.64 us -> 5.04 us
  transfers between devices with their start and end apart: 9 -> 9, of which waited for: 3 -> 3; matrix products, arithmetic and copies ran while one was open for 29% -> 30% of each run, Pallas kernels for 22% -> 22%
where the time goes in v2:
time: 166 us; the launch traced here: 165 us
  Pallas kernels  46.2 us (28%)
  matrix products  41.9 us (25%)
  starting transfers between devices  34.3 us (21%)
  waiting for transfers between devices  31 us (19%)
  other arithmetic  5.77 us (3%)
  local copies, waits for them, and re-layouts  5.04 us (3%)
    dot_general x7, matrix products, dot(): lax.dot_general(left, right, (dims, ((), ())), preferred_element_type=F32)  41.9 us
    all_to_all x3, starting transfers between devices, exchange(): return lax.all_to_all(values, axes, split_axis=0, concat_axis=0, tiled=True)  28.3 us
    all_to_all x3, waiting for transfers between devices, exchange(): return lax.all_to_all(values, axes, split_axis=0, concat_axis=0, tiled=True)  26.7 us
    pallas_call x1, Pallas kernels, trunk_back(): pl.pallas_call(functools.partial(trunk_back_kernel, factor), grid_spec=pl...  24.4 us
    pallas_call x1, Pallas kernels, trunk_head(): call(head_kernel, steps, [pl.BlockSpec((scans, TILE), lambda i, c: (0, c[...  9.45 us
    ppermute x6, starting transfers between devices, swap(): return lax.ppermute(values, axis, [(0, 1), (1, 0)])  5.96 us
    pallas_call x2, Pallas kernels, unpack(): pl.pallas_call(unpack_kernel, grid_spec=pltpu.PrefetchScalarGridSpec(num_...  5.29 us
    ppermute x6, waiting for transfers between devices, swap(): return lax.ppermute(values, axis, [(0, 1), (1, 0)])  4.21 us
  transfers between devices with their start and end apart: 9, of which 3 were waited for; matrix products, arithmetic and copies ran while one was open for 30% of the time, Pallas kernels for 22%

profile of v2, /device:TPU:1, one launch (start us, length us, event | category | flops | bytes accessed | tf_op | source)
XLA Modules:
  0.0 165.2 jit_solution(1313218310240718225)
XLA Ops:
  0.7 3.3 %constant_dynamic-slice_fusion = bf16[512,2048]{1,0:T(8,128)(2,1)} fusion(bf16[512,4096]{1,0:T(8,128)(2,1)} %kept_ref.3, s32[]{:T(128)S(6)} %select_n.18), kind=kLoop, calls=%fused_computation.16 | loop fusion | bytes 4194308 | tf_op jit(solution)/shard_map/dynamic_slice | solution.py:430
  4.0 1.4 collective-permute-start
  7.1 6.4 %fusion.high_ref = bf16[1024,2048]{1,0:T(8,128)(2,1)} fusion(f32[1024]{0:T(1024)S(1)} %bitcast.57, bf16[2048,1024]{0,1:T(8,128)(2,1)S(1)} %tanh_convert_fusion.3, bf16[1,1024,1024]{2,1,0:T(8,128)(2,1)S(1)} %copy-done.6), kind=kOutput, calls=%fused_computation.6 | convolution fusion | flops 4299161600 | bytes 10489856 | tf_op jit(solution)/shard_map/dot_general | solution.py:19
  15.0 1.7 %collective-permute-start.2 = (bf16[1024,256]{1,0:T(8,128)(2,1)}, bf16[1024,256]{1,0:T(8,128)(2,1)}, u32[]{:S(2)}, u32[]{:S(2)}) collective-permute-start(bf16[1024,256]{1,0:T(8,128)(2,1)} %constant_dynamic-update-slice_fusion), channel_id=1, source_target_pairs={{0,64},{64,0},{1,65},{65,1},{2,66},{66,2},{3,67},{67,3},{4,68},{68... | collective-permute-start | bytes 1572872 | tf_op jit(solution)/shard_map/ppermute | solution.py:27
  16.7 5.8 %fusion.1.coeffs_ref = bf16[512,1024]{1,0:T(8,128)(2,1)} fusion(bf16[2048,512]{1,0:T(8,128)(2,1)S(1)} %copy-done, bf16[1024,256]{1,0:T(8,128)(2,1)} %constant_dynamic-update-slice_fusion, bf16[256,2048]{1,0:T(8,128)(2,1)} %param.16, f32[2048]{0:T(1024)S(1)} %copy-done.9, f32[512]{0:T(512)S(1)} %copy-done.12), kind=kOutput, calls=%fused_computation.10 | convolution fusion | flops 3226468352 | bytes 4728832 | tf_op jit(solution)/shard_map/dot_general | solution.py:19
  22.6 9.5 %shard_map.204 = (bf16[512,2048]{1,0:T(8,128)(2,1)}, bf16[1024,512]{1,0:T(8,128)(2,1)}) custom-call(s32[1]{0:T(128)} %bitcast.core_ref, bf16[512,4096]{1,0:T(8,128)(2,1)} %kept_ref.3, bf16[512,2048]{1,0:T(8,128)(2,1)} %collective-permute-done.theirs_ref, bf16[1024,2048]{1,0:T(8,128)(2,1)} %fusion.high_ref, bf16[1024,512]{1,0:T(8,128)(2,1)} %out_ref.3, ...), custom_call_target="tpu_custom_call" | custom-call | flops 4294967296 | bytes 14680064 | tf_op jit(solution)/shard_map/pallas_call | solution.py:248
  32.0 11.4 %all-to-all-start = ((bf16[64,16,512]{2,1,0:T(8,128)(2,1)}), bf16[64,16,512]{2,1,0:T(8,128)(2,1)S(1)}, u32[]{:S(2)}, u32[]{:S(2)}) async-start(bf16[64,16,512]{2,1,0:T(8,128)(2,1)} %bitcast.53), calls=%async_computation | async-start | bytes 2097152 | tf_op jit(solution)/shard_map/all_to_all | solution.py:31
  43.4 24.4 %trunk_back.1 = (bf16[512,1664]{1,0:T(8,128)(2,1)}, bf16[512,1664]{1,0:T(8,128)(2,1)}) custom-call(s32[1]{0:T(128)} %bitcast.core_ref, bf16[512,4096]{1,0:T(8,128)(2,1)} %kept_ref.3, bf16[512,2048]{1,0:T(8,128)(2,1)} %collective-permute-done.theirs_ref, bf16[512,1024]{1,0:T(8,128)(2,1)} %fusion.1.coeffs_ref, bf16[512,2048]{1,0:T(8,128)(2,1)} %get-tuple-element.42.basis_ref, ...), custom_call_target="tpu_custom_call" | custom-call | flops 15569256448 | bytes 25165824 | tf_op jit(solution)/shard_map/trunk_back/pallas_call | solution.py:145
  68.5 3.6 %collective-permute-done.3.swapped_ref = bf16[512,1664]{1,0:T(8,128)(2,1)} collective-permute-done((bf16[512,1664]{1,0:T(8,128)(2,1)}, bf16[512,1664]{1,0:T(8,128)(2,1)}, u32[]{:S(2)}, u32[]{:S(2)}) %collective-permute-start.3) | collective-permute-done | bytes 1703968 | tf_op jit(solution)/shard_map/ppermute | solution.py:27
  72.0 3.7 %shard_map.205 = bf16[512,2688]{1,0:T(8,128)(2,1)} custom-call(s32[1]{0:T(128)} %bitcast.core_ref, bf16[1024,512]{1,0:T(8,128)(2,1)} %bitcast.46, bf16[512,1664]{1,0:T(8,128)(2,1)} %get-tuple-element.45.mine_ref, bf16[512,1664]{1,0:T(8,128)(2,1)} %collective-permute-done.3.swapped_ref), custom_call_target="tpu_custom_call" | custom-call | bytes 9437184 | tf_op jit(solution)/shard_map/pallas_call | solution.py:299
  75.7 10.2 %all-to-all-start.1 = ((bf16[64,8,2688]{2,1,0:T(8,128)(2,1)}), bf16[64,8,2688]{2,1,0:T(8,128)(2,1)}, u32[]{:S(2)}, u32[]{:S(2)}) async-start(bf16[64,8,2688]{2,1,0:T(8,128)(2,1)} %bitcast.43), calls=%async_computation.1 | async-start | bytes 5505024 | tf_op jit(solution)/shard_map/all_to_all | solution.py:31
  85.9 1.8 %maximum_select_fusion = bf16[2,2,512,256]{3,2,1,0:T(8,128)(2,1)S(1)} fusion(bf16[2,1,512,256]{3,2,1,0:T(8,128)(2,1)} %bitcast.12, bf16[2,1,512,256]{3,2,1,0:T(8,128)(2,1)} %bitcast.11, pred[]{:T(512)S(6)} %eq.3), kind=kLoop, calls=%fused_computation.11 | loop fusion | flops 1572864 | bytes 2097153 | tf_op jit(solution)/shard_map/jit(_where)/select_n | solution.py:473
  87.7 5.8 %tanh_convert_fusion = bf16[2048,2048]{1,0:T(8,128)(2,1)} fusion(bf16[2048,256]{1,0:T(8,128)(2,1)S(1)} %bitcast.44, bf16[256,2048]{1,0:T(8,128)(2,1)} %param.16, f32[2048]{0:T(1024)S(1)} %copy-done.9), kind=kOutput, calls=%fused_computation.2 | convolution fusion | flops 2155872256 | bytes 10493952 | tf_op jit(solution)/shard_map/dot_general | solution.py:19
  93.5 26.7 %all-to-all-done.1 = bf16[64,8,2688]{2,1,0:T(8,128)(2,1)} async-done(((bf16[64,8,2688]{2,1,0:T(8,128)(2,1)}), bf16[64,8,2688]{2,1,0:T(8,128)(2,1)}, u32[]{:S(2)}, u32[]{:S(2)}) %all-to-all-start.1) | async-done | bytes 2752544 | tf_op jit(solution)/shard_map/all_to_all | solution.py:31
  120.2 3.4 %shard_map.206 = (bf16[512,1664]{1,0:T(8,128)(2,1)}, bf16[512,1024]{1,0:T(8,128)(2,1)}) custom-call(s32[1]{0:T(128)} %bitcast.core_ref, bf16[512,2688]{1,0:T(8,128)(2,1)} %bitcast.10.got_ref), custom_call_target="tpu_custom_call" | custom-call | bytes 5505024 | tf_op jit(solution)/shard_map/pallas_call | solution.py:329
  123.6 1.9 %collective-permute-start.4 = (bf16[512,1024]{1,0:T(8,128)(2,1)}, bf16[512,1024]{1,0:T(8,128)(2,1)}, u32[]{:S(2)}, u32[]{:S(2)}) collective-permute-start(bf16[512,1024]{1,0:T(8,128)(2,1)} %get-tuple-element.51), channel_id=1, source_target_pairs={{0,32},{32,0},{1,33},{33,1},{2,34},{34,2},{3,35},{35,3},{4,36},{36... | collective-permute-start | bytes 3145736 | tf_op jit(solution)/shard_map/ppermute | solution.py:27
  125.5 6.8 %all-to-all-start.2 = ((bf16[64,8,1664]{2,1,0:T(8,128)(2,1)}), bf16[64,8,1664]{2,1,0:T(8,128)(2,1)}, u32[]{:S(2)}, u32[]{:S(2)}) async-start(bf16[64,8,1664]{2,1,0:T(8,128)(2,1)} %bitcast.52), calls=%async_computation.2 | async-start | bytes 3407872 | tf_op jit(solution)/shard_map/all_to_all | solution.py:31
  132.3 1.7 %pad_maximum_fusion = bf16[2,64,8,2,512]{4,2,3,1,0:T(8,128)(2,1)S(1)} fusion(bf16[1,64,8,2,512]{4,2,3,1,0:T(8,128)(2,1)} %bitcast.17, bf16[1,64,8,2,512]{4,2,3,1,0:T(8,128)(2,1)} %bitcast.47), kind=kLoop, calls=%fused_computation.8 | loop fusion | flops 1048576 | bytes 4194304 | tf_op jit(solution)/shard_map/stack | solution.py:481
  134.1 9.1 %convert_reduce_fusion = (f32[2048]{0:T(1024)}, bf16[2048,2048]{1,0:T(8,128)(2,1)S(1)}) fusion(bf16[2048,2048]{1,0:T(8,128)(2,1)} %tanh_convert_fusion, bf16[2048,512]{1,0:T(8,128)(2,1)S(1)} %bitcast.50, bf16[2048,512]{1,0:T(8,128)(2,1)S(1)} %copy-done), kind=kOutput, calls=%fused_computation | convolution fusion | flops 4324325376 | bytes 20979712 | tf_op jit(solution)/shard_map/dot_general | solution.py:19
  143.2 3.7 %fusion.6 = f32[256,2048]{1,0:T(8,128)} fusion(bf16[2048,256]{1,0:T(8,128)(2,1)S(1)} %bitcast.45, bf16[2048,2048]{1,0:T(8,128)(2,1)S(1)} %get-tuple-element.69), kind=kOutput, calls=%fused_computation.19 | convolution fusion | flops 2147483648 | bytes 11534336 | tf_op jit(solution)/shard_map/dot_general | solution.py:19
  146.9 2.2 %convert_reduce_fusion.1 = f32[512]{0:T(512)} fusion(bf16[1,64,8,2,512]{4,2,3,1,0:T(8,128)(2,1)} %bitcast.17, bf16[1,64,8,2,512]{4,2,3,1,0:T(8,128)(2,1)S(1)} %bitcast.48), kind=kLoop, calls=%fused_computation.7 | loop fusion | flops 3145216 | bytes 2099200 | tf_op jit(solution)/shard_map/reduce_sum | solution.py:486
  149.1 9.7 %fusion.5 = f32[2048,512]{1,0:T(8,128)} fusion(bf16[2048,2048]{1,0:T(8,128)(2,1)} %tanh_convert_fusion, bf16[2048,512]{1,0:T(8,128)(2,1)S(1)} %bitcast.51), kind=kOutput, calls=%fused_computation.18 | convolution fusion | flops 4294967296 | bytes 14680064 | tf_op jit(solution)/shard_map/dot_general | solution.py:19
  159.1 2.9 %shard_map.207 = (f32[1024,1024]{1,0:T(8,128)}, f32[1024,512]{1,0:T(8,128)}, f32[4,1024]{1,0:T(4,128)}, f32[1,1024]{1,0:T(1,128)}, f32[1,1024]{1,0:T(1,128)}, /*index=5*/f32[1,512]{1,0:T(1,128)}) custom-call(s32[1]{0:T(128)} %bitcast.core_ref, bf16[512,1664]{1,0:T(8,128)(2,1)} %bitcast.15.own_ref), custom_call_target="tpu_custom_call" | custom-call | bytes 5242880 | tf_op jit(solution)/shard_map/pallas_call | solution.py:371
  162.6 2.4 %shard_map.208 = (f32[1024,1024]{1,0:T(8,128)}, f32[1024,512]{1,0:T(8,128)}, f32[4,1024]{1,0:T(4,128)}, f32[1,1024]{1,0:T(1,128)}, f32[1,1024]{1,0:T(1,128)}, /*index=5*/f32[1,512]{1,0:T(1,128)}) custom-call(s32[1]{0:T(128)} %bitcast.21.core_ref, ...), custom_call_target="tpu_custom_call", output_to_operand_aliasing={{0}: (2, {}), {1}: (3, {}), {2}: (4, {}), {3}: (5, {}), {4}... | custom-call | bytes 5242880 | tf_op jit(solution)/shard_map/pallas_call | solution.py:371
  (41 shorter events, 4.6 us)
Async XLA Ops:
  0.6 16.1 %copy-start = (bf16[2048,512]{1,0:T(8,128)(2,1)S(1)}, bf16[2048,512]{1,0:T(8,128)(2,1)}, u32[]{:S(2)}) copy-start(bf16[2048,512]{1,0:T(8,128)(2,1)} %param.18) | copy-start | bytes 6291460
  0.7 4.8 %copy-start.5 = (bf16[512,256]{1,0:T(8,128)(2,1)S(1)}, bf16[512,256]{1,0:T(8,128)(2,1)}, u32[]{:S(2)}) copy-start(bf16[512,256]{1,0:T(8,128)(2,1)} %param.14) | copy-start | bytes 786436
  0.7 4.8 %copy-start.7 = (bf16[4,4096]{1,0:T(4,128)(2,1)S(1)}, bf16[4,4096]{1,0:T(4,128)(2,1)}, u32[]{:S(2)}) copy-start(bf16[4,4096]{1,0:T(4,128)(2,1)} %points_ref.1) | copy-start | bytes 98308
  0.7 4.8 %copy-start.8 = (bf16[4,1024]{1,0:T(4,128)(2,1)S(1)}, bf16[4,1024]{1,0:T(4,128)(2,1)}, u32[]{:S(2)}) copy-start(bf16[4,1024]{1,0:T(4,128)(2,1)} %param.20) | copy-start | bytes 24580
  0.7 4.8 %copy-start.10 = (f32[1024]{0:T(1024)S(1)}, f32[1024]{0:T(1024)}, u32[]{:S(2)}) copy-start(f32[1024]{0:T(1024)} %param.21) | copy-start | bytes 12292
  0.7 6.2 %copy-start.11 = (f32[1,1024]{1,0:T(1,128)S(1)}, f32[1,1024]{1,0:T(1,128)}, u32[]{:S(2)}) copy-start(f32[1,1024]{1,0:T(1,128)} %param.23) | copy-start | bytes 12292
  4.0 18.5 %collective-permute-start = (bf16[512,2048]{1,0:T(8,128)(2,1)}, bf16[512,2048]{1,0:T(8,128)(2,1)}, u32[]{:S(2)}, u32[]{:S(2)}) collective-permute-start(bf16[512,2048]{1,0:T(8,128)(2,1)} %constant_dynamic-slice_fusion), channel_id=1, source_target_pairs={{0,32},{32,0},{1,33},{33,1},{2,34},{34,2},{3,35},{35,3},{4,36},{36... | collective-permute-start | bytes 6291464 | tf_op jit(solution)/shard_map/ppermute | solution.py:27
  5.5 8.8 %collective-permute-start.1 = (bf16[512,256]{1,0:T(8,128)(2,1)S(1)}, bf16[512,256]{1,0:T(8,128)(2,1)S(1)}, u32[]{:S(2)}, u32[]{:S(2)}) collective-permute-start(bf16[512,256]{1,0:T(8,128)(2,1)S(1)} %copy-done.5), channel_id=1, source_target_pairs={{0,32},{32,0},{1,33},{33,1},{2,34},{34,2},{3,35},{35,3},{4,36},{36... | collective-permute-start | bytes 786440 | tf_op jit(solution)/shard_map/ppermute | solution.py:27
  5.5 1.6 copy-start.6
  6.9 6.7 %copy-start.13 = (bf16[2048,1024]{0,1:T(8,128)(2,1)}, bf16[2048,1024]{0,1:T(8,128)(2,1)S(1)}, u32[]{:S(2)}) copy-start(bf16[2048,1024]{0,1:T(8,128)(2,1)S(1)} %tanh_convert_fusion.3) | copy-start | bytes 12582916
  7.1 9.7 %copy-start.9 = (f32[2048]{0:T(1024)S(1)}, f32[2048]{0:T(1024)}, u32[]{:S(2)}) copy-start(f32[2048]{0:T(1024)} %param.17) | copy-start | bytes 24580
  7.1 9.7 %copy-start.12 = (f32[512]{0:T(512)S(1)}, f32[512]{0:T(512)}, u32[]{:S(2)}) copy-start(f32[512]{0:T(512)} %param.19) | copy-start | bytes 6148
  15.0 52.8 %collective-permute-start.2 = (bf16[1024,256]{1,0:T(8,128)(2,1)}, bf16[1024,256]{1,0:T(8,128)(2,1)}, u32[]{:S(2)}, u32[]{:S(2)}) collective-permute-start(bf16[1024,256]{1,0:T(8,128)(2,1)} %constant_dynamic-update-slice_fusion), channel_id=1, source_target_pairs={{0,64},{64,0},{1,65},{65,1},{2,66},{66,2},{3,67},{67,3},{4,68},{68... | collective-permute-start | bytes 1572872 | tf_op jit(solution)/shard_map/ppermute | solution.py:27
  32.0 35.8 %all-to-all-start = ((bf16[64,16,512]{2,1,0:T(8,128)(2,1)}), bf16[64,16,512]{2,1,0:T(8,128)(2,1)S(1)}, u32[]{:S(2)}, u32[]{:S(2)}) async-start(bf16[64,16,512]{2,1,0:T(8,128)(2,1)} %bitcast.53), calls=%async_computation | async-start | bytes 2097152 | tf_op jit(solution)/shard_map/all_to_all | solution.py:31
  67.8 4.2 %copy-start.1 = (bf16[64,16,512]{2,1,0:T(8,128)(2,1)}, bf16[64,16,512]{2,1,0:T(8,128)(2,1)S(1)}, u32[]{:S(2)}) copy-start(bf16[64,16,512]{2,1,0:T(8,128)(2,1)S(1)} %all-to-all-done) | copy-start | bytes 3145732
  67.9 4.2 %collective-permute-start.3 = (bf16[512,1664]{1,0:T(8,128)(2,1)}, bf16[512,1664]{1,0:T(8,128)(2,1)}, u32[]{:S(2)}, u32[]{:S(2)}) collective-permute-start(bf16[512,1664]{1,0:T(8,128)(2,1)} %get-tuple-element.46), channel_id=1, source_target_pairs={{0,32},{32,0},{1,33},{33,1},{2,34},{34,2},{3,35},{35,3},{4,36},{36... | collective-permute-start | bytes 5111816 | tf_op jit(solution)/shard_map/ppermute | solution.py:27
  75.7 44.5 %all-to-all-start.1 = ((bf16[64,8,2688]{2,1,0:T(8,128)(2,1)}), bf16[64,8,2688]{2,1,0:T(8,128)(2,1)}, u32[]{:S(2)}, u32[]{:S(2)}) async-start(bf16[64,8,2688]{2,1,0:T(8,128)(2,1)} %bitcast.43), calls=%async_computation.1 | async-start | bytes 5505024 | tf_op jit(solution)/shard_map/all_to_all | solution.py:31
  123.6 8.7 %collective-permute-start.4 = (bf16[512,1024]{1,0:T(8,128)(2,1)}, bf16[512,1024]{1,0:T(8,128)(2,1)}, u32[]{:S(2)}, u32[]{:S(2)}) collective-permute-start(bf16[512,1024]{1,0:T(8,128)(2,1)} %get-tuple-element.51), channel_id=1, source_target_pairs={{0,32},{32,0},{1,33},{33,1},{2,34},{34,2},{3,35},{35,3},{4,36},{36... | collective-permute-start | bytes 3145736 | tf_op jit(solution)/shard_map/ppermute | solution.py:27
  125.5 33.3 %all-to-all-start.2 = ((bf16[64,8,1664]{2,1,0:T(8,128)(2,1)}), bf16[64,8,1664]{2,1,0:T(8,128)(2,1)}, u32[]{:S(2)}, u32[]{:S(2)}) async-start(bf16[64,8,1664]{2,1,0:T(8,128)(2,1)} %bitcast.52), calls=%async_computation.2 | async-start | bytes 3407872 | tf_op jit(solution)/shard_map/all_to_all | solution.py:31
  134.1 9.1 %copy-start.3 = (bf16[2,64,8,2,512]{4,2,3,1,0:T(8,128)(2,1)}, bf16[2,64,8,2,512]{4,2,3,1,0:T(8,128)(2,1)S(1)}, u32[]{:S(2)}) copy-start(bf16[2,64,8,2,512]{4,2,3,1,0:T(8,128)(2,1)S(1)} %pad_maximum_fusion) | copy-start | bytes 6291460
  143.2 3.7 %copy-start.2 = (bf16[512,1024]{1,0:T(8,128)(2,1)S(1)}, bf16[512,1024]{1,0:T(8,128)(2,1)}, u32[]{:S(2)}) copy-start(bf16[512,1024]{1,0:T(8,128)(2,1)} %get-tuple-element.51) | copy-start | bytes 3145732
  143.2 5.9 %copy-start.4 = (bf16[2,64,8,2,512]{4,2,3,1,0:T(8,128)(2,1)S(1)}, bf16[2,64,8,2,512]{4,2,3,1,0:T(8,128)(2,1)}, u32[]{:S(2)}) copy-start(bf16[2,64,8,2,512]{4,2,3,1,0:T(8,128)(2,1)} %copy-done.3) | copy-start | bytes 6291460
  158.8 3.8 %collective-permute-start.5 = (bf16[512,1664]{1,0:T(8,128)(2,1)}, bf16[512,1664]{1,0:T(8,128)(2,1)S(1)}, u32[]{:S(2)}, u32[]{:S(2)}) collective-permute-start(bf16[512,1664]{1,0:T(8,128)(2,1)} %bitcast.15.own_ref), channel_id=1, source_target_pairs={{0,32},{32,0},{1,33},{33,1},{2,34},{34,2},{3,35},{35,3},{4,36},{36... | collective-permute-start | bytes 5111816 | tf_op jit(solution)/shard_map/ppermute | solution.py:27

commit v3 on v2

--- a/solution.py
+++ b/solution.py
@@ -46,12 +46,8 @@
 
 
 def trunk_back_kernel(
-    factor,
     core_ref,
-    kept_ref,
-    theirs_ref,
-    coeffs_ref,
-    basis_ref,
+    delta_2,
     low_ref,
     high_ref,
     points_ref,
@@ -64,15 +60,13 @@
     sum_lead,
     sum_one,
     sum_two,
-    delta_2,
     delta_1,
     delta_0,
     lead,
 ):
     step = pl.program_id(0)
     width, tile = low_ref.shape
-    basis = basis_ref.shape[0]
-    scans = kept_ref.shape[0]
+    basis = delta_2.shape[0]
 
     @pl.when(step == 0)
     def _():
@@ -89,13 +83,7 @@
         )
 
     plain, across = ((1,), (0,)), ((1,), (1,))
-    for at in range(0, basis, CHUNK):
-        rows = slice(at, at + CHUNK)
-        pulled = dot(coeffs_ref[rows, :scans], kept_ref[...], plain)
-        pulled += dot(coeffs_ref[rows, scans:], theirs_ref[...], plain)
-        delta = factor * pulled * slope(basis_ref[rows, :])
-        sum_two[rows, :] += lanes(delta)
-        delta_2[rows, :] = delta.astype(BF)
+    sum_two[...] += lanes(delta_2[...].astype(F32))
     for at in range(0, width, CHUNK):
         rows = slice(at, at + CHUNK)
         delta = dot(out_ref[rows, :], delta_2[...], plain) * slope(high_ref[rows, :])
@@ -128,10 +116,9 @@
                 at += total.shape[1]
 
 
-def trunk_back(core, cotangent, theirs, coeffs, basis_vals, low, high, points, out, mid, factor):
+def trunk_back(core, delta_2, low, high, points, out, mid):
     width, half = low.shape
-    basis = basis_vals.shape[0]
-    scans = cotangent.shape[0]
+    basis = delta_2.shape[0]
     steps = half // TILE
     columns = width + basis + 128
 
@@ -141,16 +128,13 @@
     def part(rows):
         return pl.BlockSpec((rows, TILE), lambda i, c: (0, i))
 
-    product = 2 * half * (2 * scans * basis + 2 * width * basis + 2 * width * width + width * 128)
+    product = 2 * half * (2 * width * basis + 2 * width * width + width * 128)
     return pl.pallas_call(
-        functools.partial(trunk_back_kernel, factor),
+        trunk_back_kernel,
         grid_spec=pltpu.PrefetchScalarGridSpec(
             num_scalar_prefetch=1,
             grid=(steps,),
             in_specs=[
-                pl.BlockSpec((scans, TILE), lambda i, c: (0, c[0] * steps + i)),
-                part(scans),
-                whole(coeffs),
                 part(basis),
                 part(width),
                 part(width),
@@ -165,7 +149,6 @@
                 pltpu.VMEM((width, 128), F32),
                 pltpu.VMEM((width, 128), F32),
                 pltpu.VMEM((basis, 128), F32),
-                pltpu.VMEM((basis, TILE), BF),
                 pltpu.VMEM((width, TILE), BF),
                 pltpu.VMEM((width, TILE), BF),
                 pltpu.VMEM((128, TILE), BF),
@@ -182,7 +165,7 @@
             flops=product, bytes_accessed=24 * 1024 * 1024, transcendentals=0
         ),
         name="trunk_back",
-    )(core.reshape(1), cotangent, theirs, coeffs, basis_vals, low, high, points, out, mid)
+    )(core.reshape(1), delta_2, low, high, points, out, mid)
 
 
 def call(kernel, grid, ins, outs, shapes, scratch, flops, moved, limit=ROOM):
@@ -199,15 +182,37 @@
     )
 
 
+def send_kernel(core_ref, field_ref, sent_ref):
+    sent_ref[...] = field_ref[...]
+
+
+def take_other_half(core, cotangent):
+    rows, columns = cotangent.shape
+    tile = 256
+    return call(
+        send_kernel,
+        rows // tile,
+        [pl.BlockSpec((tile, columns // 2), lambda i, c: (i, 1 - c[0]))],
+        pl.BlockSpec((tile, columns // 2), lambda i, c: (i, 0)),
+        jax.ShapeDtypeStruct((rows, columns // 2), BF),
+        [],
+        0,
+        2 * rows * columns,
+    )(core.reshape(1), cotangent)
+
+
 def head_kernel(
+    factor,
     core_ref,
     kept_ref,
     theirs_ref,
     high_ref,
+    coeffs_ref,
     out_ref,
     bias_ref,
+    delta_ref,
+    coef_ref,
     basis_ref,
-    coef_ref,
     flipped,
     column,
     mine,
@@ -232,6 +237,9 @@
         rows = slice(at, at + CHUNK)
         mine[:, rows] += dot(kept_ref[...], basis_ref[rows, :], ((1,), (1,)))
         other[:, rows] += dot(theirs_ref[...], basis_ref[rows, :], ((1,), (1,)))
+        pulled = dot(coeffs_ref[rows, :scans], kept_ref[...], ((1,), (0,)))
+        pulled += dot(coeffs_ref[rows, scans:], theirs_ref[...], ((1,), (0,)))
+        delta_ref[rows, :] = (factor * pulled * slope(basis_ref[rows, :])).astype(BF)
 
     @pl.when(step == pl.num_programs(0) - 1)
     def _():
@@ -240,18 +248,19 @@
         coef_ref[pl.ds(pl.multiple_of((1 - core) * scans, scans), scans), :] = other[...].astype(BF)
 
 
-def trunk_head(core, cotangent, theirs, high, out, bias):
+def trunk_head(core, cotangent, theirs, high, coeffs, out, bias, factor):
     width, half = high.shape
     basis = out.shape[1]
     scans = cotangent.shape[0]
     steps = half // TILE
     return call(
-        head_kernel,
+        functools.partial(head_kernel, factor),
         steps,
         [
             pl.BlockSpec((scans, TILE), lambda i, c: (0, c[0] * steps + i)),
             pl.BlockSpec((scans, TILE), lambda i, c: (0, i)),
             pl.BlockSpec((width, TILE), lambda i, c: (0, i)),
+            pl.BlockSpec((basis, 2 * scans), lambda i, c: (0, 0)),
             pl.BlockSpec((width, basis), lambda i, c: (0, 0)),
             pl.BlockSpec((1, basis), lambda i, c: (0, 0)),
         ],
@@ -264,14 +273,15 @@
             jax.ShapeDtypeStruct((2 * scans, basis), BF),
         ],
         [
+            pltpu.VMEM((basis, TILE), BF),
             pltpu.VMEM((basis, width), BF),
             pltpu.VMEM((basis, 128), F32),
             pltpu.VMEM((scans, basis), F32),
             pltpu.VMEM((scans, basis), F32),
         ],
-        2 * half * basis * (width + 2 * scans),
-        14 * 1024 * 1024,
-    )(core.reshape(1), cotangent, theirs, high, out, bias.reshape(1, basis))
+        2 * half * basis * (width + 4 * scans),
+        15 * 1024 * 1024,
+    )(core.reshape(1), cotangent, theirs, high, coeffs, out, bias.reshape(1, basis))
 
 
 def load_kernel(factor, core_ref, parts_ref, mine_ref, swapped_ref, load_ref, coef):
@@ -427,7 +437,7 @@
     width = trunk_in.shape[1]
     basis = trunk_out.shape[1]
 
-    theirs = swap(lax.dynamic_slice_in_dim(cotangent, (1 - core) * half, half, 1), "core")
+    theirs = swap(take_other_half(core, cotangent), "core")
     pair_paths = swap(scan_paths, "core")
     zl = lax.axis_index("zl")
     points = lax.dynamic_slice_in_dim(query_points, core * half, half, 1)
@@ -436,10 +446,6 @@
     trunk_0 = jnp.tanh(trunk_0).astype(BF)
     trunk_1 = dot(trunk_mid[0], trunk_0, ((0,), (0,))) + trunk_mid_bias[0][:, None]
     trunk_1 = jnp.tanh(trunk_1).astype(BF)
-    basis_vals, coef_part = trunk_head(
-        core, cotangent, theirs, trunk_1, trunk_out, trunk_out_bias
-    )
-
     local_paths = jnp.concatenate([scan_paths, pair_paths], axis=0)
     side_paths = swap(local_paths, "zl")
 
@@ -447,21 +453,13 @@
     coeffs = dot(branch_out, hidden_local, ((0,), (1,))) + branch_out_bias[:, None]
     coeffs = coeffs.astype(BF)
 
-    coef_part, coeffs = lax.optimization_barrier((coef_part, coeffs))
+    delta_2, coef_part = trunk_head(
+        core, cotangent, theirs, trunk_1, coeffs, trunk_out, trunk_out_bias, factor
+    )
     coef_parts = exchange(coef_part, ("core",) + PTS)
 
     other, mine = trunk_back(
-        core,
-        cotangent,
-        theirs,
-        coeffs,
-        basis_vals,
-        trunk_0,
-        trunk_1,
-        query_points,
-        trunk_out,
-        trunk_mid[0],
-        factor,
+        core, delta_2, trunk_0, trunk_1, query_points, trunk_out, trunk_mid[0]
     )
     coef_parts, side_paths, other = lax.optimization_barrier((coef_parts, side_paths, other))
 

time: 166 us -> 165 us (level)
  local copies, waits for them, and re-layouts: 5.04 us -> 1.71 us
  Pallas kernels: 46.2 us -> 48.5 us
    dynamic_slice x1 -> x0, local copies, waits for them, and re-layouts: 3.31 us -> none  [on_device(): lax.dynamic_slice_in_dim(cotangent, (1 - core) * half, half, 1)]
    pallas_call x2 -> x3, Pallas kernels: 33.9 us -> 35.7 us  [the longest x1 21.4 us: trunk_back(): pl.pallas_call(trunk_back_kernel, grid_spec=pltpu.PrefetchScalarGridSpec(...]
where the time goes in v3:
time: 165 us; the launch traced here: 164 us
  Pallas kernels  48.5 us (29%)
  matrix products  41.8 us (25%)
  starting transfers between devices  34.3 us (21%)
  waiting for transfers between devices  31.2 us (19%)
  other arithmetic  5.68 us (3%)
  local copies, waits for them, and re-layouts  1.71 us (1%)
    dot_general x7, matrix products, dot(): lax.dot_general(left, right, (dims, ((), ())), preferred_element_type=F32)  41.8 us
    all_to_all x3, starting transfers between devices, exchange(): return lax.all_to_all(values, axes, split_axis=0, concat_axis=0, tiled=True)  28.4 us
    all_to_all x3, waiting for transfers between devices, exchange(): return lax.all_to_all(values, axes, split_axis=0, concat_axis=0, tiled=True)  26.8 us
    pallas_call x1, Pallas kernels, trunk_back(): pl.pallas_call(trunk_back_kernel, grid_spec=pltpu.PrefetchScalarGridSpec(...  21.4 us
    pallas_call x1, Pallas kernels, trunk_head(): call(functools.partial(head_kernel, factor), steps, [pl.BlockSpec((scans,...  11.5 us
    ppermute x6, starting transfers between devices, swap(): return lax.ppermute(values, axis, [(0, 1), (1, 0)])  5.97 us
    pallas_call x2, Pallas kernels, unpack(): pl.pallas_call(unpack_kernel, grid_spec=pltpu.PrefetchScalarGridSpec(num_...  5.77 us
    ppermute x6, waiting for transfers between devices, swap(): return lax.ppermute(values, axis, [(0, 1), (1, 0)])  4.35 us
  transfers between devices with their start and end apart: 9, of which 3 were waited for; matrix products, arithmetic and copies ran while one was open for 30% of the time, Pallas kernels for 22%

profile of v3, /device:TPU:1, one launch (start us, length us, event | category | flops | bytes accessed | tf_op | source)
XLA Modules:
  0.0 164.2 jit_solution(14007851303048901336)
XLA Ops:
  0.7 2.8 %shard_map.204 = bf16[512,2048]{1,0:T(8,128)(2,1)} custom-call(s32[1]{0:T(128)} %bitcast.core_ref, bf16[512,4096]{1,0:T(8,128)(2,1)} %kept_ref.1), custom_call_target="tpu_custom_call" | custom-call | bytes 4194304 | tf_op jit(solution)/shard_map/pallas_call | solution.py:192
  3.5 1.4 collective-permute-start
  6.5 6.4 %fusion.high_ref = bf16[1024,2048]{1,0:T(8,128)(2,1)} fusion(f32[1024]{0:T(1024)S(1)} %bitcast.57, bf16[2048,1024]{0,1:T(8,128)(2,1)S(1)} %tanh_convert_fusion.3, bf16[1,1024,1024]{2,1,0:T(8,128)(2,1)S(1)} %copy-done.6), kind=kOutput, calls=%fused_computation.6 | convolution fusion | flops 4299161600 | bytes 10489856 | tf_op jit(solution)/shard_map/dot_general | solution.py:19
  14.4 1.7 %collective-permute-start.2 = (bf16[1024,256]{1,0:T(8,128)(2,1)}, bf16[1024,256]{1,0:T(8,128)(2,1)}, u32[]{:S(2)}, u32[]{:S(2)}) collective-permute-start(bf16[1024,256]{1,0:T(8,128)(2,1)} %constant_dynamic-update-slice_fusion), channel_id=1, source_target_pairs={{0,64},{64,0},{1,65},{65,1},{2,66},{66,2},{3,67},{67,3},{4,68},{68... | collective-permute-start | bytes 1572872 | tf_op jit(solution)/shard_map/ppermute | solution.py:27
  16.2 5.8 %fusion.1.coeffs_ref = bf16[512,1024]{1,0:T(8,128)(2,1)} fusion(bf16[2048,512]{1,0:T(8,128)(2,1)S(1)} %copy-done, bf16[1024,256]{1,0:T(8,128)(2,1)} %constant_dynamic-update-slice_fusion, bf16[256,2048]{1,0:T(8,128)(2,1)} %param.16, f32[2048]{0:T(1024)S(1)} %copy-done.9, f32[512]{0:T(512)S(1)} %copy-done.12), kind=kOutput, calls=%fused_computation.10 | convolution fusion | flops 3226468352 | bytes 4728832 | tf_op jit(solution)/shard_map/dot_general | solution.py:19
  22.0 11.5 %shard_map.205 = (bf16[512,2048]{1,0:T(8,128)(2,1)}, bf16[1024,512]{1,0:T(8,128)(2,1)}) custom-call(s32[1]{0:T(128)} %bitcast.core_ref, bf16[512,4096]{1,0:T(8,128)(2,1)} %kept_ref.1, bf16[512,2048]{1,0:T(8,128)(2,1)} %collective-permute-done.theirs_ref, bf16[1024,2048]{1,0:T(8,128)(2,1)} %fusion.high_ref, bf16[512,1024]{1,0:T(8,128)(2,1)} %fusion.1.coeffs_ref, ...), custom_call_target="tpu_custom_call" | custom-call | flops 6442450944 | bytes 15728640 | tf_op jit(solution)/shard_map/pallas_call | solution.py:256
  33.5 11.4 %all-to-all-start = ((bf16[64,16,512]{2,1,0:T(8,128)(2,1)}), bf16[64,16,512]{2,1,0:T(8,128)(2,1)S(1)}, u32[]{:S(2)}, u32[]{:S(2)}) async-start(bf16[64,16,512]{2,1,0:T(8,128)(2,1)} %bitcast.53), calls=%async_computation | async-start | bytes 2097152 | tf_op jit(solution)/shard_map/all_to_all | solution.py:31
  44.9 21.4 %trunk_back.1 = (bf16[512,1664]{1,0:T(8,128)(2,1)}, bf16[512,1664]{1,0:T(8,128)(2,1)}) custom-call(s32[1]{0:T(128)} %bitcast.core_ref, bf16[512,2048]{1,0:T(8,128)(2,1)} %get-tuple-element.38.delta_2, bf16[1024,2048]{1,0:T(8,128)(2,1)} %bitcast.59, bf16[1024,2048]{1,0:T(8,128)(2,1)} %fusion.high_ref, bf16[4,4096]{1,0:T(4,128)(2,1)} %points_ref.1, ...), custom_call_target="tpu_custom_call" | custom-call | flops 13421772800 | bytes 25165824 | tf_op jit(solution)/shard_map/trunk_back/pallas_call | solution.py:132
  66.9 3.6 %collective-permute-done.3.swapped_ref = bf16[512,1664]{1,0:T(8,128)(2,1)} collective-permute-done((bf16[512,1664]{1,0:T(8,128)(2,1)}, bf16[512,1664]{1,0:T(8,128)(2,1)}, u32[]{:S(2)}, u32[]{:S(2)}) %collective-permute-start.3) | collective-permute-done | bytes 1703968 | tf_op jit(solution)/shard_map/ppermute | solution.py:27
  70.4 3.7 %shard_map.206 = bf16[512,2688]{1,0:T(8,128)(2,1)} custom-call(s32[1]{0:T(128)} %bitcast.core_ref, bf16[1024,512]{1,0:T(8,128)(2,1)} %bitcast.46, bf16[512,1664]{1,0:T(8,128)(2,1)} %get-tuple-element.41.mine_ref, bf16[512,1664]{1,0:T(8,128)(2,1)} %collective-permute-done.3.swapped_ref), custom_call_target="tpu_custom_call" | custom-call | bytes 9437184 | tf_op jit(solution)/shard_map/pallas_call | solution.py:309
  74.1 10.2 %all-to-all-start.1 = ((bf16[64,8,2688]{2,1,0:T(8,128)(2,1)}), bf16[64,8,2688]{2,1,0:T(8,128)(2,1)}, u32[]{:S(2)}, u32[]{:S(2)}) async-start(bf16[64,8,2688]{2,1,0:T(8,128)(2,1)} %bitcast.43), calls=%async_computation.1 | async-start | bytes 5505024 | tf_op jit(solution)/shard_map/all_to_all | solution.py:31
  84.3 1.7 %maximum_select_fusion = bf16[2,2,512,256]{3,2,1,0:T(8,128)(2,1)S(1)} fusion(bf16[2,1,512,256]{3,2,1,0:T(8,128)(2,1)} %bitcast.12, bf16[2,1,512,256]{3,2,1,0:T(8,128)(2,1)} %bitcast.11, pred[]{:T(512)S(6)} %eq.3), kind=kLoop, calls=%fused_computation.11 | loop fusion | flops 1572864 | bytes 2097153 | tf_op jit(solution)/shard_map/jit(_where)/select_n | solution.py:471
  86.0 5.8 %tanh_convert_fusion = bf16[2048,2048]{1,0:T(8,128)(2,1)} fusion(bf16[2048,256]{1,0:T(8,128)(2,1)S(1)} %bitcast.44, bf16[256,2048]{1,0:T(8,128)(2,1)} %param.16, f32[2048]{0:T(1024)S(1)} %copy-done.9), kind=kOutput, calls=%fused_computation.2 | convolution fusion | flops 2155872256 | bytes 10493952 | tf_op jit(solution)/shard_map/dot_general | solution.py:19
  91.8 26.8 %all-to-all-done.1 = bf16[64,8,2688]{2,1,0:T(8,128)(2,1)} async-done(((bf16[64,8,2688]{2,1,0:T(8,128)(2,1)}), bf16[64,8,2688]{2,1,0:T(8,128)(2,1)}, u32[]{:S(2)}, u32[]{:S(2)}) %all-to-all-start.1) | async-done | bytes 2752544 | tf_op jit(solution)/shard_map/all_to_all | solution.py:31
  118.6 3.4 %shard_map.207 = (bf16[512,1664]{1,0:T(8,128)(2,1)}, bf16[512,1024]{1,0:T(8,128)(2,1)}) custom-call(s32[1]{0:T(128)} %bitcast.core_ref, bf16[512,2688]{1,0:T(8,128)(2,1)} %bitcast.10.got_ref), custom_call_target="tpu_custom_call" | custom-call | bytes 5505024 | tf_op jit(solution)/shard_map/pallas_call | solution.py:339
  122.0 1.9 %collective-permute-start.4 = (bf16[512,1024]{1,0:T(8,128)(2,1)}, bf16[512,1024]{1,0:T(8,128)(2,1)}, u32[]{:S(2)}, u32[]{:S(2)}) collective-permute-start(bf16[512,1024]{1,0:T(8,128)(2,1)} %get-tuple-element.47), channel_id=1, source_target_pairs={{0,32},{32,0},{1,33},{33,1},{2,34},{34,2},{3,35},{35,3},{4,36},{36... | collective-permute-start | bytes 3145736 | tf_op jit(solution)/shard_map/ppermute | solution.py:27
  123.9 6.8 %all-to-all-start.2 = ((bf16[64,8,1664]{2,1,0:T(8,128)(2,1)}), bf16[64,8,1664]{2,1,0:T(8,128)(2,1)}, u32[]{:S(2)}, u32[]{:S(2)}) async-start(bf16[64,8,1664]{2,1,0:T(8,128)(2,1)} %bitcast.52), calls=%async_computation.2 | async-start | bytes 3407872 | tf_op jit(solution)/shard_map/all_to_all | solution.py:31
  130.8 1.7 %pad_maximum_fusion = bf16[2,64,8,2,512]{4,2,3,1,0:T(8,128)(2,1)S(1)} fusion(bf16[1,64,8,2,512]{4,2,3,1,0:T(8,128)(2,1)} %bitcast.17, bf16[1,64,8,2,512]{4,2,3,1,0:T(8,128)(2,1)} %bitcast.47), kind=kLoop, calls=%fused_computation.8 | loop fusion | flops 1048576 | bytes 4194304 | tf_op jit(solution)/shard_map/stack | solution.py:479
  132.5 9.1 %convert_reduce_fusion = (f32[2048]{0:T(1024)}, bf16[2048,2048]{1,0:T(8,128)(2,1)S(1)}) fusion(bf16[2048,2048]{1,0:T(8,128)(2,1)} %tanh_convert_fusion, bf16[2048,512]{1,0:T(8,128)(2,1)S(1)} %bitcast.50, bf16[2048,512]{1,0:T(8,128)(2,1)S(1)} %copy-done), kind=kOutput, calls=%fused_computation | convolution fusion | flops 4324325376 | bytes 20979712 | tf_op jit(solution)/shard_map/dot_general | solution.py:19
  141.6 3.7 %fusion.6 = f32[256,2048]{1,0:T(8,128)} fusion(bf16[2048,256]{1,0:T(8,128)(2,1)S(1)} %bitcast.45, bf16[2048,2048]{1,0:T(8,128)(2,1)S(1)} %get-tuple-element.65), kind=kOutput, calls=%fused_computation.18 | convolution fusion | flops 2147483648 | bytes 11534336 | tf_op jit(solution)/shard_map/dot_general | solution.py:19
  145.3 2.2 %convert_reduce_fusion.1 = f32[512]{0:T(512)} fusion(bf16[1,64,8,2,512]{4,2,3,1,0:T(8,128)(2,1)} %bitcast.17, bf16[1,64,8,2,512]{4,2,3,1,0:T(8,128)(2,1)S(1)} %bitcast.48), kind=kLoop, calls=%fused_computation.7 | loop fusion | flops 3145216 | bytes 2099200 | tf_op jit(solution)/shard_map/reduce_sum | solution.py:484
  147.5 9.7 %fusion.5 = f32[2048,512]{1,0:T(8,128)} fusion(bf16[2048,2048]{1,0:T(8,128)(2,1)} %tanh_convert_fusion, bf16[2048,512]{1,0:T(8,128)(2,1)S(1)} %bitcast.51), kind=kOutput, calls=%fused_computation.17 | convolution fusion | flops 4294967296 | bytes 14680064 | tf_op jit(solution)/shard_map/dot_general | solution.py:19
  157.5 2.9 %shard_map.208 = (f32[1024,1024]{1,0:T(8,128)}, f32[1024,512]{1,0:T(8,128)}, f32[4,1024]{1,0:T(4,128)}, f32[1,1024]{1,0:T(1,128)}, f32[1,1024]{1,0:T(1,128)}, /*index=5*/f32[1,512]{1,0:T(1,128)}) custom-call(s32[1]{0:T(128)} %bitcast.core_ref, bf16[512,1664]{1,0:T(8,128)(2,1)} %bitcast.15.own_ref), custom_call_target="tpu_custom_call" | custom-call | bytes 5242880 | tf_op jit(solution)/shard_map/pallas_call | solution.py:381
  161.2 2.9 %shard_map.209 = (f32[1024,1024]{1,0:T(8,128)}, f32[1024,512]{1,0:T(8,128)}, f32[4,1024]{1,0:T(4,128)}, f32[1,1024]{1,0:T(1,128)}, f32[1,1024]{1,0:T(1,128)}, /*index=5*/f32[1,512]{1,0:T(1,128)}) custom-call(s32[1]{0:T(128)} %bitcast.21.core_ref, ...), custom_call_target="tpu_custom_call", output_to_operand_aliasing={{0}: (2, {}), {1}: (3, {}), {2}: (4, {}), {3}: (5, {}), {4}... | custom-call | bytes 5242880 | tf_op jit(solution)/shard_map/pallas_call | solution.py:381
  (41 shorter events, 4.7 us)
Async XLA Ops:
  0.6 15.5 %copy-start = (bf16[2048,512]{1,0:T(8,128)(2,1)S(1)}, bf16[2048,512]{1,0:T(8,128)(2,1)}, u32[]{:S(2)}) copy-start(bf16[2048,512]{1,0:T(8,128)(2,1)} %param.18) | copy-start | bytes 6291460
  0.7 4.3 %copy-start.5 = (bf16[512,256]{1,0:T(8,128)(2,1)S(1)}, bf16[512,256]{1,0:T(8,128)(2,1)}, u32[]{:S(2)}) copy-start(bf16[512,256]{1,0:T(8,128)(2,1)} %param.14) | copy-start | bytes 786436
  0.7 4.3 %copy-start.7 = (bf16[4,4096]{1,0:T(4,128)(2,1)S(1)}, bf16[4,4096]{1,0:T(4,128)(2,1)}, u32[]{:S(2)}) copy-start(bf16[4,4096]{1,0:T(4,128)(2,1)} %points_ref.1) | copy-start | bytes 98308
  0.7 4.2 %copy-start.8 = (bf16[4,1024]{1,0:T(4,128)(2,1)S(1)}, bf16[4,1024]{1,0:T(4,128)(2,1)}, u32[]{:S(2)}) copy-start(bf16[4,1024]{1,0:T(4,128)(2,1)} %param.20) | copy-start | bytes 24580
  0.7 4.2 %copy-start.10 = (f32[1024]{0:T(1024)S(1)}, f32[1024]{0:T(1024)}, u32[]{:S(2)}) copy-start(f32[1024]{0:T(1024)} %param.21) | copy-start | bytes 12292
  0.7 5.6 %copy-start.11 = (f32[1,1024]{1,0:T(1,128)S(1)}, f32[1,1024]{1,0:T(1,128)}, u32[]{:S(2)}) copy-start(f32[1,1024]{1,0:T(1,128)} %param.23) | copy-start | bytes 12292
  3.5 18.5 %collective-permute-start = (bf16[512,2048]{1,0:T(8,128)(2,1)}, bf16[512,2048]{1,0:T(8,128)(2,1)}, u32[]{:S(2)}, u32[]{:S(2)}) collective-permute-start(bf16[512,2048]{1,0:T(8,128)(2,1)} %shard_map.204), channel_id=1, source_target_pairs={{0,32},{32,0},{1,33},{33,1},{2,34},{34,2},{3,35},{35,3},{4,36},{36... | collective-permute-start | bytes 6291464 | tf_op jit(solution)/shard_map/ppermute | solution.py:27
  4.9 8.8 %collective-permute-start.1 = (bf16[512,256]{1,0:T(8,128)(2,1)S(1)}, bf16[512,256]{1,0:T(8,128)(2,1)S(1)}, u32[]{:S(2)}, u32[]{:S(2)}) collective-permute-start(bf16[512,256]{1,0:T(8,128)(2,1)S(1)} %copy-done.5), channel_id=1, source_target_pairs={{0,32},{32,0},{1,33},{33,1},{2,34},{34,2},{3,35},{35,3},{4,36},{36... | collective-permute-start | bytes 786440 | tf_op jit(solution)/shard_map/ppermute | solution.py:27
  4.9 1.6 copy-start.6
  6.3 6.7 %copy-start.13 = (bf16[2048,1024]{0,1:T(8,128)(2,1)}, bf16[2048,1024]{0,1:T(8,128)(2,1)S(1)}, u32[]{:S(2)}) copy-start(bf16[2048,1024]{0,1:T(8,128)(2,1)S(1)} %tanh_convert_fusion.3) | copy-start | bytes 12582916
  6.5 9.6 %copy-start.9 = (f32[2048]{0:T(1024)S(1)}, f32[2048]{0:T(1024)}, u32[]{:S(2)}) copy-start(f32[2048]{0:T(1024)} %param.17) | copy-start | bytes 24580
  6.5 9.6 %copy-start.12 = (f32[512]{0:T(512)S(1)}, f32[512]{0:T(512)}, u32[]{:S(2)}) copy-start(f32[512]{0:T(512)} %param.19) | copy-start | bytes 6148
  14.4 51.8 %collective-permute-start.2 = (bf16[1024,256]{1,0:T(8,128)(2,1)}, bf16[1024,256]{1,0:T(8,128)(2,1)}, u32[]{:S(2)}, u32[]{:S(2)}) collective-permute-start(bf16[1024,256]{1,0:T(8,128)(2,1)} %constant_dynamic-update-slice_fusion), channel_id=1, source_target_pairs={{0,64},{64,0},{1,65},{65,1},{2,66},{66,2},{3,67},{67,3},{4,68},{68... | collective-permute-start | bytes 1572872 | tf_op jit(solution)/shard_map/ppermute | solution.py:27
  33.5 32.8 %all-to-all-start = ((bf16[64,16,512]{2,1,0:T(8,128)(2,1)}), bf16[64,16,512]{2,1,0:T(8,128)(2,1)S(1)}, u32[]{:S(2)}, u32[]{:S(2)}) async-start(bf16[64,16,512]{2,1,0:T(8,128)(2,1)} %bitcast.53), calls=%async_computation | async-start | bytes 2097152 | tf_op jit(solution)/shard_map/all_to_all | solution.py:31
  66.3 4.2 %copy-start.1 = (bf16[64,16,512]{2,1,0:T(8,128)(2,1)}, bf16[64,16,512]{2,1,0:T(8,128)(2,1)S(1)}, u32[]{:S(2)}) copy-start(bf16[64,16,512]{2,1,0:T(8,128)(2,1)S(1)} %all-to-all-done) | copy-start | bytes 3145732
  66.3 4.2 %collective-permute-start.3 = (bf16[512,1664]{1,0:T(8,128)(2,1)}, bf16[512,1664]{1,0:T(8,128)(2,1)}, u32[]{:S(2)}, u32[]{:S(2)}) collective-permute-start(bf16[512,1664]{1,0:T(8,128)(2,1)} %get-tuple-element.42), channel_id=1, source_target_pairs={{0,32},{32,0},{1,33},{33,1},{2,34},{34,2},{3,35},{35,3},{4,36},{36... | collective-permute-start | bytes 5111816 | tf_op jit(solution)/shard_map/ppermute | solution.py:27
  74.1 44.5 %all-to-all-start.1 = ((bf16[64,8,2688]{2,1,0:T(8,128)(2,1)}), bf16[64,8,2688]{2,1,0:T(8,128)(2,1)}, u32[]{:S(2)}, u32[]{:S(2)}) async-start(bf16[64,8,2688]{2,1,0:T(8,128)(2,1)} %bitcast.43), calls=%async_computation.1 | async-start | bytes 5505024 | tf_op jit(solution)/shard_map/all_to_all | solution.py:31
  122.0 8.8 %collective-permute-start.4 = (bf16[512,1024]{1,0:T(8,128)(2,1)}, bf16[512,1024]{1,0:T(8,128)(2,1)}, u32[]{:S(2)}, u32[]{:S(2)}) collective-permute-start(bf16[512,1024]{1,0:T(8,128)(2,1)} %get-tuple-element.47), channel_id=1, source_target_pairs={{0,32},{32,0},{1,33},{33,1},{2,34},{34,2},{3,35},{35,3},{4,36},{36... | collective-permute-start | bytes 3145736 | tf_op jit(solution)/shard_map/ppermute | solution.py:27
  123.9 33.3 %all-to-all-start.2 = ((bf16[64,8,1664]{2,1,0:T(8,128)(2,1)}), bf16[64,8,1664]{2,1,0:T(8,128)(2,1)}, u32[]{:S(2)}, u32[]{:S(2)}) async-start(bf16[64,8,1664]{2,1,0:T(8,128)(2,1)} %bitcast.52), calls=%async_computation.2 | async-start | bytes 3407872 | tf_op jit(solution)/shard_map/all_to_all | solution.py:31
  132.5 9.1 %copy-start.3 = (bf16[2,64,8,2,512]{4,2,3,1,0:T(8,128)(2,1)}, bf16[2,64,8,2,512]{4,2,3,1,0:T(8,128)(2,1)S(1)}, u32[]{:S(2)}) copy-start(bf16[2,64,8,2,512]{4,2,3,1,0:T(8,128)(2,1)S(1)} %pad_maximum_fusion) | copy-start | bytes 6291460
  141.6 3.7 %copy-start.2 = (bf16[512,1024]{1,0:T(8,128)(2,1)S(1)}, bf16[512,1024]{1,0:T(8,128)(2,1)}, u32[]{:S(2)}) copy-start(bf16[512,1024]{1,0:T(8,128)(2,1)} %get-tuple-element.47) | copy-start | bytes 3145732
  141.6 5.9 %copy-start.4 = (bf16[2,64,8,2,512]{4,2,3,1,0:T(8,128)(2,1)S(1)}, bf16[2,64,8,2,512]{4,2,3,1,0:T(8,128)(2,1)}, u32[]{:S(2)}) copy-start(bf16[2,64,8,2,512]{4,2,3,1,0:T(8,128)(2,1)} %copy-done.3) | copy-start | bytes 6291460
  157.2 3.9 %collective-permute-start.5 = (bf16[512,1664]{1,0:T(8,128)(2,1)}, bf16[512,1664]{1,0:T(8,128)(2,1)}, u32[]{:S(2)}, u32[]{:S(2)}) collective-permute-start(bf16[512,1664]{1,0:T(8,128)(2,1)} %bitcast.15.own_ref), channel_id=1, source_target_pairs={{0,32},{32,0},{1,33},{33,1},{2,34},{34,2},{3,35},{35,3},{4,36},{36... | collective-permute-start | bytes 5111816 | tf_op jit(solution)/shard_map/ppermute | solution.py:27

commit v4 on v3

--- a/solution.py
+++ b/solution.py
@@ -54,19 +54,21 @@
     out_ref,
     mid_ref,
     other_ref,
-    mine_ref,
+    delta_1,
+    tail_ref,
     sum_mid,
     sum_out,
     sum_lead,
     sum_one,
     sum_two,
-    delta_1,
     delta_0,
     lead,
 ):
     step = pl.program_id(0)
     width, tile = low_ref.shape
+    half = width // 2
     basis = delta_2.shape[0]
+    core = core_ref[0]
 
     @pl.when(step == 0)
     def _():
@@ -95,9 +97,12 @@
         delta_0[rows, :] = delta.astype(BF)
     for at in range(0, width, CHUNK):
         rows = slice(at, at + CHUNK)
-        sum_out[rows, :] += dot(high_ref[rows, :], delta_2[...], across)
-        sum_mid[rows, :] += dot(low_ref[rows, :], delta_1[...], across)
         sum_lead[rows, :] += dot(delta_0[rows, :], lead[...], across)
+    for at in range(0, half, CHUNK):
+        rows = slice(at, at + CHUNK)
+        read = pl.ds(pl.multiple_of((1 - core) * half + at, CHUNK), CHUNK)
+        sum_out[rows, :] += dot(high_ref[read, :], delta_2[...], across)
+        sum_mid[rows, :] += dot(low_ref[read, :], delta_1[...], across)
 
     @pl.when(step == pl.num_programs(0) - 1)
     def _():
@@ -106,14 +111,11 @@
         sum_lead[...] = jnp.where(lane == 5, one, sum_lead[...])
         two = jnp.sum(sum_two[...], axis=1, keepdims=True)
         sum_lead[:basis, :] = jnp.where(lane[:basis] == 6, two, sum_lead[:basis, :])
-        core = core_ref[0]
-        half = width // 2
-        for target, start in ((other_ref, (1 - core) * half), (mine_ref, core * half)):
-            rows = pl.ds(pl.multiple_of(start, half), half)
-            at = 0
-            for total in (sum_mid, sum_out, sum_lead):
-                target[:, at : at + total.shape[1]] = total[rows, :].astype(target.dtype)
-                at += total.shape[1]
+        theirs = pl.ds(pl.multiple_of((1 - core) * half, half), half)
+        other_ref[:, :width] = sum_mid[...].astype(BF)
+        other_ref[:, width : width + basis] = sum_out[...].astype(BF)
+        other_ref[:, width + basis :] = sum_lead[theirs, :].astype(BF)
+        tail_ref[...] = sum_lead[pl.ds(pl.multiple_of(core * half, half), half), :]
 
 
 def trunk_back(core, delta_2, low, high, points, out, mid):
@@ -128,44 +130,83 @@
     def part(rows):
         return pl.BlockSpec((rows, TILE), lambda i, c: (0, i))
 
-    product = 2 * half * (2 * width * basis + 2 * width * width + width * 128)
-    return pl.pallas_call(
+    return call(
         trunk_back_kernel,
-        grid_spec=pltpu.PrefetchScalarGridSpec(
-            num_scalar_prefetch=1,
-            grid=(steps,),
-            in_specs=[
-                part(basis),
-                part(width),
-                part(width),
-                pl.BlockSpec((points.shape[0], TILE), lambda i, c: (0, c[0] * steps + i)),
-                whole(out),
-                whole(mid),
-            ],
-            out_specs=[pl.BlockSpec((width // 2, columns), lambda i, c: (0, 0))] * 2,
-            scratch_shapes=[
-                pltpu.VMEM((width, width), F32),
-                pltpu.VMEM((width, basis), F32),
-                pltpu.VMEM((width, 128), F32),
-                pltpu.VMEM((width, 128), F32),
-                pltpu.VMEM((basis, 128), F32),
-                pltpu.VMEM((width, TILE), BF),
-                pltpu.VMEM((width, TILE), BF),
-                pltpu.VMEM((128, TILE), BF),
-            ],
-        ),
-        out_shape=[
+        steps,
+        [
+            part(basis),
+            part(width),
+            part(width),
+            pl.BlockSpec((points.shape[0], TILE), lambda i, c: (0, c[0] * steps + i)),
+            whole(out),
+            whole(mid),
+        ],
+        [
+            pl.BlockSpec((width // 2, columns), lambda i, c: (0, 0)),
+            part(width),
+            pl.BlockSpec((width // 2, 128), lambda i, c: (0, 0)),
+        ],
+        [
             jax.ShapeDtypeStruct((width // 2, columns), BF),
-            jax.ShapeDtypeStruct((width // 2, columns), BF),
-        ],
-        compiler_params=pltpu.CompilerParams(
-            dimension_semantics=("arbitrary",), vmem_limit_bytes=ROOM * 1024 * 1024
-        ),
-        cost_estimate=pl.CostEstimate(
-            flops=product, bytes_accessed=24 * 1024 * 1024, transcendentals=0
-        ),
-        name="trunk_back",
+            jax.ShapeDtypeStruct((width, half), BF),
+            jax.ShapeDtypeStruct((width // 2, 128), F32),
+        ],
+        [
+            pltpu.VMEM((width // 2, width), F32),
+            pltpu.VMEM((width // 2, basis), F32),
+            pltpu.VMEM((width, 128), F32),
+            pltpu.VMEM((width, 128), F32),
+            pltpu.VMEM((basis, 128), F32),
+            pltpu.VMEM((width, TILE), BF),
+            pltpu.VMEM((128, TILE), BF),
+        ],
+        half * width * (3 * basis + 3 * width + 256),
+        20 * 1024 * 1024,
     )(core.reshape(1), delta_2, low, high, points, out, mid)
+
+
+def own_grads_kernel(
+    core_ref, delta_2, delta_1, low_ref, high_ref, tail_ref, mine_ref, sum_mid, sum_out
+):
+    step = pl.program_id(0)
+    width, basis = sum_mid.shape[1], sum_out.shape[1]
+
+    @pl.when(step == 0)
+    def _():
+        sum_mid[...] = jnp.zeros_like(sum_mid)
+        sum_out[...] = jnp.zeros_like(sum_out)
+
+    for at in range(0, low_ref.shape[0], CHUNK):
+        rows = slice(at, at + CHUNK)
+        sum_out[rows, :] += dot(high_ref[rows, :], delta_2[...], ((1,), (1,)))
+        sum_mid[rows, :] += dot(low_ref[rows, :], delta_1[...], ((1,), (1,)))
+
+    @pl.when(step == pl.num_programs(0) - 1)
+    def _():
+        mine_ref[:, :width] = sum_mid[...].astype(BF)
+        mine_ref[:, width : width + basis] = sum_out[...].astype(BF)
+        mine_ref[:, width + basis :] = tail_ref[...].astype(BF)
+
+
+def own_grads(core, delta_2, delta_1, low, high, tail):
+    width, points = low.shape
+    half, basis = width // 2, delta_2.shape[0]
+    columns = width + basis + 128
+
+    def part(rows):
+        return pl.BlockSpec((rows, TILE), lambda i, c: (0, i))
+
+    own = pl.BlockSpec((half, TILE), lambda i, c: (c[0], i))
+    return call(
+        own_grads_kernel,
+        points // TILE,
+        [part(basis), part(width), own, own, pl.BlockSpec(tail.shape, lambda i, c: (0, 0))],
+        pl.BlockSpec((half, columns), lambda i, c: (0, 0)),
+        jax.ShapeDtypeStruct((half, columns), BF),
+        [pltpu.VMEM((half, width), F32), pltpu.VMEM((half, basis), F32)],
+        2 * half * points * (width + basis),
+        12 * 1024 * 1024,
+    )(core.reshape(1), delta_2, delta_1, low, high, tail)
 
 
 def call(kernel, grid, ins, outs, shapes, scratch, flops, moved, limit=ROOM):
@@ -458,13 +499,15 @@
     )
     coef_parts = exchange(coef_part, ("core",) + PTS)
 
-    other, mine = trunk_back(
+    other, delta_1, tail = trunk_back(
         core, delta_2, trunk_0, trunk_1, query_points, trunk_out, trunk_mid[0]
     )
     coef_parts, side_paths, other = lax.optimization_barrier((coef_parts, side_paths, other))
+    swapped = swap(other, "core")
+    mine = own_grads(core, delta_2, delta_1, trunk_0, trunk_1, tail)
 
     columns = mine.shape[1]
-    load = pack_load(core, coef_parts, mine, swap(other, "core"), factor)
+    load = pack_load(core, coef_parts, mine, swapped, factor)
     got = exchange(load, CHIPS)
     local = local_paths.reshape(2, scan_rows, -1)
     side = side_paths.reshape(2, scan_rows, -1)

time: 165 us -> 171 us (1.036)
  Pallas kernels: 48.5 us -> 53.2 us
  waiting for transfers between devices: 31.2 us -> 33.3 us
    pallas_call x1 -> x2, Pallas kernels: 21.4 us -> 26.2 us  [the longest x1 17.6 us: trunk_back(): call(trunk_back_kernel, steps, [part(basis), part(width), part(width), pl...]
    ppermute x6, waiting for transfers between devices: 4.35 us -> 6.61 us  [swap(): return lax.ppermute(values, axis, [(0, 1), (1, 0)])]
  transfers between devices with their start and end apart: 9 -> 9, of which waited for: 3 -> 3; matrix products, arithmetic and copies ran while one was open for 30% -> 28% of each run, Pallas kernels for 22% -> 19%
where the time goes in v4:
time: 171 us
  Pallas kernels  53.2 us (31%)
  matrix products  41.9 us (25%)
  starting transfers between devices  35.3 us (21%)
  waiting for transfers between devices  33.3 us (19%)
  other arithmetic  5.67 us (3%)
    dot_general x7, matrix products, dot(): lax.dot_general(left, right, (dims, ((), ())), preferred_element_type=F32)  41.9 us
    all_to_all x3, starting transfers between devices, exchange(): return lax.all_to_all(values, axes, split_axis=0, concat_axis=0, tiled=True)  29.1 us
    all_to_all x3, waiting for transfers between devices, exchange(): return lax.all_to_all(values, axes, split_axis=0, concat_axis=0, tiled=True)  26.6 us
    pallas_call x1, Pallas kernels, trunk_back(): call(trunk_back_kernel, steps, [part(basis), part(width), part(width), pl...  17.6 us
    pallas_call x1, Pallas kernels, trunk_head(): call(functools.partial(head_kernel, factor), steps, [pl.BlockSpec((scans,...  11.6 us
    pallas_call x1, Pallas kernels, own_grads(): call(own_grads_kernel, points // TILE, [part(basis), part(width), own, ow...  8.6 us
    ppermute x6, waiting for transfers between devices, swap(): return lax.ppermute(values, axis, [(0, 1), (1, 0)])  6.61 us
    ppermute x6, starting transfers between devices, swap(): return lax.ppermute(values, axis, [(0, 1), (1, 0)])  6.15 us
  transfers between devices with their start and end apart: 9, of which 3 were waited for; matrix products, arithmetic and copies ran while one was open for 28% of the time, Pallas kernels for 19%

profile of v4, /device:TPU:1, one launch (start us, length us, event | category | flops | bytes accessed | tf_op | source)
XLA Modules:
  0.0 170.6 jit_solution(730259633278506363)
XLA Ops:
  0.7 1.5 collective-permute-start.1
  2.2 2.6 %shard_map.204 = bf16[512,2048]{1,0:T(8,128)(2,1)} custom-call(s32[1]{0:T(128)} %bitcast.core_ref, bf16[512,4096]{1,0:T(8,128)(2,1)} %kept_ref.1), custom_call_target="tpu_custom_call" | custom-call | bytes 4194304 | tf_op jit(solution)/shard_map/pallas_call | solution.py:233
  6.6 6.4 %fusion.high_ref = bf16[1024,2048]{1,0:T(8,128)(2,1)} fusion(f32[1024]{0:T(1024)S(1)} %bitcast.60, bf16[2048,1024]{0,1:T(8,128)(2,1)S(1)} %tanh_convert_fusion.3, bf16[1,1024,1024]{2,1,0:T(8,128)(2,1)S(1)} %copy-done.8), kind=kOutput, calls=%fused_computation.6 | convolution fusion | flops 4299161600 | bytes 10489856 | tf_op jit(solution)/shard_map/dot_general | solution.py:19
  13.1 5.8 %fusion.1.coeffs_ref = bf16[512,1024]{1,0:T(8,128)(2,1)} fusion(bf16[2048,512]{1,0:T(8,128)(2,1)S(1)} %copy-done, bf16[1024,256]{1,0:T(8,128)(2,1)S(1)} %constant_dynamic-update-slice_fusion, bf16[256,2048]{1,0:T(8,128)(2,1)} %param.16, f32[2048]{0:T(1024)S(1)} %copy-done.11, f32[512]{0:T(512)S(1)} %copy-done.14), kind=kOutput, calls=%fused_computation.10 | convolution fusion | flops 3226468352 | bytes 4728832 | tf_op jit(solution)/shard_map/dot_general | solution.py:19
  18.9 11.6 %shard_map.205 = (bf16[512,2048]{1,0:T(8,128)(2,1)}, bf16[1024,512]{1,0:T(8,128)(2,1)}) custom-call(s32[1]{0:T(128)} %bitcast.core_ref, bf16[512,4096]{1,0:T(8,128)(2,1)} %kept_ref.1, bf16[512,2048]{1,0:T(8,128)(2,1)} %collective-permute-done.theirs_ref, bf16[1024,2048]{1,0:T(8,128)(2,1)} %fusion.high_ref, bf16[512,1024]{1,0:T(8,128)(2,1)} %fusion.1.coeffs_ref, ...), custom_call_target="tpu_custom_call" | custom-call | flops 6442450944 | bytes 15728640 | tf_op jit(solution)/shard_map/pallas_call | solution.py:297
  30.5 11.3 %all-to-all-start = ((bf16[64,16,512]{2,1,0:T(8,128)(2,1)}), bf16[64,16,512]{2,1,0:T(8,128)(2,1)S(1)}, u32[]{:S(2)}, u32[]{:S(2)}) async-start(bf16[64,16,512]{2,1,0:T(8,128)(2,1)} %bitcast.56), calls=%async_computation | async-start | bytes 2097152 | tf_op jit(solution)/shard_map/all_to_all | solution.py:31
  42.9 17.6 %shard_map.206 = (bf16[512,1664]{1,0:T(8,128)(2,1)}, bf16[1024,2048]{1,0:T(8,128)(2,1)}, f32[512,128]{1,0:T(8,128)}) custom-call(s32[1]{0:T(128)} %bitcast.core_ref, bf16[512,2048]{1,0:T(8,128)(2,1)} %get-tuple-element.39.delta_2, bf16[1024,2048]{1,0:T(8,128)(2,1)} %bitcast.46, bf16[1024,2048]{1,0:T(8,128)(2,1)} %fusion.high_ref, ...), custom_call_target="tpu_custom_call" | custom-call | flops 10200547328 | bytes 20971520 | tf_op jit(solution)/shard_map/pallas_call | solution.py:133
  60.5 5.8 %collective-permute-done.2 = bf16[1024,256]{1,0:T(8,128)(2,1)} collective-permute-done((bf16[1024,256]{1,0:T(8,128)(2,1)}, bf16[1024,256]{1,0:T(8,128)(2,1)}, u32[]{:S(2)}, u32[]{:S(2)}) %collective-permute-start.2) | collective-permute-done | bytes 524320 | tf_op jit(solution)/shard_map/ppermute | solution.py:27
  67.3 8.6 %shard_map.207.mine_ref = bf16[512,1664]{1,0:T(8,128)(2,1)} custom-call(s32[1]{0:T(128)} %bitcast.core_ref, bf16[512,2048]{1,0:T(8,128)(2,1)} %get-tuple-element.39.delta_2, bf16[1024,2048]{1,0:T(8,128)(2,1)} %get-tuple-element.42.delta_1, bf16[1024,2048]{1,0:T(8,128)(2,1)} %bitcast.47, bf16[1024,2048]{1,0:T(8,128)(2,1)} %fusion.high_ref, ...), custom_call_target="tpu_custom_call" | custom-call | flops 3221225472 | bytes 12582912 | tf_op jit(solution)/shard_map/pallas_call | solution.py:200
  75.9 3.7 %shard_map.208 = bf16[512,2688]{1,0:T(8,128)(2,1)} custom-call(s32[1]{0:T(128)} %bitcast.core_ref, bf16[1024,512]{1,0:T(8,128)(2,1)} %bitcast.48, bf16[512,1664]{1,0:T(8,128)(2,1)} %shard_map.207.mine_ref, bf16[512,1664]{1,0:T(8,128)(2,1)} %collective-permute-done.3.swapped_ref), custom_call_target="tpu_custom_call" | custom-call | bytes 9437184 | tf_op jit(solution)/shard_map/pallas_call | solution.py:350
  79.6 10.3 %all-to-all-start.1 = ((bf16[64,8,2688]{2,1,0:T(8,128)(2,1)}), bf16[64,8,2688]{2,1,0:T(8,128)(2,1)}, u32[]{:S(2)}, u32[]{:S(2)}) async-start(bf16[64,8,2688]{2,1,0:T(8,128)(2,1)} %bitcast.43), calls=%async_computation.1 | async-start | bytes 5505024 | tf_op jit(solution)/shard_map/all_to_all | solution.py:31
  89.9 1.7 maximum_select_fusion
  91.6 5.8 %tanh_convert_fusion = bf16[2048,2048]{1,0:T(8,128)(2,1)} fusion(bf16[2048,256]{1,0:T(8,128)(2,1)S(1)} %bitcast.44, bf16[256,2048]{1,0:T(8,128)(2,1)} %param.16, f32[2048]{0:T(1024)S(1)} %copy-done.11), kind=kOutput, calls=%fused_computation.2 | convolution fusion | flops 2155872256 | bytes 10493952 | tf_op jit(solution)/shard_map/dot_general | solution.py:19
  97.4 26.6 %all-to-all-done.1 = bf16[64,8,2688]{2,1,0:T(8,128)(2,1)} async-done(((bf16[64,8,2688]{2,1,0:T(8,128)(2,1)}), bf16[64,8,2688]{2,1,0:T(8,128)(2,1)}, u32[]{:S(2)}, u32[]{:S(2)}) %all-to-all-start.1) | async-done | bytes 2752544 | tf_op jit(solution)/shard_map/all_to_all | solution.py:31
  124.1 3.4 %shard_map.209 = (bf16[512,1664]{1,0:T(8,128)(2,1)}, bf16[512,1024]{1,0:T(8,128)(2,1)}) custom-call(s32[1]{0:T(128)} %bitcast.core_ref, bf16[512,2688]{1,0:T(8,128)(2,1)} %bitcast.10.got_ref), custom_call_target="tpu_custom_call" | custom-call | bytes 5505024 | tf_op jit(solution)/shard_map/pallas_call | solution.py:380
  127.4 2.2 %collective-permute-start.4 = (bf16[512,1024]{1,0:T(8,128)(2,1)}, bf16[512,1024]{1,0:T(8,128)(2,1)}, u32[]{:S(2)}, u32[]{:S(2)}) collective-permute-start(bf16[512,1024]{1,0:T(8,128)(2,1)} %get-tuple-element.49), channel_id=1, source_target_pairs={{0,32},{32,0},{1,33},{33,1},{2,34},{34,2},{3,35},{35,3},{4,36},{36... | collective-permute-start | bytes 3145736 | tf_op jit(solution)/shard_map/ppermute | solution.py:27
  129.6 7.5 %all-to-all-start.2 = ((bf16[64,8,1664]{2,1,0:T(8,128)(2,1)}), bf16[64,8,1664]{2,1,0:T(8,128)(2,1)}, u32[]{:S(2)}, u32[]{:S(2)}) async-start(bf16[64,8,1664]{2,1,0:T(8,128)(2,1)} %bitcast.54), calls=%async_computation.2 | async-start | bytes 3407872 | tf_op jit(solution)/shard_map/all_to_all | solution.py:31
  137.1 1.7 %pad_maximum_fusion = bf16[2,64,8,2,512]{4,2,3,1,0:T(8,128)(2,1)S(1)} fusion(bf16[1,64,8,2,512]{4,2,3,1,0:T(8,128)(2,1)} %bitcast.17, bf16[1,64,8,2,512]{4,2,3,1,0:T(8,128)(2,1)} %bitcast.49), kind=kLoop, calls=%fused_computation.8 | loop fusion | flops 1048576 | bytes 4194304 | tf_op jit(solution)/shard_map/stack | solution.py:522
  138.9 9.1 %convert_reduce_fusion = (f32[2048]{0:T(1024)}, bf16[2048,2048]{1,0:T(8,128)(2,1)S(1)}) fusion(bf16[2048,2048]{1,0:T(8,128)(2,1)} %tanh_convert_fusion, bf16[2048,512]{1,0:T(8,128)(2,1)S(1)} %bitcast.52, bf16[2048,512]{1,0:T(8,128)(2,1)S(1)} %copy-done), kind=kOutput, calls=%fused_computation | convolution fusion | flops 4324325376 | bytes 20979712 | tf_op jit(solution)/shard_map/dot_general | solution.py:19
  148.0 3.7 %fusion.6 = f32[256,2048]{1,0:T(8,128)} fusion(bf16[2048,256]{1,0:T(8,128)(2,1)S(1)} %bitcast.45, bf16[2048,2048]{1,0:T(8,128)(2,1)S(1)} %get-tuple-element.67), kind=kOutput, calls=%fused_computation.18 | convolution fusion | flops 2147483648 | bytes 11534336 | tf_op jit(solution)/shard_map/dot_general | solution.py:19
  151.7 2.2 %convert_reduce_fusion.1 = f32[512]{0:T(512)} fusion(bf16[1,64,8,2,512]{4,2,3,1,0:T(8,128)(2,1)} %bitcast.17, bf16[1,64,8,2,512]{4,2,3,1,0:T(8,128)(2,1)S(1)} %bitcast.50), kind=kLoop, calls=%fused_computation.7 | loop fusion | flops 3145216 | bytes 2099200 | tf_op jit(solution)/shard_map/reduce_sum | solution.py:527
  153.9 9.7 %fusion.5 = f32[2048,512]{1,0:T(8,128)} fusion(bf16[2048,2048]{1,0:T(8,128)(2,1)} %tanh_convert_fusion, bf16[2048,512]{1,0:T(8,128)(2,1)S(1)} %bitcast.53), kind=kOutput, calls=%fused_computation.17 | convolution fusion | flops 4294967296 | bytes 14680064 | tf_op jit(solution)/shard_map/dot_general | solution.py:19
  163.9 2.9 %shard_map.210 = (f32[1024,1024]{1,0:T(8,128)}, f32[1024,512]{1,0:T(8,128)}, f32[4,1024]{1,0:T(4,128)}, f32[1,1024]{1,0:T(1,128)}, f32[1,1024]{1,0:T(1,128)}, /*index=5*/f32[1,512]{1,0:T(1,128)}) custom-call(s32[1]{0:T(128)} %bitcast.core_ref, bf16[512,1664]{1,0:T(8,128)(2,1)} %bitcast.15.own_ref), custom_call_target="tpu_custom_call" | custom-call | bytes 5242880 | tf_op jit(solution)/shard_map/pallas_call | solution.py:422
  167.5 2.9 %shard_map.211 = (f32[1024,1024]{1,0:T(8,128)}, f32[1024,512]{1,0:T(8,128)}, f32[4,1024]{1,0:T(4,128)}, f32[1,1024]{1,0:T(1,128)}, f32[1,1024]{1,0:T(1,128)}, /*index=5*/f32[1,512]{1,0:T(1,128)}) custom-call(s32[1]{0:T(128)} %bitcast.21.core_ref, ...), custom_call_target="tpu_custom_call", output_to_operand_aliasing={{0}: (2, {}), {1}: (3, {}), {2}: (4, {}), {3}: (5, {}), {4}... | custom-call | bytes 5242880 | tf_op jit(solution)/shard_map/pallas_call | solution.py:422
  (44 shorter events, 4.9 us)
Async XLA Ops:
  0.6 12.4 %copy-start = (bf16[2048,512]{1,0:T(8,128)(2,1)S(1)}, bf16[2048,512]{1,0:T(8,128)(2,1)}, u32[]{:S(2)}) copy-start(bf16[2048,512]{1,0:T(8,128)(2,1)} %param.18) | copy-start | bytes 6291460
  0.7 4.3 %copy-start.9 = (bf16[4,4096]{1,0:T(4,128)(2,1)S(1)}, bf16[4,4096]{1,0:T(4,128)(2,1)}, u32[]{:S(2)}) copy-start(bf16[4,4096]{1,0:T(4,128)(2,1)} %points_ref.1) | copy-start | bytes 98308
  0.7 4.3 %copy-start.12 = (f32[1024]{0:T(1024)S(1)}, f32[1024]{0:T(1024)}, u32[]{:S(2)}) copy-start(f32[1024]{0:T(1024)} %param.21) | copy-start | bytes 12292
  0.7 4.3 %copy-start.10 = (bf16[4,1024]{1,0:T(4,128)(2,1)S(1)}, bf16[4,1024]{1,0:T(4,128)(2,1)}, u32[]{:S(2)}) copy-start(bf16[4,1024]{1,0:T(4,128)(2,1)} %param.20) | copy-start | bytes 24580
  0.7 12.4 %collective-permute-start.1 = (bf16[512,256]{1,0:T(8,128)(2,1)}, bf16[512,256]{1,0:T(8,128)(2,1)S(1)}, u32[]{:S(2)}, u32[]{:S(2)}) collective-permute-start(bf16[512,256]{1,0:T(8,128)(2,1)} %param.14), channel_id=1, source_target_pairs={{0,32},{32,0},{1,33},{33,1},{2,34},{34,2},{3,35},{35,3},{4,36},{36... | collective-permute-start | bytes 786440 | tf_op jit(solution)/shard_map/ppermute | solution.py:27
  2.2 4.2 %copy-start.13 = (f32[1,1024]{1,0:T(1,128)S(1)}, f32[1,1024]{1,0:T(1,128)}, u32[]{:S(2)}) copy-start(f32[1,1024]{1,0:T(1,128)} %param.23) | copy-start | bytes 12292
  4.8 14.1 %collective-permute-start = (bf16[512,2048]{1,0:T(8,128)(2,1)}, bf16[512,2048]{1,0:T(8,128)(2,1)}, u32[]{:S(2)}, u32[]{:S(2)}) collective-permute-start(bf16[512,2048]{1,0:T(8,128)(2,1)} %shard_map.204), channel_id=1, source_target_pairs={{0,32},{32,0},{1,33},{33,1},{2,34},{34,2},{3,35},{35,3},{4,36},{36... | collective-permute-start | bytes 6291464 | tf_op jit(solution)/shard_map/ppermute | solution.py:27
  5.0 1.6 copy-start.8
  6.4 6.7 %copy-start.1 = (bf16[2048,1024]{0,1:T(8,128)(2,1)}, bf16[2048,1024]{0,1:T(8,128)(2,1)S(1)}, u32[]{:S(2)}) copy-start(bf16[2048,1024]{0,1:T(8,128)(2,1)S(1)} %tanh_convert_fusion.3) | copy-start | bytes 12582916
  6.6 6.5 %copy-start.7 = (bf16[512,256]{1,0:T(8,128)(2,1)S(1)}, bf16[512,256]{1,0:T(8,128)(2,1)}, u32[]{:S(2)}) copy-start(bf16[512,256]{1,0:T(8,128)(2,1)} %param.14) | copy-start | bytes 786436
  6.6 6.5 %copy-start.11 = (f32[2048]{0:T(1024)S(1)}, f32[2048]{0:T(1024)}, u32[]{:S(2)}) copy-start(f32[2048]{0:T(1024)} %param.17) | copy-start | bytes 24580
  6.6 6.5 %copy-start.14 = (f32[512]{0:T(512)S(1)}, f32[512]{0:T(512)}, u32[]{:S(2)}) copy-start(f32[512]{0:T(512)} %param.19) | copy-start | bytes 6148
  13.1 5.8 %copy-start.6 = (bf16[1024,256]{1,0:T(8,128)(2,1)}, bf16[1024,256]{1,0:T(8,128)(2,1)S(1)}, u32[]{:S(2)}) copy-start(bf16[1024,256]{1,0:T(8,128)(2,1)S(1)} %constant_dynamic-update-slice_fusion) | copy-start | bytes 1572868
  30.5 35.8 %all-to-all-start = ((bf16[64,16,512]{2,1,0:T(8,128)(2,1)}), bf16[64,16,512]{2,1,0:T(8,128)(2,1)S(1)}, u32[]{:S(2)}, u32[]{:S(2)}) async-start(bf16[64,16,512]{2,1,0:T(8,128)(2,1)} %bitcast.56), calls=%async_computation | async-start | bytes 2097152 | tf_op jit(solution)/shard_map/all_to_all | solution.py:31
  41.9 24.4 %collective-permute-start.2 = (bf16[1024,256]{1,0:T(8,128)(2,1)}, bf16[1024,256]{1,0:T(8,128)(2,1)}, u32[]{:S(2)}, u32[]{:S(2)}) collective-permute-start(bf16[1024,256]{1,0:T(8,128)(2,1)} %copy-done.6), channel_id=1, source_target_pairs={{0,64},{64,0},{1,65},{65,1},{2,66},{66,2},{3,67},{67,3},{4,68},{68... | collective-permute-start | bytes 1572872 | tf_op jit(solution)/shard_map/ppermute | solution.py:27
  66.3 9.6 %copy-start.2 = (bf16[64,16,512]{2,1,0:T(8,128)(2,1)}, bf16[64,16,512]{2,1,0:T(8,128)(2,1)S(1)}, u32[]{:S(2)}) copy-start(bf16[64,16,512]{2,1,0:T(8,128)(2,1)S(1)} %all-to-all-done) | copy-start | bytes 3145732
  66.3 9.6 %collective-permute-start.3 = (bf16[512,1664]{1,0:T(8,128)(2,1)}, bf16[512,1664]{1,0:T(8,128)(2,1)}, u32[]{:S(2)}, u32[]{:S(2)}) collective-permute-start(bf16[512,1664]{1,0:T(8,128)(2,1)} %get-tuple-element.44), channel_id=1, source_target_pairs={{0,32},{32,0},{1,33},{33,1},{2,34},{34,2},{3,35},{35,3},{4,36},{36... | collective-permute-start | bytes 5111816 | tf_op jit(solution)/shard_map/ppermute | solution.py:27
  79.6 44.5 %all-to-all-start.1 = ((bf16[64,8,2688]{2,1,0:T(8,128)(2,1)}), bf16[64,8,2688]{2,1,0:T(8,128)(2,1)}, u32[]{:S(2)}, u32[]{:S(2)}) async-start(bf16[64,8,2688]{2,1,0:T(8,128)(2,1)} %bitcast.43), calls=%async_computation.1 | async-start | bytes 5505024 | tf_op jit(solution)/shard_map/all_to_all | solution.py:31
  127.4 9.7 %collective-permute-start.4 = (bf16[512,1024]{1,0:T(8,128)(2,1)}, bf16[512,1024]{1,0:T(8,128)(2,1)}, u32[]{:S(2)}, u32[]{:S(2)}) collective-permute-start(bf16[512,1024]{1,0:T(8,128)(2,1)} %get-tuple-element.49), channel_id=1, source_target_pairs={{0,32},{32,0},{1,33},{33,1},{2,34},{34,2},{3,35},{35,3},{4,36},{36... | collective-permute-start | bytes 3145736 | tf_op jit(solution)/shard_map/ppermute | solution.py:27
  129.6 34.0 %all-to-all-start.2 = ((bf16[64,8,1664]{2,1,0:T(8,128)(2,1)}), bf16[64,8,1664]{2,1,0:T(8,128)(2,1)}, u32[]{:S(2)}, u32[]{:S(2)}) async-start(bf16[64,8,1664]{2,1,0:T(8,128)(2,1)} %bitcast.54), calls=%async_computation.2 | async-start | bytes 3407872 | tf_op jit(solution)/shard_map/all_to_all | solution.py:31
  138.9 9.1 %copy-start.4 = (bf16[2,64,8,2,512]{4,2,3,1,0:T(8,128)(2,1)}, bf16[2,64,8,2,512]{4,2,3,1,0:T(8,128)(2,1)S(1)}, u32[]{:S(2)}) copy-start(bf16[2,64,8,2,512]{4,2,3,1,0:T(8,128)(2,1)S(1)} %pad_maximum_fusion) | copy-start | bytes 6291460
  148.0 3.7 %copy-start.3 = (bf16[512,1024]{1,0:T(8,128)(2,1)S(1)}, bf16[512,1024]{1,0:T(8,128)(2,1)}, u32[]{:S(2)}) copy-start(bf16[512,1024]{1,0:T(8,128)(2,1)} %get-tuple-element.49) | copy-start | bytes 3145732
  148.0 5.9 %copy-start.5 = (bf16[2,64,8,2,512]{4,2,3,1,0:T(8,128)(2,1)S(1)}, bf16[2,64,8,2,512]{4,2,3,1,0:T(8,128)(2,1)}, u32[]{:S(2)}) copy-start(bf16[2,64,8,2,512]{4,2,3,1,0:T(8,128)(2,1)} %copy-done.4) | copy-start | bytes 6291460
  163.6 3.9 %collective-permute-start.5 = (bf16[512,1664]{1,0:T(8,128)(2,1)}, bf16[512,1664]{1,0:T(8,128)(2,1)}, u32[]{:S(2)}, u32[]{:S(2)}) collective-permute-start(bf16[512,1664]{1,0:T(8,128)(2,1)} %bitcast.15.own_ref), channel_id=1, source_target_pairs={{0,32},{32,0},{1,33},{33,1},{2,34},{34,2},{3,35},{35,3},{4,36},{36... | collective-permute-start | bytes 5111816 | tf_op jit(solution)/shard_map/ppermute | solution.py:27

commit v5 on v3

--- a/solution.py
+++ b/solution.py
@@ -182,6 +182,41 @@
     )
 
 
+def branch_out_kernel(core_ref, hidden_ref, coef_ref, grad_ref, bias_ref):
+    grad_ref[...] = dot(hidden_ref[...], coef_ref[...], ((1,), (0,)))
+
+    @pl.when(pl.program_id(0) == 0)
+    def _():
+        total = jnp.zeros((16, coef_ref.shape[1]), F32)
+        for at in range(0, coef_ref.shape[0], 16):
+            total += coef_ref[at : at + 16, :].astype(F32)
+        bias_ref[...] = jnp.sum(total, axis=0, keepdims=True)
+
+
+def branch_out_grads(core, hidden, coef):
+    width, scans = hidden.shape
+    basis = coef.shape[1]
+    return call(
+        branch_out_kernel,
+        width // TILE,
+        [
+            pl.BlockSpec((TILE, scans), lambda i, c: (i, 0)),
+            pl.BlockSpec(coef.shape, lambda i, c: (0, 0), pipeline_mode=pl.Buffered(1)),
+        ],
+        [
+            pl.BlockSpec((TILE, basis), lambda i, c: (i, 0)),
+            pl.BlockSpec((1, basis), lambda i, c: (0, 0)),
+        ],
+        [
+            jax.ShapeDtypeStruct((width, basis), F32),
+            jax.ShapeDtypeStruct((1, basis), F32),
+        ],
+        [],
+        2 * width * scans * basis,
+        14 * 1024 * 1024,
+    )(core.reshape(1), hidden, coef)
+
+
 def send_kernel(core_ref, field_ref, sent_ref):
     sent_ref[...] = field_ref[...]
 
@@ -471,7 +506,8 @@
     paths = jnp.where(
         zl == 0, jnp.stack([local, side], axis=1), jnp.stack([side, local], axis=1)
     ).reshape(4 * scan_rows, -1)
-    hidden = tanh_layer(paths, branch_in, branch_in_bias)
+    hidden = dot(branch_in, paths, ((0,), (1,))) + branch_in_bias[:, None]
+    hidden = jnp.tanh(hidden).astype(BF)
     got, hidden = lax.optimization_barrier((got, hidden))
     wide, coef_own = sum_spread(core, got, columns)
     spread = exchange(wide, CHIPS)
@@ -480,11 +516,10 @@
     rows = coef_own.shape[0] // chips
     coef_all = coef_all.reshape(2, chips, rows, 2, basis).transpose(0, 1, 3, 2, 4)
     coef_all = coef_all.reshape(4 * scan_rows, basis)
-    grad_branch_out = rows_rows(hidden, coef_all)
-    grad_branch_out_bias = jnp.sum(coef_all.astype(F32), axis=0)
-    branch_delta = (dot(coef_all, branch_out, ((1,), (1,))) * slope(hidden)).astype(BF)
-    grad_branch_in = rows_rows(paths, branch_delta)
-    grad_branch_in_bias = jnp.sum(branch_delta.astype(F32), axis=0)
+    grad_branch_out, grad_branch_out_bias = branch_out_grads(core, hidden, coef_all)
+    branch_delta = (dot(branch_out, coef_all, ((1,), (1,))) * slope(hidden)).astype(BF)
+    grad_branch_in = dot(paths, branch_delta, ((0,), (1,)))
+    grad_branch_in_bias = jnp.sum(branch_delta.astype(F32), axis=1)
 
     spread, grad_branch_out, grad_branch_in, grad_branch_out_bias = lax.optimization_barrier(
         (spread, grad_branch_out, grad_branch_in, grad_branch_out_bias)
@@ -498,7 +533,7 @@
         grad_branch_in,
         grad_branch_in_bias,
         grad_branch_out,
-        grad_branch_out_bias,
+        grad_branch_out_bias[0],
         grad_in,
         bias_0[0],
         grad_mid[None],

time: 165 us -> 168 us (1.018)
  Pallas kernels: 48.5 us -> 57.8 us
  matrix products: 41.8 us -> 37.1 us
  other arithmetic: 5.68 us -> 3.45 us
    pallas_call x0 -> x1, Pallas kernels: none -> 9.36 us  [branch_out_grads(): call(branch_out_kernel, width // TILE, [pl.BlockSpec((TILE, scans), lambd...]
    dot_general x7 -> x6, matrix products: 41.8 us -> 37.1 us  [dot(): lax.dot_general(left, right, (dims, ((), ())), preferred_element_type=F32)]
    reduce_sum x1 -> x0, other arithmetic: 2.23 us -> none  [on_device(): grad_branch_out_bias = jnp.sum(coef_all.astype(F32), axis=0)]
  transfers between devices with their start and end apart: 9 -> 9, of which waited for: 3 -> 3; matrix products, arithmetic and copies ran while one was open for 30% -> 25% of each run, Pallas kernels for 22% -> 27%
where the time goes in v5:
time: 168 us; the launch traced here: 167 us
  Pallas kernels  57.8 us (34%)
  matrix products  37.1 us (22%)
  starting transfers between devices  34.3 us (20%)
  waiting for transfers between devices  30.6 us (18%)
  other arithmetic  3.45 us (2%)
  local copies, waits for them, and re-layouts  3.01 us (2%)
    dot_general x6, matrix products, dot(): lax.dot_general(left, right, (dims, ((), ())), preferred_element_type=F32)  37.1 us
    all_to_all x3, starting transfers between devices, exchange(): return lax.all_to_all(values, axes, split_axis=0, concat_axis=0, tiled=True)  28.3 us
    all_to_all x3, waiting for transfers between devices, exchange(): return lax.all_to_all(values, axes, split_axis=0, concat_axis=0, tiled=True)  26.2 us
    pallas_call x1, Pallas kernels, trunk_back(): pl.pallas_call(trunk_back_kernel, grid_spec=pltpu.PrefetchScalarGridSpec(...  21.3 us
    pallas_call x1, Pallas kernels, trunk_head(): call(functools.partial(head_kernel, factor), steps, [pl.BlockSpec((scans,...  11.6 us
    pallas_call x1, Pallas kernels, branch_out_grads(): call(branch_out_kernel, width // TILE, [pl.BlockSpec((TILE, scans), lambd...  9.36 us
    ppermute x6, starting transfers between devices, swap(): return lax.ppermute(values, axis, [(0, 1), (1, 0)])  5.98 us
    pallas_call x2, Pallas kernels, unpack(): pl.pallas_call(unpack_kernel, grid_spec=pltpu.PrefetchScalarGridSpec(num_...  5.77 us
  transfers between devices with their start and end apart: 9, of which 3 were waited for; matrix products, arithmetic and copies ran while one was open for 25% of the time, Pallas kernels for 27%

profile of v5, /device:TPU:1, one launch (start us, length us, event | category | flops | bytes accessed | tf_op | source)
XLA Modules:
  0.0 167.3 jit_solution(1191096898167249787)
XLA Ops:
  0.7 2.8 %shard_map.204 = bf16[512,2048]{1,0:T(8,128)(2,1)} custom-call(s32[1]{0:T(128)} %bitcast.core_ref, bf16[512,4096]{1,0:T(8,128)(2,1)} %kept_ref.1), custom_call_target="tpu_custom_call" | custom-call | bytes 4194304 | tf_op jit(solution)/shard_map/pallas_call | solution.py:227
  3.5 1.4 collective-permute-start
  5.0 1.4 tanh_convert_fusion.3
  6.5 6.4 %fusion.2.high_ref = bf16[1024,2048]{1,0:T(8,128)(2,1)} fusion(f32[1024]{0:T(1024)S(1)} %bitcast.60, bf16[2048,1024]{0,1:T(8,128)(2,1)S(1)} %tanh_convert_fusion.3, bf16[1,1024,1024]{2,1,0:T(8,128)(2,1)S(1)} %copy-done.4), kind=kOutput, calls=%fused_computation.8 | convolution fusion | flops 4299161600 | bytes 10489856 | tf_op jit(solution)/shard_map/dot_general | solution.py:19
  14.4 1.7 %collective-permute-start.2 = (bf16[1024,256]{1,0:T(8,128)(2,1)}, bf16[1024,256]{1,0:T(8,128)(2,1)}, u32[]{:S(2)}, u32[]{:S(2)}) collective-permute-start(bf16[1024,256]{1,0:T(8,128)(2,1)} %constant_dynamic-update-slice_fusion), channel_id=1, source_target_pairs={{0,64},{64,0},{1,65},{65,1},{2,66},{66,2},{3,67},{67,3},{4,68},{68... | collective-permute-start | bytes 1572872 | tf_op jit(solution)/shard_map/ppermute | solution.py:27
  16.2 5.8 %fusion.3.coeffs_ref = bf16[512,1024]{1,0:T(8,128)(2,1)} fusion(bf16[2048,512]{1,0:T(8,128)(2,1)S(1)} %copy-done, bf16[1024,256]{1,0:T(8,128)(2,1)} %constant_dynamic-update-slice_fusion, bf16[256,2048]{1,0:T(8,128)(2,1)} %param.16, f32[2048]{0:T(1024)S(1)} %copy-done.7, f32[512]{0:T(512)S(1)} %copy-done.10), kind=kOutput, calls=%fused_computation.11 | convolution fusion | flops 3226468352 | bytes 4728832 | tf_op jit(solution)/shard_map/dot_general | solution.py:19
  21.9 11.6 %shard_map.205 = (bf16[512,2048]{1,0:T(8,128)(2,1)}, bf16[1024,512]{1,0:T(8,128)(2,1)}) custom-call(s32[1]{0:T(128)} %bitcast.core_ref, bf16[512,4096]{1,0:T(8,128)(2,1)} %kept_ref.1, bf16[512,2048]{1,0:T(8,128)(2,1)} %collective-permute-done.theirs_ref, bf16[1024,2048]{1,0:T(8,128)(2,1)} %fusion.2.high_ref, bf16[512,1024]{1,0:T(8,128)(2,1)} %fusion.3.coeffs_ref, ...), custom_call_target="tpu_custom_call" | custom-call | flops 6442450944 | bytes 15728640 | tf_op jit(solution)/shard_map/pallas_call | solution.py:291
  33.5 11.4 %all-to-all-start = ((bf16[64,16,512]{2,1,0:T(8,128)(2,1)}), bf16[64,16,512]{2,1,0:T(8,128)(2,1)S(1)}, u32[]{:S(2)}, u32[]{:S(2)}) async-start(bf16[64,16,512]{2,1,0:T(8,128)(2,1)} %bitcast.55), calls=%async_computation | async-start | bytes 2097152 | tf_op jit(solution)/shard_map/all_to_all | solution.py:31
  44.9 21.3 %trunk_back.1 = (bf16[512,1664]{1,0:T(8,128)(2,1)}, bf16[512,1664]{1,0:T(8,128)(2,1)}) custom-call(s32[1]{0:T(128)} %bitcast.core_ref, bf16[512,2048]{1,0:T(8,128)(2,1)} %get-tuple-element.40.delta_2, bf16[1024,2048]{1,0:T(8,128)(2,1)} %bitcast.62, bf16[1024,2048]{1,0:T(8,128)(2,1)} %fusion.2.high_ref, bf16[4,4096]{1,0:T(4,128)(2,1)} %points_ref.1, ...), custom_call_target="tpu_custom_call" | custom-call | flops 13421772800 | bytes 25165824 | tf_op jit(solution)/shard_map/trunk_back/pallas_call | solution.py:132
  66.9 3.6 %collective-permute-done.3.swapped_ref = bf16[512,1664]{1,0:T(8,128)(2,1)} collective-permute-done((bf16[512,1664]{1,0:T(8,128)(2,1)}, bf16[512,1664]{1,0:T(8,128)(2,1)}, u32[]{:S(2)}, u32[]{:S(2)}) %collective-permute-start.3) | collective-permute-done | bytes 1703968 | tf_op jit(solution)/shard_map/ppermute | solution.py:27
  70.4 3.7 %shard_map.206 = bf16[512,2688]{1,0:T(8,128)(2,1)} custom-call(s32[1]{0:T(128)} %bitcast.core_ref, bf16[1024,512]{1,0:T(8,128)(2,1)} %bitcast.48, bf16[512,1664]{1,0:T(8,128)(2,1)} %get-tuple-element.43.mine_ref, bf16[512,1664]{1,0:T(8,128)(2,1)} %collective-permute-done.3.swapped_ref), custom_call_target="tpu_custom_call" | custom-call | bytes 9437184 | tf_op jit(solution)/shard_map/pallas_call | solution.py:344
  74.1 10.2 %all-to-all-start.1 = ((bf16[64,8,2688]{2,1,0:T(8,128)(2,1)}), bf16[64,8,2688]{2,1,0:T(8,128)(2,1)}, u32[]{:S(2)}, u32[]{:S(2)}) async-start(bf16[64,8,2688]{2,1,0:T(8,128)(2,1)} %bitcast.47), calls=%async_computation.1 | async-start | bytes 5505024 | tf_op jit(solution)/shard_map/all_to_all | solution.py:31
  84.3 1.7 %maximum_select_fusion = bf16[2,2,512,256]{3,2,1,0:T(8,128)(2,1)S(1)} fusion(bf16[2,1,512,256]{3,2,1,0:T(8,128)(2,1)} %bitcast.12, bf16[2,1,512,256]{3,2,1,0:T(8,128)(2,1)} %bitcast.11, pred[]{:T(512)S(6)} %eq.3), kind=kLoop, calls=%fused_computation.12 | loop fusion | flops 1572864 | bytes 2097153 | tf_op jit(solution)/shard_map/jit(_where)/select_n | solution.py:506
  86.0 6.4 %fusion.1.hidden_ref = bf16[2048,2048]{1,0:T(8,128)(2,1)} fusion(f32[2048]{0:T(1024)S(1)} %copy-done.7, bf16[2048,256]{1,0:T(8,128)(2,1)S(1)} %bitcast.53, bf16[256,2048]{1,0:T(8,128)(2,1)} %param.16), kind=kOutput, calls=%fused_computation.7 | convolution fusion | flops 2155872256 | bytes 10493952 | tf_op jit(solution)/shard_map/dot_general | solution.py:19
  92.4 26.2 %all-to-all-done.1 = bf16[64,8,2688]{2,1,0:T(8,128)(2,1)} async-done(((bf16[64,8,2688]{2,1,0:T(8,128)(2,1)}), bf16[64,8,2688]{2,1,0:T(8,128)(2,1)}, u32[]{:S(2)}, u32[]{:S(2)}) %all-to-all-start.1) | async-done | bytes 2752544 | tf_op jit(solution)/shard_map/all_to_all | solution.py:31
  118.6 3.4 %shard_map.207 = (bf16[512,1664]{1,0:T(8,128)(2,1)}, bf16[512,1024]{1,0:T(8,128)(2,1)}) custom-call(s32[1]{0:T(128)} %bitcast.core_ref, bf16[512,2688]{1,0:T(8,128)(2,1)} %bitcast.10.got_ref), custom_call_target="tpu_custom_call" | custom-call | bytes 5505024 | tf_op jit(solution)/shard_map/pallas_call | solution.py:374
  122.0 1.9 %collective-permute-start.4 = (bf16[512,1024]{1,0:T(8,128)(2,1)}, bf16[512,1024]{1,0:T(8,128)(2,1)}, u32[]{:S(2)}, u32[]{:S(2)}) collective-permute-start(bf16[512,1024]{1,0:T(8,128)(2,1)} %get-tuple-element.49), channel_id=1, source_target_pairs={{0,32},{32,0},{1,33},{33,1},{2,34},{34,2},{3,35},{35,3},{4,36},{36... | collective-permute-start | bytes 3145736 | tf_op jit(solution)/shard_map/ppermute | solution.py:27
  123.9 6.8 %all-to-all-start.2 = ((bf16[64,8,1664]{2,1,0:T(8,128)(2,1)}), bf16[64,8,1664]{2,1,0:T(8,128)(2,1)}, u32[]{:S(2)}, u32[]{:S(2)}) async-start(bf16[64,8,1664]{2,1,0:T(8,128)(2,1)} %bitcast.52), calls=%async_computation.2 | async-start | bytes 3407872 | tf_op jit(solution)/shard_map/all_to_all | solution.py:31
  130.7 1.7 %pad_maximum_fusion = bf16[2,64,8,2,512]{4,2,3,1,0:T(8,128)(2,1)S(1)} fusion(bf16[1,64,8,2,512]{4,2,3,1,0:T(8,128)(2,1)} %bitcast.18, bf16[1,64,8,2,512]{4,2,3,1,0:T(8,128)(2,1)} %bitcast.56), kind=kLoop, calls=%fused_computation.9 | loop fusion | flops 1048576 | bytes 4194304 | tf_op jit(solution)/shard_map/stack | solution.py:515
  133.8 10.1 %convert_reduce_fusion = (f32[2048]{0:T(1024)}, bf16[2048,2048]{1,0:T(8,128)(2,1)}) fusion(bf16[2048,2048]{1,0:T(8,128)(2,1)} %fusion.1.hidden_ref, bf16[2048,512]{1,0:T(8,128)(2,1)S(1)} %bitcast.50, bf16[2048,512]{1,0:T(8,128)(2,1)S(1)} %copy-done), kind=kOutput, calls=%fused_computation.2 | convolution fusion | flops 4324325376 | bytes 20979712 | tf_op jit(solution)/shard_map/dot_general | solution.py:19
  143.9 9.4 %shard_map.208 = (f32[2048,512]{1,0:T(8,128)}, f32[1,512]{1,0:T(1,128)}) custom-call(s32[1]{0:T(128)} %bitcast.core_ref, bf16[2048,2048]{1,0:T(8,128)(2,1)} %fusion.1.hidden_ref, bf16[2048,512]{1,0:T(8,128)(2,1)} %bitcast.51), custom_call_target="tpu_custom_call" | custom-call | flops 4294967296 | bytes 14680064 | tf_op jit(solution)/shard_map/pallas_call | solution.py:199
  153.2 7.1 %fusion.7 = f32[256,2048]{1,0:T(8,128)} fusion(bf16[2048,256]{1,0:T(8,128)(2,1)S(1)} %bitcast.54, bf16[2048,2048]{1,0:T(8,128)(2,1)} %get-tuple-element.69), kind=kOutput, calls=%fused_computation.18 | convolution fusion | flops 2147483648 | bytes 11534336 | tf_op jit(solution)/shard_map/dot_general | solution.py:19
  160.6 2.9 %shard_map.209 = (f32[1024,1024]{1,0:T(8,128)}, f32[1024,512]{1,0:T(8,128)}, f32[4,1024]{1,0:T(4,128)}, f32[1,1024]{1,0:T(1,128)}, f32[1,1024]{1,0:T(1,128)}, /*index=5*/f32[1,512]{1,0:T(1,128)}) custom-call(s32[1]{0:T(128)} %bitcast.core_ref, bf16[512,1664]{1,0:T(8,128)(2,1)} %bitcast.16.own_ref), custom_call_target="tpu_custom_call" | custom-call | bytes 5242880 | tf_op jit(solution)/shard_map/pallas_call | solution.py:416
  164.3 2.9 %shard_map.210 = (f32[1024,1024]{1,0:T(8,128)}, f32[1024,512]{1,0:T(8,128)}, f32[4,1024]{1,0:T(4,128)}, f32[1,1024]{1,0:T(1,128)}, f32[1,1024]{1,0:T(1,128)}, /*index=5*/f32[1,512]{1,0:T(1,128)}) custom-call(s32[1]{0:T(128)} %bitcast.24.core_ref, ...), custom_call_target="tpu_custom_call", output_to_operand_aliasing={{0}: (2, {}), {1}: (3, {}), {2}: (4, {}), {3}: (5, {}), {4}... | custom-call | bytes 5242880 | tf_op jit(solution)/shard_map/pallas_call | solution.py:416
  (36 shorter events, 4.7 us)
Async XLA Ops:
  0.6 15.5 %copy-start = (bf16[2048,512]{1,0:T(8,128)(2,1)S(1)}, bf16[2048,512]{1,0:T(8,128)(2,1)}, u32[]{:S(2)}) copy-start(bf16[2048,512]{1,0:T(8,128)(2,1)} %param.18) | copy-start | bytes 6291460
  0.7 4.3 %copy-start.3 = (bf16[512,256]{1,0:T(8,128)(2,1)S(1)}, bf16[512,256]{1,0:T(8,128)(2,1)}, u32[]{:S(2)}) copy-start(bf16[512,256]{1,0:T(8,128)(2,1)} %param.14) | copy-start | bytes 786436
  0.7 4.3 %copy-start.5 = (bf16[4,4096]{1,0:T(4,128)(2,1)S(1)}, bf16[4,4096]{1,0:T(4,128)(2,1)}, u32[]{:S(2)}) copy-start(bf16[4,4096]{1,0:T(4,128)(2,1)} %points_ref.1) | copy-start | bytes 98308
  0.7 4.2 %copy-start.6 = (bf16[4,1024]{1,0:T(4,128)(2,1)S(1)}, bf16[4,1024]{1,0:T(4,128)(2,1)}, u32[]{:S(2)}) copy-start(bf16[4,1024]{1,0:T(4,128)(2,1)} %param.20) | copy-start | bytes 24580
  0.7 4.2 %copy-start.8 = (f32[1024]{0:T(1024)S(1)}, f32[1024]{0:T(1024)}, u32[]{:S(2)}) copy-start(f32[1024]{0:T(1024)} %param.21) | copy-start | bytes 12292
  0.7 5.6 %copy-start.9 = (f32[1,1024]{1,0:T(1,128)S(1)}, f32[1,1024]{1,0:T(1,128)}, u32[]{:S(2)}) copy-start(f32[1,1024]{1,0:T(1,128)} %param.23) | copy-start | bytes 12292
  3.5 18.5 %collective-permute-start = (bf16[512,2048]{1,0:T(8,128)(2,1)}, bf16[512,2048]{1,0:T(8,128)(2,1)}, u32[]{:S(2)}, u32[]{:S(2)}) collective-permute-start(bf16[512,2048]{1,0:T(8,128)(2,1)} %shard_map.204), channel_id=1, source_target_pairs={{0,32},{32,0},{1,33},{33,1},{2,34},{34,2},{3,35},{35,3},{4,36},{36... | collective-permute-start | bytes 6291464 | tf_op jit(solution)/shard_map/ppermute | solution.py:27
  4.9 8.8 %collective-permute-start.1 = (bf16[512,256]{1,0:T(8,128)(2,1)S(1)}, bf16[512,256]{1,0:T(8,128)(2,1)S(1)}, u32[]{:S(2)}, u32[]{:S(2)}) collective-permute-start(bf16[512,256]{1,0:T(8,128)(2,1)S(1)} %copy-done.3), channel_id=1, source_target_pairs={{0,32},{32,0},{1,33},{33,1},{2,34},{34,2},{3,35},{35,3},{4,36},{36... | collective-permute-start | bytes 786440 | tf_op jit(solution)/shard_map/ppermute | solution.py:27
  4.9 1.6 copy-start.4
  6.3 6.7 %copy-start.11 = (bf16[2048,1024]{0,1:T(8,128)(2,1)}, bf16[2048,1024]{0,1:T(8,128)(2,1)S(1)}, u32[]{:S(2)}) copy-start(bf16[2048,1024]{0,1:T(8,128)(2,1)S(1)} %tanh_convert_fusion.3) | copy-start | bytes 12582916
  6.5 9.6 %copy-start.7 = (f32[2048]{0:T(1024)S(1)}, f32[2048]{0:T(1024)}, u32[]{:S(2)}) copy-start(f32[2048]{0:T(1024)} %param.17) | copy-start | bytes 24580
  6.5 9.6 %copy-start.10 = (f32[512]{0:T(512)S(1)}, f32[512]{0:T(512)}, u32[]{:S(2)}) copy-start(f32[512]{0:T(512)} %param.19) | copy-start | bytes 6148
  14.4 51.8 %collective-permute-start.2 = (bf16[1024,256]{1,0:T(8,128)(2,1)}, bf16[1024,256]{1,0:T(8,128)(2,1)}, u32[]{:S(2)}, u32[]{:S(2)}) collective-permute-start(bf16[1024,256]{1,0:T(8,128)(2,1)} %constant_dynamic-update-slice_fusion), channel_id=1, source_target_pairs={{0,64},{64,0},{1,65},{65,1},{2,66},{66,2},{3,67},{67,3},{4,68},{68... | collective-permute-start | bytes 1572872 | tf_op jit(solution)/shard_map/ppermute | solution.py:27
  33.5 32.7 %all-to-all-start = ((bf16[64,16,512]{2,1,0:T(8,128)(2,1)}), bf16[64,16,512]{2,1,0:T(8,128)(2,1)S(1)}, u32[]{:S(2)}, u32[]{:S(2)}) async-start(bf16[64,16,512]{2,1,0:T(8,128)(2,1)} %bitcast.55), calls=%async_computation | async-start | bytes 2097152 | tf_op jit(solution)/shard_map/all_to_all | solution.py:31
  66.2 4.2 %copy-start.1 = (bf16[64,16,512]{2,1,0:T(8,128)(2,1)}, bf16[64,16,512]{2,1,0:T(8,128)(2,1)S(1)}, u32[]{:S(2)}) copy-start(bf16[64,16,512]{2,1,0:T(8,128)(2,1)S(1)} %all-to-all-done) | copy-start | bytes 3145732
  66.3 4.2 %collective-permute-start.3 = (bf16[512,1664]{1,0:T(8,128)(2,1)}, bf16[512,1664]{1,0:T(8,128)(2,1)}, u32[]{:S(2)}, u32[]{:S(2)}) collective-permute-start(bf16[512,1664]{1,0:T(8,128)(2,1)} %get-tuple-element.44), channel_id=1, source_target_pairs={{0,32},{32,0},{1,33},{33,1},{2,34},{34,2},{3,35},{35,3},{4,36},{36... | collective-permute-start | bytes 5111816 | tf_op jit(solution)/shard_map/ppermute | solution.py:27
  74.1 44.5 %all-to-all-start.1 = ((bf16[64,8,2688]{2,1,0:T(8,128)(2,1)}), bf16[64,8,2688]{2,1,0:T(8,128)(2,1)}, u32[]{:S(2)}, u32[]{:S(2)}) async-start(bf16[64,8,2688]{2,1,0:T(8,128)(2,1)} %bitcast.47), calls=%async_computation.1 | async-start | bytes 5505024 | tf_op jit(solution)/shard_map/all_to_all | solution.py:31
  122.0 8.7 %collective-permute-start.4 = (bf16[512,1024]{1,0:T(8,128)(2,1)}, bf16[512,1024]{1,0:T(8,128)(2,1)}, u32[]{:S(2)}, u32[]{:S(2)}) collective-permute-start(bf16[512,1024]{1,0:T(8,128)(2,1)} %get-tuple-element.49), channel_id=1, source_target_pairs={{0,32},{32,0},{1,33},{33,1},{2,34},{34,2},{3,35},{35,3},{4,36},{36... | collective-permute-start | bytes 3145736 | tf_op jit(solution)/shard_map/ppermute | solution.py:27
  123.9 36.4 %all-to-all-start.2 = ((bf16[64,8,1664]{2,1,0:T(8,128)(2,1)}), bf16[64,8,1664]{2,1,0:T(8,128)(2,1)}, u32[]{:S(2)}, u32[]{:S(2)}) async-start(bf16[64,8,1664]{2,1,0:T(8,128)(2,1)} %bitcast.52), calls=%async_computation.2 | async-start | bytes 3407872 | tf_op jit(solution)/shard_map/all_to_all | solution.py:31
  132.5 1.3 copy-start.2
  160.3 3.9 %collective-permute-start.5 = (bf16[512,1664]{1,0:T(8,128)(2,1)}, bf16[512,1664]{1,0:T(8,128)(2,1)}, u32[]{:S(2)}, u32[]{:S(2)}) collective-permute-start(bf16[512,1664]{1,0:T(8,128)(2,1)} %bitcast.16.own_ref), channel_id=1, source_target_pairs={{0,32},{32,0},{1,33},{33,1},{2,34},{34,2},{3,35},{35,3},{4,36},{36... | collective-permute-start | bytes 5111816 | tf_op jit(solution)/shard_map/ppermute | solution.py:27

commit v6 on v3

--- a/solution.py
+++ b/solution.py
@@ -481,7 +481,7 @@
     coef_all = coef_all.reshape(2, chips, rows, 2, basis).transpose(0, 1, 3, 2, 4)
     coef_all = coef_all.reshape(4 * scan_rows, basis)
     grad_branch_out = rows_rows(hidden, coef_all)
-    grad_branch_out_bias = jnp.sum(coef_all.astype(F32), axis=0)
+    grad_branch_out_bias = dot(jnp.ones((8, 4 * scan_rows), BF), coef_all, ((1,), (0,)))[0]
     branch_delta = (dot(coef_all, branch_out, ((1,), (1,))) * slope(hidden)).astype(BF)
     grad_branch_in = rows_rows(paths, branch_delta)
     grad_branch_in_bias = jnp.sum(branch_delta.astype(F32), axis=0)

time: 165 us -> 163 us (0.988)
  other arithmetic: 5.68 us -> 3.45 us
    reduce_sum x1 -> x0, other arithmetic: 2.23 us -> none  [on_device(): grad_branch_out_bias = jnp.sum(coef_all.astype(F32), axis=0)]
    dot_general x7 -> x8, matrix products: 41.8 us -> 42 us  [dot(): lax.dot_general(left, right, (dims, ((), ())), preferred_element_type=F32)]
  transfers between devices with their start and end apart: 9 -> 9, of which waited for: 3 -> 3; matrix products, arithmetic and copies ran while one was open for 30% -> 29% of each run, Pallas kernels for 22% -> 22%
where the time goes in v6:
time: 163 us
  Pallas kernels  48.5 us (30%)
  matrix products  42 us (26%)
  starting transfers between devices  34.8 us (21%)
  waiting for transfers between devices  31.1 us (19%)
  other arithmetic  3.45 us (2%)
  local copies, waits for them, and re-layouts  1.7 us (1%)
    dot_general x8, matrix products, dot(): lax.dot_general(left, right, (dims, ((), ())), preferred_element_type=F32)  42 us
    all_to_all x3, starting transfers between devices, exchange(): return lax.all_to_all(values, axes, split_axis=0, concat_axis=0, tiled=True)  28.3 us
    all_to_all x3, waiting for transfers between devices, exchange(): return lax.all_to_all(values, axes, split_axis=0, concat_axis=0, tiled=True)  26.8 us
    pallas_call x1, Pallas kernels, trunk_back(): pl.pallas_call(trunk_back_kernel, grid_spec=pltpu.PrefetchScalarGridSpec(...  21.3 us
    pallas_call x1, Pallas kernels, trunk_head(): call(functools.partial(head_kernel, factor), steps, [pl.BlockSpec((scans,...  11.5 us
    ppermute x6, starting transfers between devices, swap(): return lax.ppermute(values, axis, [(0, 1), (1, 0)])  6.43 us
    pallas_call x2, Pallas kernels, unpack(): pl.pallas_call(unpack_kernel, grid_spec=pltpu.PrefetchScalarGridSpec(num_...  5.77 us
    ppermute x6, waiting for transfers between devices, swap(): return lax.ppermute(values, axis, [(0, 1), (1, 0)])  4.26 us
  transfers between devices with their start and end apart: 9, of which 3 were waited for; matrix products, arithmetic and copies ran while one was open for 29% of the time, Pallas kernels for 22%

profile of v6, /device:TPU:1, one launch (start us, length us, event | category | flops | bytes accessed | tf_op | source)
XLA Modules:
  0.0 162.5 jit_solution(13340690516340543717)
XLA Ops:
  0.7 2.8 %shard_map.204 = bf16[512,2048]{1,0:T(8,128)(2,1)} custom-call(s32[1]{0:T(128)} %bitcast.core_ref, bf16[512,4096]{1,0:T(8,128)(2,1)} %kept_ref.1), custom_call_target="tpu_custom_call" | custom-call | bytes 4194304 | tf_op jit(solution)/shard_map/pallas_call | solution.py:192
  3.5 1.4 collective-permute-start
  5.0 1.4 tanh_convert_fusion.3
  6.5 6.4 %fusion.high_ref = bf16[1024,2048]{1,0:T(8,128)(2,1)} fusion(f32[1024]{0:T(1024)S(1)} %bitcast.59, bf16[2048,1024]{0,1:T(8,128)(2,1)S(1)} %tanh_convert_fusion.3, bf16[1,1024,1024]{2,1,0:T(8,128)(2,1)S(1)} %copy-done.3), kind=kOutput, calls=%fused_computation.6 | convolution fusion | flops 4299161600 | bytes 10489856 | tf_op jit(solution)/shard_map/dot_general | solution.py:19
  14.4 1.7 %collective-permute-start.2 = (bf16[1024,256]{1,0:T(8,128)(2,1)}, bf16[1024,256]{1,0:T(8,128)(2,1)}, u32[]{:S(2)}, u32[]{:S(2)}) collective-permute-start(bf16[1024,256]{1,0:T(8,128)(2,1)} %constant_dynamic-update-slice_fusion), channel_id=1, source_target_pairs={{0,64},{64,0},{1,65},{65,1},{2,66},{66,2},{3,67},{67,3},{4,68},{68... | collective-permute-start | bytes 1572872 | tf_op jit(solution)/shard_map/ppermute | solution.py:27
  16.2 5.8 %fusion.1.coeffs_ref = bf16[512,1024]{1,0:T(8,128)(2,1)} fusion(bf16[2048,512]{1,0:T(8,128)(2,1)S(1)} %copy-done, bf16[1024,256]{1,0:T(8,128)(2,1)} %constant_dynamic-update-slice_fusion, bf16[256,2048]{1,0:T(8,128)(2,1)} %param.16, f32[2048]{0:T(1024)S(1)} %copy-done.6, f32[512]{0:T(512)S(1)} %copy-done.9), kind=kOutput, calls=%fused_computation.9 | convolution fusion | flops 3226468352 | bytes 4728832 | tf_op jit(solution)/shard_map/dot_general | solution.py:19
  22.0 11.5 %shard_map.205 = (bf16[512,2048]{1,0:T(8,128)(2,1)}, bf16[1024,512]{1,0:T(8,128)(2,1)}) custom-call(s32[1]{0:T(128)} %bitcast.core_ref, bf16[512,4096]{1,0:T(8,128)(2,1)} %kept_ref.1, bf16[512,2048]{1,0:T(8,128)(2,1)} %collective-permute-done.theirs_ref, bf16[1024,2048]{1,0:T(8,128)(2,1)} %fusion.high_ref, bf16[512,1024]{1,0:T(8,128)(2,1)} %fusion.1.coeffs_ref, ...), custom_call_target="tpu_custom_call" | custom-call | flops 6442450944 | bytes 15728640 | tf_op jit(solution)/shard_map/pallas_call | solution.py:256
  33.5 11.4 %all-to-all-start = ((bf16[64,16,512]{2,1,0:T(8,128)(2,1)}), bf16[64,16,512]{2,1,0:T(8,128)(2,1)S(1)}, u32[]{:S(2)}, u32[]{:S(2)}) async-start(bf16[64,16,512]{2,1,0:T(8,128)(2,1)} %bitcast.53), calls=%async_computation | async-start | bytes 2097152 | tf_op jit(solution)/shard_map/all_to_all | solution.py:31
  44.9 21.3 %trunk_back.1 = (bf16[512,1664]{1,0:T(8,128)(2,1)}, bf16[512,1664]{1,0:T(8,128)(2,1)}) custom-call(s32[1]{0:T(128)} %bitcast.core_ref, bf16[512,2048]{1,0:T(8,128)(2,1)} %get-tuple-element.38.delta_2, bf16[1024,2048]{1,0:T(8,128)(2,1)} %bitcast.61, bf16[1024,2048]{1,0:T(8,128)(2,1)} %fusion.high_ref, bf16[4,4096]{1,0:T(4,128)(2,1)} %points_ref.1, ...), custom_call_target="tpu_custom_call" | custom-call | flops 13421772800 | bytes 25165824 | tf_op jit(solution)/shard_map/trunk_back/pallas_call | solution.py:132
  66.9 3.6 %collective-permute-done.3.swapped_ref = bf16[512,1664]{1,0:T(8,128)(2,1)} collective-permute-done((bf16[512,1664]{1,0:T(8,128)(2,1)}, bf16[512,1664]{1,0:T(8,128)(2,1)}, u32[]{:S(2)}, u32[]{:S(2)}) %collective-permute-start.3) | collective-permute-done | bytes 1703968 | tf_op jit(solution)/shard_map/ppermute | solution.py:27
  70.4 3.7 %shard_map.206 = bf16[512,2688]{1,0:T(8,128)(2,1)} custom-call(s32[1]{0:T(128)} %bitcast.core_ref, bf16[1024,512]{1,0:T(8,128)(2,1)} %bitcast.50, bf16[512,1664]{1,0:T(8,128)(2,1)} %get-tuple-element.41.mine_ref, bf16[512,1664]{1,0:T(8,128)(2,1)} %collective-permute-done.3.swapped_ref), custom_call_target="tpu_custom_call" | custom-call | bytes 9437184 | tf_op jit(solution)/shard_map/pallas_call | solution.py:309
  74.1 10.2 %all-to-all-start.1 = ((bf16[64,8,2688]{2,1,0:T(8,128)(2,1)}), bf16[64,8,2688]{2,1,0:T(8,128)(2,1)}, u32[]{:S(2)}, u32[]{:S(2)}) async-start(bf16[64,8,2688]{2,1,0:T(8,128)(2,1)} %bitcast.44), calls=%async_computation.1 | async-start | bytes 5505024 | tf_op jit(solution)/shard_map/all_to_all | solution.py:31
  84.3 1.7 %maximum_select_fusion = bf16[2,2,512,256]{3,2,1,0:T(8,128)(2,1)S(1)} fusion(bf16[2,1,512,256]{3,2,1,0:T(8,128)(2,1)} %bitcast.12, bf16[2,1,512,256]{3,2,1,0:T(8,128)(2,1)} %bitcast.11, pred[]{:T(512)S(6)} %eq.3), kind=kLoop, calls=%fused_computation.10 | loop fusion | flops 1572864 | bytes 2097153 | tf_op jit(solution)/shard_map/jit(_where)/select_n | solution.py:471
  86.0 5.8 %tanh_convert_fusion = bf16[2048,2048]{1,0:T(8,128)(2,1)} fusion(bf16[2048,256]{1,0:T(8,128)(2,1)S(1)} %bitcast.48, bf16[256,2048]{1,0:T(8,128)(2,1)} %param.16, f32[2048]{0:T(1024)S(1)} %copy-done.6), kind=kOutput, calls=%fused_computation.2 | convolution fusion | flops 2155872256 | bytes 10493952 | tf_op jit(solution)/shard_map/dot_general | solution.py:19
  91.8 26.8 %all-to-all-done.1 = bf16[64,8,2688]{2,1,0:T(8,128)(2,1)} async-done(((bf16[64,8,2688]{2,1,0:T(8,128)(2,1)}), bf16[64,8,2688]{2,1,0:T(8,128)(2,1)}, u32[]{:S(2)}, u32[]{:S(2)}) %all-to-all-start.1) | async-done | bytes 2752544 | tf_op jit(solution)/shard_map/all_to_all | solution.py:31
  118.6 3.4 %shard_map.207 = (bf16[512,1664]{1,0:T(8,128)(2,1)}, bf16[512,1024]{1,0:T(8,128)(2,1)}) custom-call(s32[1]{0:T(128)} %bitcast.core_ref, bf16[512,2688]{1,0:T(8,128)(2,1)} %bitcast.10.got_ref), custom_call_target="tpu_custom_call" | custom-call | bytes 5505024 | tf_op jit(solution)/shard_map/pallas_call | solution.py:339
  122.0 1.9 %collective-permute-start.4 = (bf16[512,1024]{1,0:T(8,128)(2,1)}, bf16[512,1024]{1,0:T(8,128)(2,1)}, u32[]{:S(2)}, u32[]{:S(2)}) collective-permute-start(bf16[512,1024]{1,0:T(8,128)(2,1)} %get-tuple-element.47), channel_id=1, source_target_pairs={{0,32},{32,0},{1,33},{33,1},{2,34},{34,2},{3,35},{35,3},{4,36},{36... | collective-permute-start | bytes 3145736 | tf_op jit(solution)/shard_map/ppermute | solution.py:27
  123.9 6.8 %all-to-all-start.2 = ((bf16[64,8,1664]{2,1,0:T(8,128)(2,1)}), bf16[64,8,1664]{2,1,0:T(8,128)(2,1)}, u32[]{:S(2)}, u32[]{:S(2)}) async-start(bf16[64,8,1664]{2,1,0:T(8,128)(2,1)} %bitcast.52), calls=%async_computation.2 | async-start | bytes 3407872 | tf_op jit(solution)/shard_map/all_to_all | solution.py:31
  130.7 1.7 %pad_maximum_fusion = bf16[2,64,8,2,512]{4,2,3,1,0:T(8,128)(2,1)S(1)} fusion(bf16[1,64,8,2,512]{4,2,3,1,0:T(8,128)(2,1)} %bitcast.17, bf16[1,64,8,2,512]{4,2,3,1,0:T(8,128)(2,1)} %bitcast.54), kind=kLoop, calls=%fused_computation.7 | loop fusion | flops 1048576 | bytes 4194304 | tf_op jit(solution)/shard_map/stack | solution.py:479
  132.5 8.3 %convert_reduce_fusion = (f32[2048]{0:T(1024)}, bf16[2048,2048]{1,0:T(8,128)(2,1)S(1)}) fusion(bf16[2048,2048]{1,0:T(8,128)(2,1)} %tanh_convert_fusion, bf16[2048,512]{1,0:T(8,128)(2,1)S(1)} %bitcast.45, bf16[2048,512]{1,0:T(8,128)(2,1)S(1)} %copy-done), kind=kOutput, calls=%fused_computation | convolution fusion | flops 4324325376 | bytes 20979712 | tf_op jit(solution)/shard_map/dot_general | solution.py:19
  140.8 3.7 %fusion.9 = f32[256,2048]{1,0:T(8,128)} fusion(bf16[2048,256]{1,0:T(8,128)(2,1)S(1)} %bitcast.49, bf16[2048,2048]{1,0:T(8,128)(2,1)S(1)} %get-tuple-element.65), kind=kOutput, calls=%fused_computation.20 | convolution fusion | flops 2147483648 | bytes 11534336 | tf_op jit(solution)/shard_map/dot_general | solution.py:19
  145.5 9.7 %fusion.8 = f32[2048,512]{1,0:T(8,128)} fusion(bf16[2048,2048]{1,0:T(8,128)(2,1)} %tanh_convert_fusion, bf16[2048,512]{1,0:T(8,128)(2,1)S(1)} %bitcast.47), kind=kOutput, calls=%fused_computation.19 | convolution fusion | flops 4294967296 | bytes 14680064 | tf_op jit(solution)/shard_map/dot_general | solution.py:19
  155.9 2.9 %shard_map.208 = (f32[1024,1024]{1,0:T(8,128)}, f32[1024,512]{1,0:T(8,128)}, f32[4,1024]{1,0:T(4,128)}, f32[1,1024]{1,0:T(1,128)}, f32[1,1024]{1,0:T(1,128)}, /*index=5*/f32[1,512]{1,0:T(1,128)}) custom-call(s32[1]{0:T(128)} %bitcast.core_ref, bf16[512,1664]{1,0:T(8,128)(2,1)} %bitcast.15.own_ref), custom_call_target="tpu_custom_call" | custom-call | bytes 5242880 | tf_op jit(solution)/shard_map/pallas_call | solution.py:381
  159.5 2.9 %shard_map.209 = (f32[1024,1024]{1,0:T(8,128)}, f32[1024,512]{1,0:T(8,128)}, f32[4,1024]{1,0:T(4,128)}, f32[1,1024]{1,0:T(1,128)}, f32[1,1024]{1,0:T(1,128)}, /*index=5*/f32[1,512]{1,0:T(1,128)}) custom-call(s32[1]{0:T(128)} %bitcast.22.core_ref, ...), custom_call_target="tpu_custom_call", output_to_operand_aliasing={{0}: (2, {}), {1}: (3, {}), {2}: (4, {}), {3}: (5, {}), {4}... | custom-call | bytes 5242880 | tf_op jit(solution)/shard_map/pallas_call | solution.py:381
  (35 shorter events, 4.7 us)
Async XLA Ops:
  0.6 15.5 %copy-start = (bf16[2048,512]{1,0:T(8,128)(2,1)S(1)}, bf16[2048,512]{1,0:T(8,128)(2,1)}, u32[]{:S(2)}) copy-start(bf16[2048,512]{1,0:T(8,128)(2,1)} %param.18) | copy-start | bytes 6291460
  0.7 4.3 %copy-start.2 = (bf16[512,256]{1,0:T(8,128)(2,1)S(1)}, bf16[512,256]{1,0:T(8,128)(2,1)}, u32[]{:S(2)}) copy-start(bf16[512,256]{1,0:T(8,128)(2,1)} %param.14) | copy-start | bytes 786436
  0.7 4.3 %copy-start.4 = (bf16[4,4096]{1,0:T(4,128)(2,1)S(1)}, bf16[4,4096]{1,0:T(4,128)(2,1)}, u32[]{:S(2)}) copy-start(bf16[4,4096]{1,0:T(4,128)(2,1)} %points_ref.1) | copy-start | bytes 98308
  0.7 4.2 %copy-start.5 = (bf16[4,1024]{1,0:T(4,128)(2,1)S(1)}, bf16[4,1024]{1,0:T(4,128)(2,1)}, u32[]{:S(2)}) copy-start(bf16[4,1024]{1,0:T(4,128)(2,1)} %param.20) | copy-start | bytes 24580
  0.7 4.2 %copy-start.7 = (f32[1024]{0:T(1024)S(1)}, f32[1024]{0:T(1024)}, u32[]{:S(2)}) copy-start(f32[1024]{0:T(1024)} %param.21) | copy-start | bytes 12292
  0.7 5.6 %copy-start.8 = (f32[1,1024]{1,0:T(1,128)S(1)}, f32[1,1024]{1,0:T(1,128)}, u32[]{:S(2)}) copy-start(f32[1,1024]{1,0:T(1,128)} %param.23) | copy-start | bytes 12292
  3.5 18.5 %collective-permute-start = (bf16[512,2048]{1,0:T(8,128)(2,1)}, bf16[512,2048]{1,0:T(8,128)(2,1)}, u32[]{:S(2)}, u32[]{:S(2)}) collective-permute-start(bf16[512,2048]{1,0:T(8,128)(2,1)} %shard_map.204), channel_id=1, source_target_pairs={{0,32},{32,0},{1,33},{33,1},{2,34},{34,2},{3,35},{35,3},{4,36},{36... | collective-permute-start | bytes 6291464 | tf_op jit(solution)/shard_map/ppermute | solution.py:27
  4.9 8.8 %collective-permute-start.1 = (bf16[512,256]{1,0:T(8,128)(2,1)S(1)}, bf16[512,256]{1,0:T(8,128)(2,1)S(1)}, u32[]{:S(2)}, u32[]{:S(2)}) collective-permute-start(bf16[512,256]{1,0:T(8,128)(2,1)S(1)} %copy-done.2), channel_id=1, source_target_pairs={{0,32},{32,0},{1,33},{33,1},{2,34},{34,2},{3,35},{35,3},{4,36},{36... | collective-permute-start | bytes 786440 | tf_op jit(solution)/shard_map/ppermute | solution.py:27
  4.9 1.6 copy-start.3
  6.3 6.7 %copy-start.10 = (bf16[2048,1024]{0,1:T(8,128)(2,1)}, bf16[2048,1024]{0,1:T(8,128)(2,1)S(1)}, u32[]{:S(2)}) copy-start(bf16[2048,1024]{0,1:T(8,128)(2,1)S(1)} %tanh_convert_fusion.3) | copy-start | bytes 12582916
  6.5 9.6 %copy-start.6 = (f32[2048]{0:T(1024)S(1)}, f32[2048]{0:T(1024)}, u32[]{:S(2)}) copy-start(f32[2048]{0:T(1024)} %param.17) | copy-start | bytes 24580
  6.5 9.6 %copy-start.9 = (f32[512]{0:T(512)S(1)}, f32[512]{0:T(512)}, u32[]{:S(2)}) copy-start(f32[512]{0:T(512)} %param.19) | copy-start | bytes 6148
  14.4 51.8 %collective-permute-start.2 = (bf16[1024,256]{1,0:T(8,128)(2,1)}, bf16[1024,256]{1,0:T(8,128)(2,1)}, u32[]{:S(2)}, u32[]{:S(2)}) collective-permute-start(bf16[1024,256]{1,0:T(8,128)(2,1)} %constant_dynamic-update-slice_fusion), channel_id=1, source_target_pairs={{0,64},{64,0},{1,65},{65,1},{2,66},{66,2},{3,67},{67,3},{4,68},{68... | collective-permute-start | bytes 1572872 | tf_op jit(solution)/shard_map/ppermute | solution.py:27
  33.5 32.7 %all-to-all-start = ((bf16[64,16,512]{2,1,0:T(8,128)(2,1)}), bf16[64,16,512]{2,1,0:T(8,128)(2,1)S(1)}, u32[]{:S(2)}, u32[]{:S(2)}) async-start(bf16[64,16,512]{2,1,0:T(8,128)(2,1)} %bitcast.53), calls=%async_computation | async-start | bytes 2097152 | tf_op jit(solution)/shard_map/all_to_all | solution.py:31
  66.2 4.2 %copy-start.1 = (bf16[64,16,512]{2,1,0:T(8,128)(2,1)}, bf16[64,16,512]{2,1,0:T(8,128)(2,1)S(1)}, u32[]{:S(2)}) copy-start(bf16[64,16,512]{2,1,0:T(8,128)(2,1)S(1)} %all-to-all-done) | copy-start | bytes 3145732
  66.3 4.2 %collective-permute-start.3 = (bf16[512,1664]{1,0:T(8,128)(2,1)}, bf16[512,1664]{1,0:T(8,128)(2,1)}, u32[]{:S(2)}, u32[]{:S(2)}) collective-permute-start(bf16[512,1664]{1,0:T(8,128)(2,1)} %get-tuple-element.42), channel_id=1, source_target_pairs={{0,32},{32,0},{1,33},{33,1},{2,34},{34,2},{3,35},{35,3},{4,36},{36... | collective-permute-start | bytes 5111816 | tf_op jit(solution)/shard_map/ppermute | solution.py:27
  74.1 44.5 %all-to-all-start.1 = ((bf16[64,8,2688]{2,1,0:T(8,128)(2,1)}), bf16[64,8,2688]{2,1,0:T(8,128)(2,1)}, u32[]{:S(2)}, u32[]{:S(2)}) async-start(bf16[64,8,2688]{2,1,0:T(8,128)(2,1)} %bitcast.44), calls=%async_computation.1 | async-start | bytes 5505024 | tf_op jit(solution)/shard_map/all_to_all | solution.py:31
  122.0 8.7 %collective-permute-start.4 = (bf16[512,1024]{1,0:T(8,128)(2,1)}, bf16[512,1024]{1,0:T(8,128)(2,1)}, u32[]{:S(2)}, u32[]{:S(2)}) collective-permute-start(bf16[512,1024]{1,0:T(8,128)(2,1)} %get-tuple-element.47), channel_id=1, source_target_pairs={{0,32},{32,0},{1,33},{33,1},{2,34},{34,2},{3,35},{35,3},{4,36},{36... | collective-permute-start | bytes 3145736 | tf_op jit(solution)/shard_map/ppermute | solution.py:27
  123.9 31.2 %all-to-all-start.2 = ((bf16[64,8,1664]{2,1,0:T(8,128)(2,1)}), bf16[64,8,1664]{2,1,0:T(8,128)(2,1)}, u32[]{:S(2)}, u32[]{:S(2)}) async-start(bf16[64,8,1664]{2,1,0:T(8,128)(2,1)} %bitcast.52), calls=%async_computation.2 | async-start | bytes 3407872 | tf_op jit(solution)/shard_map/all_to_all | solution.py:31
  155.2 4.3 %collective-permute-start.5 = (bf16[512,1664]{1,0:T(8,128)(2,1)}, bf16[512,1664]{1,0:T(8,128)(2,1)}, u32[]{:S(2)}, u32[]{:S(2)}) collective-permute-start(bf16[512,1664]{1,0:T(8,128)(2,1)} %bitcast.15.own_ref), channel_id=1, source_target_pairs={{0,32},{32,0},{1,33},{33,1},{2,34},{34,2},{3,35},{35,3},{4,36},{36... | collective-permute-start | bytes 5111816 | tf_op jit(solution)/shard_map/ppermute | solution.py:27
